TPU v7x, 256 devices: a whole 4x4x8 slice. The times are simulated.
256 devices in a mesh: tm: 4 (over z_lo, core), height: 64 (over z_hi, y, x).
Axes of the slice: x: 4, y: 4, z: 8 (z_hi: 4, z_lo: 2; z = z_hi * 2 + z_lo), core: 2. Of those that a mesh axis runs over, the one named last changes fastest.
Arguments:
- quantized: bfloat16 [8, 128, 128, 128], P('tm', 'height'), may hold values from -127 to 127
- exponents: int32 [4, 8, 128], P(None, 'tm', 'height'), may hold values from -8 to -5
- out_grad: bfloat16 [8, 128, 128, 128], P('tm', 'height'), may hold values from -6 to 6
- kernel_one: bfloat16 [3, 3, 3, 128, 128], replicated, may hold values from -0.109375 to 0.109375
- kernel_two: bfloat16 [3, 3, 3, 128, 128], replicated, may hold values from -0.109375 to 0.109375
Outputs:
- in_grad: bfloat16 [8, 128, 128, 128], P('tm', 'height')
- kernel_one_grad: float32 [3, 3, 3, 128, 128], replicated
- kernel_two_grad: float32 [3, 3, 3, 128, 128], replicated
All inputs are finite; a program needn't handle non-finite values.
Results may differ from a plain program's by a relative error of at most 0.0049.
Values may be sent and summed in bfloat16 or wider, within the bound.
No kernel may reach another device: no remote copies, remote signals or barrier semaphores. Data moves between devices by JAX's collectives and lax.ppermute only.
A program may use at most 64 MiB of HBM per device.

v0:
```python
import math

import jax
import jax.numpy as jnp
from jax import lax
from jax.sharding import PartitionSpec as P


def shifted(value, axis, steps):
    count = lax.axis_size(axis)
    leading, last = (max(0, -steps), min(count, count - steps))
    return lax.ppermute(value, axis, [(source, source + steps) for source in range(leading, last)])


def extended_2(shard, sides, width):
    for axis, dim in sides:
        size, length = (lax.axis_size(axis), shard.shape[dim])
        up = [(i, (i + 1) % size) for i in range(size - 1)]
        down = [(j, i) for i, j in up]
        last = lax.slice_in_dim(shard, length - width, length, axis=dim)
        leading = lax.slice_in_dim(shard, 0, width, axis=dim)
        before = lax.ppermute(last, axis, up)
        after = lax.ppermute(leading, axis, down)
        shard = jnp.concatenate([before, shard, after], axis=dim)
    return shard


def extend(values, later):
    step = -1 if later else 1
    edge = values if later else values
    nearby = shifted(edge, "tm", step)
    joined = (values, nearby) if later else (nearby, values)
    return extended_2(jnp.concatenate(joined, axis=0), (("height", 1),), 1)


def convolve(extended, kernel, frames, rows, columns):
    padded = jnp.pad(extended, ((0, 0), (0, 0), (1, 1), (0, 0)))
    channels = padded.shape[3]
    total = jnp.zeros((frames * rows * columns, kernel.shape[4]), jnp.float32)
    for tap_t in range(3):
        for tap_r in range(3):
            slab = jnp.concatenate(
                [
                    padded[tap_t : tap_t + frames, tap_r : tap_r + rows, tap_w : tap_w + columns]
                    for tap_w in range(3)
                ],
                axis=3,
            )
            total = total + jnp.dot(
                slab.reshape(-1, 3 * channels),
                kernel[tap_t, tap_r].reshape(3 * channels, -1),
                preferred_element_type=jnp.float32,
            )
    return total.reshape(frames, rows, columns, -1)


def kernel_grad(values, extended, frames, rows, columns):
    padded = jnp.pad(extended, ((0, 0), (0, 0), (1, 1), (0, 0)))
    channels = values.shape[3]
    outward = padded.shape[3]
    flat_values = values.reshape(-1, channels)
    outer_list = []
    for tap_t in range(3):
        inner_list = []
        for tap_r in range(3):
            slab = jnp.concatenate(
                [
                    padded[
                        2 - tap_t : 2 - tap_t + frames,
                        2 - tap_r : 2 - tap_r + rows,
                        2 - tap_w : 2 - tap_w + columns,
                    ]
                    for tap_w in range(3)
                ],
                axis=3,
            )
            product = lax.dot_general(
                flat_values,
                slab.reshape(-1, 3 * outward),
                (((0,), (0,)), ((), ())),
                preferred_element_type=jnp.float32,
            )
            inner_list.append(jnp.transpose(product.reshape(channels, 3, outward), (1, 0, 2)))
        outer_list.append(jnp.stack(inner_list))
    return jnp.stack(outer_list)


def body(quantized, exponents, out_grad, kernel_one, kernel_two):
    frames, rows, columns, channels = quantized.shape
    blocks = exponents.shape[0]
    scale = jnp.exp2(exponents.astype(jnp.float32))
    scale = jnp.transpose(scale, (1, 2, 0))[:, :, None, :, None]
    codes_float = quantized.astype(jnp.float32).reshape(
        frames, rows, columns, blocks, channels // blocks
    )
    inputs = (codes_float * scale).reshape(frames, rows, columns, channels).astype(jnp.bfloat16)
    input_margin = extend(inputs, False)
    pre = convolve(input_margin, kernel_one, frames, rows, columns)
    hidden = jax.nn.silu(pre).astype(jnp.bfloat16)
    grad_margin = extend(out_grad, True)
    flipped_two = jnp.swapaxes(jnp.flip(kernel_two, (0, 1, 2)), 3, 4)
    hid_grad = convolve(grad_margin, flipped_two, frames, rows, columns)
    sigma = jax.nn.sigmoid(pre)
    pre_grad = (hid_grad * sigma * (1.0 + pre * (1.0 - sigma))).astype(jnp.bfloat16)
    two_local = kernel_grad(hidden, grad_margin, frames, rows, columns)
    pre_margin = extend(pre_grad, True)
    flipped_one = jnp.swapaxes(jnp.flip(kernel_one, (0, 1, 2)), 3, 4)
    in_grad = convolve(pre_margin, flipped_one, frames, rows, columns).astype(jnp.bfloat16)
    one_local = kernel_grad(inputs, pre_margin, frames, rows, columns)
    one_total, two_total = lax.psum((one_local, two_local), ("tm", "height"))
    positions = frames * lax.axis_size("tm") * rows * lax.axis_size("height") * columns
    factor = 1.0 / math.sqrt(positions)
    return (in_grad, one_total * factor, two_total * factor)


def solution(mesh):
    placed = (
        P("tm", "height", None, None),
        P(None, "tm", "height"),
        P("tm", "height", None, None),
        P(),
        P(),
    )
    return jax.shard_map(
        body,
        mesh=mesh,
        in_specs=placed,
        out_specs=(P("tm", "height", None, None), P(), P()),
        check_vma=False,
    )
```

profile of v0, /device:TPU:1, one launch (start us, length us, event | category | flops | bytes accessed | tf_op | source)
XLA Modules:
  0.0 393.3 jit_solution(14576470111140466968)
XLA Ops:
  7.2 0.8 exponential_bitcast_fusion
  8.1 0.9 multiply_convert_fusion.2
  9.1 4.9 %collective-permute-start.3 = (bf16[2,2,128,128]{3,2,1,0:T(8,128)(2,1)S(1)}, bf16[2,2,128,128]{3,2,1,0:T(8,128)(2,1)S(1)}, u32[]{:S(2)}, u32[]{:S(2)}) collective-permute-start(bf16[2,2,128,128]{3,2,1,0:T(8,128)(2,1)S(1)} %multiply_convert_fusion.2), channel_id=1, source_target_pairs={{0,64},{64,128},{128,192},{1,65},{65,129},{129,193},{2,66},{66,130... | collective-permute-start | bytes 393224 | tf_op jit(solution)/shard_map/ppermute | solution.py:12
  14.0 1.9 collective-permute-start
  16.0 2.0 fusion.68
  18.0 1.4 copy.45
  19.4 2.0 copy.44
  21.6 0.9 fusion.66
  22.7 1.3 collective-permute-start.5
  24.0 4.0 %collective-permute-start.4 = (bf16[4,1,128,128]{3,2,1,0:T(8,128)(2,1)S(1)}, bf16[4,1,128,128]{3,2,1,0:T(8,128)(2,1)S(1)}, u32[]{:S(2)}, u32[]{:S(2)}) collective-permute-start(bf16[4,1,128,128]{3,2,1,0:T(8,128)(2,1)S(1)} %get-tuple-element.151), channel_id=1, source_target_pairs={{0,1},{1,2},{2,3},{3,4},{4,5},{5,6},{6,7},{7,8},{8,9},{9,10},{10,1... | collective-permute-start | bytes 393224 | tf_op jit(solution)/shard_map/ppermute | solution.py:22
  28.0 1.3 collective-permute-start.2
  29.3 4.0 %collective-permute-start.1 = (bf16[4,1,128,128]{3,2,1,0:T(8,128)(2,1)S(1)}, bf16[4,1,128,128]{3,2,1,0:T(8,128)(2,1)S(1)}, u32[]{:S(2)}, u32[]{:S(2)}) collective-permute-start(bf16[4,1,128,128]{3,2,1,0:T(8,128)(2,1)S(1)} %get-tuple-element.148), channel_id=1, source_target_pairs={{0,1},{1,2},{2,3},{3,4},{4,5},{5,6},{6,7},{7,8},{8,9},{9,10},{10,1... | collective-permute-start | bytes 393224 | tf_op jit(solution)/shard_map/ppermute | solution.py:22
  33.5 0.5 fusion.71
  34.2 1.2 collective-permute-done.2
  35.4 0.9 collective-permute-done.1
  36.5 0.5 fusion.70
  37.5 0.8 fusion.46
  38.8 0.7 copy-done.36
  40.1 0.5 copy-done.34
  42.1 0.5 copy-done.37
  42.6 0.3 multiply_convert_fusion
  44.8 0.9 pad_maximum_fusion.50
  46.6 2.6 collective-permute-start.6
  49.2 1.9 copy.80
  51.2 0.9 copy.78
  52.1 2.0 convolution_bitcast_fusion
  54.1 2.0 convolution_bitcast_fusion.1
  56.2 0.3 convolution_bitcast_fusion.2
  56.7 0.3 convolution_bitcast_fusion.3
  57.2 0.3 convolution_bitcast_fusion.4
  57.7 0.3 convolution_bitcast_fusion.5
  58.4 0.3 convolution_bitcast_fusion.6
  58.9 0.3 convolution_bitcast_fusion.7
  59.4 0.3 convolution_bitcast_fusion.8
  60.1 1.3 collective-permute-start.8
  61.4 4.9 %collective-permute-start.7 = (bf16[4,1,128,128]{3,2,1,0:T(8,128)(2,1)S(1)}, bf16[4,1,128,128]{3,2,1,0:T(8,128)(2,1)S(1)}, u32[]{:S(2)}, u32[]{:S(2)}) collective-permute-start(bf16[4,1,128,128]{3,2,1,0:T(8,128)(2,1)S(1)} %get-tuple-element.143), channel_id=1, source_target_pairs={{0,1},{1,2},{2,3},{3,4},{4,5},{5,6},{6,7},{7,8},{8,9},{9,10},{10,1... | collective-permute-start | bytes 393224 | tf_op jit(solution)/shard_map/ppermute | solution.py:22
  66.4 1.4 pad_maximum_fusion.1
  67.8 1.6 collective-permute-done.7
  69.4 0.8 fusion.73
  70.4 1.2 fusion.69
  71.6 0.8 fusion.72
  72.9 0.3 convolution_bitcast_fusion.9
  73.2 0.3 convolution_bitcast_fusion.10
  73.5 0.3 copy-done.19
  73.9 0.8 fusion.28
  74.9 1.0 convolution_bitcast_fusion.11
  75.9 0.8 fusion.26
  76.9 1.0 convolution_bitcast_fusion.12
  77.9 1.1 fusion.20
  79.3 1.0 convolution_bitcast_fusion.13
  80.2 2.1 fusion.24
  82.5 1.0 convolution_bitcast_fusion.14
  83.4 1.7 fusion.22
  85.4 1.0 convolution_bitcast_fusion.15
  86.6 1.0 convolution_bitcast_fusion.16
  87.8 0.3 convolution_bitcast_fusion.17
  88.2 0.3 copy-done.25
  89.3 0.4 copy-done.13
  89.9 1.4 pad_maximum_fusion
  91.3 0.8 copy-done.32
  95.0 0.9 fusion
  95.9 286.1 %all-reduce.6.cloned.1.call-done = (f32[3,3,3,128,128]{4,3,2,1,0:T(8,128)}, f32[3,3,3,128,128]{4,3,2,1,0:T(8,128)}) async-done(((f32[3,3,3,128,128]{4,3,2,1,0:T(8,128)}, f32[3,3,3,128,128]{4,3,2,1,0:T(8,128)}), (f32[3,3,3,128,128]{4,3,2,1,0:T(8,128)}, f32[3,3,3,128,128]{4,3,2,1,0:T(8,128)})) %all-reduce.6.cloned.1.call-update) | async-done | bytes 3538960 | tf_op jit(solution)/shard_map/psum | solution.py:110
  382.0 3.1 broadcast_multiply_fusion.1
  385.1 1.4 broadcast_multiply_fusion
  (153 shorter events, 14.4 us)
Async XLA Ops:
  7.2 10.8 %copy-start = (bf16[3,3,3,128,128]{4,3,2,1,0:T(8,128)(2,1)S(1)}, bf16[3,3,3,128,128]{4,3,2,1,0:T(8,128)(2,1)}, u32[]{:S(2)}) copy-start(bf16[3,3,3,128,128]{4,3,2,1,0:T(8,128)(2,1)} %param.8) | copy-start | bytes 2654212
  7.2 374.8 %all-reduce.6.cloned.1.call-start = ((), (), s32[]{:S(2)}) async-start(), calls=%async_computation | async-start | bytes 7077888 | tf_op jit(solution)/shard_map/psum | solution.py:110
  9.1 13.5 %collective-permute-start.3 = (bf16[2,2,128,128]{3,2,1,0:T(8,128)(2,1)S(1)}, bf16[2,2,128,128]{3,2,1,0:T(8,128)(2,1)S(1)}, u32[]{:S(2)}, u32[]{:S(2)}) collective-permute-start(bf16[2,2,128,128]{3,2,1,0:T(8,128)(2,1)S(1)} %multiply_convert_fusion.2), channel_id=1, source_target_pairs={{0,64},{64,128},{128,192},{1,65},{65,129},{129,193},{2,66},{66,130... | collective-permute-start | bytes 393224 | tf_op jit(solution)/shard_map/ppermute | solution.py:12
  14.0 13.9 %collective-permute-start = (bf16[2,2,128,128]{3,2,1,0:T(8,128)(2,1)}, bf16[2,2,128,128]{3,2,1,0:T(8,128)(2,1)S(1)}, u32[]{:S(2)}, u32[]{:S(2)}) collective-permute-start(bf16[2,2,128,128]{3,2,1,0:T(8,128)(2,1)} %param.7), channel_id=1, source_target_pairs={{64,0},{128,64},{192,128},{65,1},{129,65},{193,129},{66,2},{130,66... | collective-permute-start | bytes 393224 | tf_op jit(solution)/shard_map/ppermute | solution.py:12
  21.6 1.0 copy-start.20
  22.7 10.7 %collective-permute-start.5 = (bf16[4,1,128,128]{3,2,1,0:T(8,128)(2,1)S(1)}, bf16[4,1,128,128]{3,2,1,0:T(8,128)(2,1)S(1)}, u32[]{:S(2)}, u32[]{:S(2)}) collective-permute-start(bf16[4,1,128,128]{3,2,1,0:T(8,128)(2,1)S(1)} %get-tuple-element.152), channel_id=1, source_target_pairs={{1,0},{2,1},{3,2},{4,3},{5,4},{6,5},{7,6},{8,7},{9,8},{10,9},{11,1... | collective-permute-start | bytes 393224 | tf_op jit(solution)/shard_map/ppermute | solution.py:23
  24.0 9.4 %collective-permute-start.4 = (bf16[4,1,128,128]{3,2,1,0:T(8,128)(2,1)S(1)}, bf16[4,1,128,128]{3,2,1,0:T(8,128)(2,1)S(1)}, u32[]{:S(2)}, u32[]{:S(2)}) collective-permute-start(bf16[4,1,128,128]{3,2,1,0:T(8,128)(2,1)S(1)} %get-tuple-element.151), channel_id=1, source_target_pairs={{0,1},{1,2},{2,3},{3,4},{4,5},{5,6},{6,7},{7,8},{8,9},{9,10},{10,1... | collective-permute-start | bytes 393224 | tf_op jit(solution)/shard_map/ppermute | solution.py:22
  28.0 7.4 %collective-permute-start.2 = (bf16[4,1,128,128]{3,2,1,0:T(8,128)(2,1)S(1)}, bf16[4,1,128,128]{3,2,1,0:T(8,128)(2,1)S(1)}, u32[]{:S(2)}, u32[]{:S(2)}) collective-permute-start(bf16[4,1,128,128]{3,2,1,0:T(8,128)(2,1)S(1)} %get-tuple-element.147), channel_id=1, source_target_pairs={{1,0},{2,1},{3,2},{4,3},{5,4},{6,5},{7,6},{8,7},{9,8},{10,9},{11,1... | collective-permute-start | bytes 393224 | tf_op jit(solution)/shard_map/ppermute | solution.py:23
  29.3 7.0 %collective-permute-start.1 = (bf16[4,1,128,128]{3,2,1,0:T(8,128)(2,1)S(1)}, bf16[4,1,128,128]{3,2,1,0:T(8,128)(2,1)S(1)}, u32[]{:S(2)}, u32[]{:S(2)}) collective-permute-start(bf16[4,1,128,128]{3,2,1,0:T(8,128)(2,1)S(1)} %get-tuple-element.148), channel_id=1, source_target_pairs={{0,1},{1,2},{2,3},{3,4},{4,5},{5,6},{6,7},{7,8},{8,9},{9,10},{10,1... | collective-permute-start | bytes 393224 | tf_op jit(solution)/shard_map/ppermute | solution.py:22
  38.5 0.9 copy-start.36
  38.6 1.2 copy-start.35
  39.7 0.9 copy-start.34
  40.0 0.9 copy-start.33
  41.7 0.9 copy-start.37
  46.6 13.5 %collective-permute-start.6 = (bf16[2,2,128,128]{3,2,1,0:T(8,128)(2,1)S(1)}, bf16[2,2,128,128]{3,2,1,0:T(8,128)(2,1)S(1)}, u32[]{:S(2)}, u32[]{:S(2)}) collective-permute-start(bf16[2,2,128,128]{3,2,1,0:T(8,128)(2,1)S(1)} %multiply_convert_fusion.1), channel_id=1, source_target_pairs={{64,0},{128,64},{192,128},{65,1},{129,65},{193,129},{66,2},{130,66... | collective-permute-start | bytes 393224 | tf_op jit(solution)/shard_map/ppermute | solution.py:12
  57.2 1.0 copy-start.2
  58.9 0.9 copy-start.11
  58.9 1.0 copy-start.12
  60.1 7.6 %collective-permute-start.8 = (bf16[4,1,128,128]{3,2,1,0:T(8,128)(2,1)S(1)}, bf16[4,1,128,128]{3,2,1,0:T(8,128)(2,1)S(1)}, u32[]{:S(2)}, u32[]{:S(2)}) collective-permute-start(bf16[4,1,128,128]{3,2,1,0:T(8,128)(2,1)S(1)} %get-tuple-element.142), channel_id=1, source_target_pairs={{1,0},{2,1},{3,2},{4,3},{5,4},{6,5},{7,6},{8,7},{9,8},{10,9},{11,1... | collective-permute-start | bytes 393224 | tf_op jit(solution)/shard_map/ppermute | solution.py:23
  61.4 8.0 %collective-permute-start.7 = (bf16[4,1,128,128]{3,2,1,0:T(8,128)(2,1)S(1)}, bf16[4,1,128,128]{3,2,1,0:T(8,128)(2,1)S(1)}, u32[]{:S(2)}, u32[]{:S(2)}) collective-permute-start(bf16[4,1,128,128]{3,2,1,0:T(8,128)(2,1)S(1)} %get-tuple-element.143), channel_id=1, source_target_pairs={{0,1},{1,2},{2,3},{3,4},{4,5},{5,6},{6,7},{7,8},{8,9},{9,10},{10,1... | collective-permute-start | bytes 393224 | tf_op jit(solution)/shard_map/ppermute | solution.py:22
  72.9 0.9 copy-start.19
  72.9 1.0 copy-start.23
  73.9 2.0 copy-start.22
  80.2 3.2 copy-start.17
  80.2 3.2 copy-start.18
  85.4 2.2 copy-start.15
  85.4 2.2 copy-start.16
  86.4 1.2 copy-start.21
  87.6 0.9 copy-start.25
  87.8 1.0 copy-start.7
  88.1 1.0 copy-start.8
  88.1 1.0 copy-start.9
  88.2 1.1 copy-start.10
  88.8 1.0 copy-start.13
  88.8 1.0 copy-start.14
  91.3 0.9 copy-start.32
  91.3 1.2 copy-start.31
  91.3 1.2 copy-start.3
  91.3 1.4 copy-start.4
  91.3 1.4 copy-start.30
  92.5 0.9 copy-start.29
  92.8 1.0 copy-start.5
  92.8 1.0 copy-start.28
  93.1 1.0 copy-start.6
  93.1 1.1 copy-start.27
  93.6 1.0 copy-start.26
  94.0 0.9 copy-start.24
  382.0 3.1 copy-start.1
Sparse Core Ops, SparseCore 0:
  91.4 290.5 all-reduce.5
where the time goes:
time: 395 us; the launch traced here: 393 us
  waiting for transfers between devices  290 us (73%)
  starting transfers between devices  26.3 us (7%)
  local copies, waits for them, and re-layouts  22.1 us (6%)
  matrix products  20.5 us (5%)
  other arithmetic  19.5 us (5%)
  between operations  15.1 us (4%)
    psum x1, waiting for transfers between devices, body(): one_total, two_total = lax.psum((one_local, two_local), ('tm', 'height'))  286 us
    ppermute x3, starting transfers between devices, extended_2(): before = lax.ppermute(last, axis, up)  12.9 us
    dot_general x18, matrix products, kernel_grad(): lax.dot_general(flat_values, slab.reshape(-1, 3 * outward), (((0,), (0,))...  12.7 us
    ppermute x3, starting transfers between devices, shifted(): lax.ppermute(value, axis, [(source, source + steps) for source in range(l...  9.44 us
    concatenate x13, other arithmetic, kernel_grad(): jnp.concatenate([padded[2 - tap_t:2 - tap_t + frames, 2 - tap_r:2 - tap_r...  9.02 us
    unnamed x79, local copies, waits for them, and re-layouts  8.89 us
  transfers between devices with their start and end apart: 10, of which 4 were waited for; matrix products, arithmetic and copies ran while one was open for 6% of the time, Pallas kernels for 0%

commit v1 on v0

v1 whole, which is shorter than its diff:
```python
import math

import jax
import jax.numpy as jnp
from jax import lax
from jax.experimental import pallas as pl
from jax.experimental.pallas import tpu as pltpu
from jax.sharding import PartitionSpec as P

BF = jnp.bfloat16
F32 = jnp.float32
AXES = ("tm", "height")
TM, HEIGHT = 4, 64
COUNT = TM * HEIGHT
C = 128
ROWS = 27 * C
PART = ROWS // 16


def tm_pairs(first):
    pairs = []
    for tm in range(TM):
        for h in range(HEIGHT):
            if first:
                pairs.append((tm * HEIGHT + h, (tm ^ 1) * HEIGHT + h))
            elif tm in (1, 2):
                pairs.append((tm * HEIGHT + h, (3 - tm) * HEIGHT + h))
            else:
                pairs.append((tm * HEIGHT + h, tm * HEIGHT + (h ^ 1)))
    return pairs


def height_pairs(odd):
    pairs = []
    for tm in range(TM):
        for h in range(HEIGHT):
            up = (h % 2 == 1) if odd else (h % 2 == 0)
            other = h + 1 if up else h - 1
            if 0 <= other < HEIGHT:
                pairs.append((tm * HEIGHT + h, tm * HEIGHT + other))
            else:
                pairs.append((tm * HEIGHT + h, (tm ^ 1) * HEIGHT + h))
    return pairs


def flip_pairs(mask):
    return [(d, d ^ mask) for d in range(COUNT)]


SIBLING = flip_pairs(64)
PLANE = [[base + n for n in range(16)] for base in range(0, COUNT, 16)]


def send(value, pairs):
    return lax.ppermute(value, AXES, pairs)


def exchange(value):
    return lax.all_to_all(value, AXES, 0, 0, axis_index_groups=PLANE, tiled=True)


VMEM = pl.BlockSpec(memory_space=pltpu.VMEM)
SMEM = pl.BlockSpec(memory_space=pltpu.SMEM)
ANY = pl.BlockSpec(memory_space=pl.ANY)


def call(kernel, outs, ins, scratch=(), specs=None, out_specs=None, flops=0, moved=1 << 20, limit=8):
    return pl.pallas_call(
        kernel,
        out_shape=[jax.ShapeDtypeStruct(shape, kind) for shape, kind in outs],
        in_specs=specs or [VMEM] * len(ins),
        out_specs=out_specs or [VMEM] * len(outs),
        scratch_shapes=list(scratch),
        compiler_params=pltpu.CompilerParams(vmem_limit_bytes=limit << 20),
        cost_estimate=pl.CostEstimate(flops=flops, bytes_accessed=moved, transcendentals=0),
    )(*ins)


def columns(value):
    wide = value.astype(F32)
    row = lax.broadcasted_iota(jnp.int32, wide.shape, 0)
    before = jnp.where(row == 0, 0.0, pltpu.roll(wide, 1, 0)).astype(BF)
    after = jnp.where(row == 127, 0.0, pltpu.roll(wide, 127, 0)).astype(BF)
    return before, value, after


def dot(a, b):
    return lax.dot_general(a, b, (((1,), (0,)), ((), ())), preferred_element_type=F32)


def dot_nt(a, b):
    return lax.dot_general(a, b, (((1,), (1,)), ((), ())), preferred_element_type=F32)


def turned(kernel_ref, i, j):
    base = (2 - i) * 9 + (2 - j) * 3
    return jnp.concatenate([kernel_ref[base + 2], kernel_ref[base + 1], kernel_ref[base]], axis=1)


def main_kernel(
    place_ref, near_ref, far_ref, own_ref, grad_ref, one_ref, two_ref,
    keep_ref, away_ref, pre_grad_ref,
    slab_i, slab_g, slab_p, input_t, hidden_t,
):
    core = place_ref[0]

    def margin(t, r, later):
        inside = place_ref[1] < TM - 1 if later else place_ref[1] > 0
        value = jnp.where(core == (0 if later else 1), near_ref[t, r], far_ref[t, r])
        return jnp.where(inside, value, 0).astype(BF)

    for t in range(4):
        for r in range(4):
            value = margin(t, r, False) if t < 2 else own_ref[t - 2, r]
            for k, part in enumerate(columns(value)):
                slab_i[t, r, :, k * C : (k + 1) * C] = part
            flipped = value.T
            if r < 3:
                input_t[t, r, :, 0:C] = flipped
            if r > 0:
                input_t[t, r - 1, :, C : 2 * C] = flipped
            value = grad_ref[t, r] if t < 2 else margin(t - 2, r, True)
            for k, part in enumerate(columns(value)):
                slab_g[t, r, :, k * C : (k + 1) * C] = part
    pre = jnp.zeros((512, C), F32)
    hid = jnp.zeros((512, C), F32)
    for i in range(3):
        for j in range(3):
            pre += dot(slab_i[i : i + 2, j : j + 2].reshape(512, 3 * C), one_ref[i * 3 + j])
            hid += dot_nt(slab_g[i : i + 2, j : j + 2].reshape(512, 3 * C), turned(two_ref, i, j))
    gate = 1.0 / (1.0 + jnp.exp(-pre))
    hidden = (pre * gate).astype(BF)
    pre_grad = (hid * gate * (1.0 + pre * (1.0 - gate))).astype(BF)
    for t in range(2):
        for r in range(2):
            n = 2 * t + r
            hidden_t[:, n * C : (n + 1) * C] = hidden[n * C : (n + 1) * C].T
            value = pre_grad[n * C : (n + 1) * C]
            pre_grad_ref[t, r] = value
            for k, part in enumerate(columns(value)):
                slab_p[t, r * C : (r + 1) * C, k * C : (k + 1) * C] = part

    def store(first, base, value):
        for k in range(3):
            rows = pl.ds((base + 2 - k) * C, C)
            part = value[:, k * C : (k + 1) * C]

            @pl.when(core == first)
            def _():
                keep_ref[rows, :] = part

            @pl.when(core != first)
            def _():
                away_ref[rows, :] = part.astype(BF)

    for i in range(3):
        for j in range(3):
            value = dot(input_t[i, j], slab_p[0]) + dot(input_t[i + 1, j], slab_p[1])
            store(0, i * 9 + j * 3, value)
    for i in range(3):
        for j in range(3):
            value = dot(hidden_t[...], slab_g[i : i + 2, j : j + 2].reshape(512, 3 * C))
            store(1, (2 - i) * 9 + (2 - j) * 3, value)


def in_grad_kernel(place_ref, near_ref, far_ref, own_ref, one_ref, out_ref, slab):
    def later(t, r):
        value = jnp.where(place_ref[0] == 0, near_ref[t, r], far_ref[t, r])
        return jnp.where(place_ref[1] < TM - 1, value, 0).astype(BF)

    for t in range(4):
        for r in range(4):
            value = own_ref[t, r] if t < 2 else later(t - 2, r)
            for k, part in enumerate(columns(value)):
                slab[t, r, :, k * C : (k + 1) * C] = part
    total = jnp.zeros((512, C), F32)
    for i in range(3):
        for j in range(3):
            total += dot_nt(slab[i : i + 2, j : j + 2].reshape(512, 3 * C), turned(one_ref, i, j))
    out_ref[...] = total.astype(BF).reshape(2, 2, C, C)


def body(quantized, exponents, out_grad, kernel_one, kernel_two):
    tm = lax.axis_index("tm")
    index = lax.axis_index("height")
    core = tm % 2
    odd = index % 2 == 1
    where = jnp.stack([core, tm]).astype(jnp.int32)
    one = kernel_one.reshape(27, C, C)
    two = kernel_two.reshape(27, C, C)
    block = (2, 2, C, C)
    scale = jnp.exp2(exponents.astype(F32))
    scale = jnp.repeat(jnp.transpose(scale, (1, 2, 0)), C // 4, axis=2)

    def scaled(codes, powers):
        return (codes.astype(F32) * powers[..., None, :]).astype(BF)

    def met(near, far):
        inside = jnp.where(odd, index < HEIGHT - 1, index > 0)
        far = lax.optimization_barrier(jnp.where(inside, far, 0))
        before = jnp.where(odd, near, far)
        after = jnp.where(odd, far, near)
        return before, after

    def band(before, value, after):
        return jnp.concatenate([before[:, None], value, after[:, None]], axis=1)

    codes = jnp.where(odd, quantized[:, 1], quantized[:, 0])
    powers = jnp.where(odd, scale[:, 1], scale[:, 0])
    edge = jnp.where(odd, out_grad[:, 1], out_grad[:, 0])
    leaving = jnp.concatenate([scaled(codes, powers), edge], axis=0)
    leaving, quantized = lax.optimization_barrier((leaving, quantized))
    far = send(leaving, height_pairs(True))
    inputs = scaled(quantized, scale)
    edge = jnp.where(odd, out_grad[:, 0], out_grad[:, 1])
    leaving = jnp.concatenate([jnp.where(odd, inputs[:, 0], inputs[:, 1]), edge], axis=0)
    inputs, leaving = lax.optimization_barrier((inputs, leaving))
    near = send(leaving, height_pairs(False))
    before, after = met(near, far)
    banded = band(before[:2], inputs, after[:2])
    grad_banded = band(before[2:], out_grad, after[2:])
    near = send(jnp.where(core == 0, banded, grad_banded), tm_pairs(True))
    far = send(jnp.where(core == 0, grad_banded, banded), tm_pairs(False))
    keep, away, pre_grad = call(
        main_kernel,
        [((ROWS, C), F32), ((ROWS, C), BF), (block, BF)],
        [where, near, far, banded, grad_banded, one.reshape(9, 3 * C, C), two],
        specs=[SMEM] + [VMEM] * 6,
        scratch=[
            pltpu.VMEM((4, 4, C, 3 * C), BF),
            pltpu.VMEM((4, 4, C, 3 * C), BF),
            pltpu.VMEM((2, 2 * C, 3 * C), BF),
            pltpu.VMEM((4, 3, C, 2 * C), BF),
            pltpu.VMEM((C, 4 * C), BF),
        ],
        flops=4 * 2 * 27 * C * C * 512,
        limit=32,
    )
    near = send(jnp.where(odd, pre_grad[:, 0], pre_grad[:, 1]), height_pairs(False))
    far = send(jnp.where(odd, pre_grad[:, 1], pre_grad[:, 0]), height_pairs(True))
    before, after = met(near, far)
    total = (keep + send(away, SIBLING).astype(F32)).astype(BF).reshape(16, PART, C)
    total = jnp.sum(exchange(total).astype(F32), axis=0).astype(BF)
    total, before, after = lax.optimization_barrier((total, before, after))
    pre_banded = band(before, pre_grad, after)
    pre_near = send(pre_banded, tm_pairs(True))
    pre_far = send(pre_banded, tm_pairs(False))
    total = total.astype(F32) + send(total, flip_pairs(128)).astype(F32)
    total = total.astype(BF)
    others = [send(total, flip_pairs(16 * n)).astype(F32) for n in (1, 3, 2)]
    factor = 1.0 / math.sqrt(8 * 128 * 128)
    total = (((total.astype(F32) + others[0]) + (others[1] + others[2])) * factor).astype(BF)
    total, pre_near, pre_far = lax.optimization_barrier((total, pre_near, pre_far))
    mine = exchange(jnp.broadcast_to(total[None], (16, PART, C))).reshape(ROWS, C)
    theirs = send(mine, SIBLING)
    one_total = jnp.where(core == 0, mine, theirs).astype(F32)
    two_total = jnp.where(core == 0, theirs, mine).astype(F32)
    (in_grad,) = call(
        in_grad_kernel,
        [(block, BF)],
        [where, pre_near, pre_far, pre_banded, one],
        specs=[SMEM] + [VMEM] * 4,
        scratch=[pltpu.VMEM((4, 4, C, 3 * C), BF)],
        flops=2 * 27 * C * C * 512,
    )
    shape = (3, 3, 3, C, C)
    return (in_grad, one_total.reshape(shape), two_total.reshape(shape))


def solution(mesh):
    placed = (
        P("tm", "height", None, None),
        P(None, "tm", "height"),
        P("tm", "height", None, None),
        P(),
        P(),
    )
    return jax.shard_map(
        body,
        mesh=mesh,
        in_specs=placed,
        out_specs=(P("tm", "height", None, None), P(), P()),
        check_vma=False,
    )
```

time: 395 us -> 102 us (0.26)
  waiting for transfers between devices: 290 us -> 32.2 us
  local copies, waits for them, and re-layouts: 22.1 us -> 0.39 us
  matrix products: 20.5 us -> 0 us
  blocking collectives: 0 us -> 18.3 us
  between operations: 15.1 us -> 0.9 us
  other arithmetic: 19.5 us -> 8.22 us
  Pallas kernels: 0 us -> 9.25 us
  starting transfers between devices: 26.3 us -> 32.7 us
    psum x1 -> x0, waiting for transfers between devices: 286 us -> none  [body(): one_total, two_total = lax.psum((one_local, two_local), ('tm', 'height'))]
    ppermute x9 -> x14, waiting for transfers between devices: 3.75 us -> 30.3 us  [send(): return lax.ppermute(value, AXES, pairs)]
    dot_general x45 -> x0, matrix products: 20.5 us -> none  [the longest x18 12.7 us: kernel_grad(): lax.dot_general(flat_values, slab.reshape(-1, 3 * outward), (((0,), (0,))...]
    all_to_all x0 -> x1, blocking collectives: none -> 18.3 us  [exchange(): lax.all_to_all(value, AXES, 0, 0, axis_index_groups=PLANE, tiled=True)]
    all_to_all x0 -> x1, starting transfers between devices: none -> 10.3 us  [exchange(): lax.all_to_all(value, AXES, 0, 0, axis_index_groups=PLANE, tiled=True)]
    concatenate x25 -> x3, other arithmetic: 10.2 us -> 0.06 us  [the longest x1 0.03 us: band(): return jnp.concatenate([before[:, None], value, after[:, None]], axis=1)]
    pallas_call x0 -> x2, Pallas kernels: none -> 9.25 us  [call(): pl.pallas_call(kernel, out_shape=[jax.ShapeDtypeStruct(shape, kind) for s...]
    unnamed x79 -> x6, local copies, waits for them, and re-layouts: 8.89 us -> 0.02 us
  transfers between devices with their start and end apart: 10 -> 15, of which waited for: 4 -> 8; matrix products, arithmetic and copies ran while one was open for 6% -> 1% of each run, Pallas kernels for 0% -> 2%
where the time goes in v1:
time: 102 us
  starting transfers between devices  32.7 us (32%)
  waiting for transfers between devices  32.2 us (32%)
  blocking collectives  18.3 us (18%)
  Pallas kernels  9.25 us (9%)
  other arithmetic  8.22 us (8%)
    ppermute x14, waiting for transfers between devices, send(): return lax.ppermute(value, AXES, pairs)  30.3 us
    ppermute x14, starting transfers between devices, send(): return lax.ppermute(value, AXES, pairs)  22.3 us
    all_to_all x1, blocking collectives, exchange(): lax.all_to_all(value, AXES, 0, 0, axis_index_groups=PLANE, tiled=True)  18.3 us
    all_to_all x1, starting transfers between devices, exchange(): lax.all_to_all(value, AXES, 0, 0, axis_index_groups=PLANE, tiled=True)  10.3 us
    pallas_call x2, Pallas kernels, call(): pl.pallas_call(kernel, out_shape=[jax.ShapeDtypeStruct(shape, kind) for s...  9.25 us
    reshape x2, other arithmetic, body(): return (in_grad, one_total.reshape(shape), two_total.reshape(shape))  2.81 us
  transfers between devices with their start and end apart: 15, of which 8 were waited for; matrix products, arithmetic and copies ran while one was open for 1% of the time, Pallas kernels for 2%

profile of v1, /device:TPU:1, one launch (start us, length us, event | category | flops | bytes accessed | tf_op | source)
XLA Modules:
  0.0 102.0 jit_solution(7944683945943549671)
XLA Ops:
  0.6 0.0 copy-start.2
  0.7 0.7 exponential_bitcast_fusion
  1.4 0.1 broadcast_in_dim.36
  1.5 0.1 reshape.49
  1.6 0.9 select_bitcast_fusion.2
  2.5 0.9 fusion
  3.4 3.3 %collective-permute-start.1 = (bf16[4,128,128]{2,1,0:T(8,128)(2,1)S(1)}, bf16[4,128,128]{2,1,0:T(8,128)(2,1)S(1)}, u32[]{:S(2)}, u32[]{:S(2)}) collective-permute-start(bf16[4,128,128]{2,1,0:T(8,128)(2,1)S(1)} %pad_maximum_fusion.3), channel_id=1, source_target_pairs={{0,64},{1,2},{2,1},{3,4},{4,3},{5,6},{6,5},{7,8},{8,7},{9,10},{10,... | collective-permute-start | bytes 393224 | tf_op jit(solution)/shard_map/ppermute | solution.py:55
  6.7 0.9 multiply_convert_fusion
  7.7 0.1 collective-permute-start
  7.8 0.0 collective-permute-done.1
  7.9 5.0 %collective-permute-done = bf16[4,128,128]{2,1,0:T(8,128)(2,1)S(1)} collective-permute-done((bf16[4,128,128]{2,1,0:T(8,128)(2,1)S(1)}, bf16[4,128,128]{2,1,0:T(8,128)(2,1)S(1)}, u32[]{:S(2)}, u32[]{:S(2)}) %collective-permute-start) | collective-permute-done | bytes 131104 | tf_op jit(solution)/shard_map/ppermute | solution.py:55
  13.0 0.0 copy-done.2
  13.0 0.0 copy-start
  13.0 0.0 copy-start.1
  13.0 0.2 broadcast_select_fusion.2
  13.2 1.0 collective-permute-start.3
  14.2 0.2 collective-permute-start.2
  14.4 0.1 pad_add_fusion.place_ref
  14.6 5.9 %collective-permute-done.3 = bf16[2,4,128,128]{3,2,0,1:T(8,128)(2,1)S(1)} collective-permute-done((bf16[2,4,128,128]{3,2,0,1:T(8,128)(2,1)S(1)}, bf16[2,4,128,128]{3,2,0,1:T(8,128)(2,1)S(1)}, u32[]{:S(2)}, u32[]{:S(2)}) %collective-permute-start.3) | collective-permute-done | bytes 262176 | tf_op jit(solution)/shard_map/ppermute | solution.py:55
  20.5 0.0 collective-permute-done.2
  20.5 0.0 copy-done
  20.6 0.0 copy-done.1
  20.6 6.9 %shard_map.76 = (f32[3456,128]{1,0:T(8,128)S(1)}, bf16[3456,128]{1,0:T(8,128)(2,1)S(1)}, bf16[2,2,128,128]{3,2,1,0:T(8,128)(2,1)S(1)}) custom-call(s32[2]{0:T(128)S(1)} %pad_add_fusion.place_ref, bf16[2,4,128,128]{3,2,1,0:T(8,128)(2,1)S(1)} %copy.15.near_ref, bf16[2,4,128,128]{3,2,1,0:T(8,128)(2,1)S(1)} %copy.16.far_ref, ...), custom_call_target="tpu_custom_call" | custom-call | flops 1811939328 | bytes 1048576 | tf_op jit(solution)/shard_map/pallas_call | solution.py:68
  27.5 0.1 collective-permute-start.4
  27.6 2.4 %collective-permute-done.4 = bf16[3456,128]{1,0:T(8,128)(2,1)S(1)} collective-permute-done((bf16[3456,128]{1,0:T(8,128)(2,1)S(1)}, bf16[3456,128]{1,0:T(8,128)(2,1)S(1)}, u32[]{:S(2)}, u32[]{:S(2)}) %collective-permute-start.4) | collective-permute-done | bytes 884768 | tf_op jit(solution)/shard_map/ppermute | solution.py:55
  30.0 1.1 %add_convert_fusion = bf16[3456,128]{1,0:T(8,128)(2,1)} fusion(f32[3456,128]{1,0:T(8,128)S(1)} %get-tuple-element.20, bf16[3456,128]{1,0:T(8,128)(2,1)S(1)} %collective-permute-done.4), kind=kLoop, calls=%fused_computation | loop fusion | flops 1327104 | bytes 3538944 | tf_op jit(solution)/shard_map/convert_element_type | solution.py:242
  31.1 10.3 %all-to-all-start = ((bf16[16,216,128]{2,1,0:T(8,128)(2,1)}), bf16[16,216,128]{2,1,0:T(8,128)(2,1)S(1)}, u32[]{:S(2)}, u32[]{:S(2)}) async-start(bf16[16,216,128]{2,1,0:T(8,128)(2,1)} %bitcast.14), calls=%async_computation | async-start | bytes 1769472 | tf_op jit(solution)/shard_map/all_to_all | solution.py:59
  41.5 0.7 collective-permute-start.6
  42.3 1.9 %collective-permute-start.5 = (bf16[2,128,128]{2,1,0:T(8,128)(2,1)S(1)}, bf16[2,128,128]{2,1,0:T(8,128)(2,1)S(1)}, u32[]{:S(2)}, u32[]{:S(2)}) collective-permute-start(bf16[2,128,128]{2,1,0:T(8,128)(2,1)S(1)} %get-tuple-element.40), channel_id=1, source_target_pairs={{0,1},{1,0},{2,3},{3,2},{4,5},{5,4},{6,7},{7,6},{8,9},{9,8},{10,11... | collective-permute-start | bytes 196616 | tf_op jit(solution)/shard_map/ppermute | solution.py:55
  44.2 0.0 collective-permute-done.6
  44.2 10.0 %collective-permute-done.5 = bf16[2,128,128]{2,1,0:T(8,128)(2,1)S(1)} collective-permute-done((bf16[2,128,128]{2,1,0:T(8,128)(2,1)S(1)}, bf16[2,128,128]{2,1,0:T(8,128)(2,1)S(1)}, u32[]{:S(2)}, u32[]{:S(2)}) %collective-permute-start.5) | collective-permute-done | bytes 65568 | tf_op jit(solution)/shard_map/ppermute | solution.py:55
  54.2 1.9 %all-to-all-done = bf16[16,216,128]{2,1,0:T(8,128)(2,1)S(1)} async-done(((bf16[16,216,128]{2,1,0:T(8,128)(2,1)}), bf16[16,216,128]{2,1,0:T(8,128)(2,1)S(1)}, u32[]{:S(2)}, u32[]{:S(2)}) %all-to-all-start) | async-done | bytes 884768 | tf_op jit(solution)/shard_map/all_to_all | solution.py:59
  56.1 0.1 reduce_sum.12
  56.2 0.1 collective-permute-start.7
  56.3 3.0 %collective-permute-done.7 = bf16[216,128]{1,0:T(8,128)(2,1)S(1)} collective-permute-done((bf16[216,128]{1,0:T(8,128)(2,1)S(1)}, bf16[216,128]{1,0:T(8,128)(2,1)S(1)}, u32[]{:S(2)}, u32[]{:S(2)}) %collective-permute-start.7) | collective-permute-done | bytes 55328 | tf_op jit(solution)/shard_map/ppermute | solution.py:55
  59.3 7.1 %collective-permute-start.10 = (bf16[216,128]{1,0:T(8,128)(2,1)S(1)}, bf16[216,128]{1,0:T(8,128)(2,1)S(1)}, u32[]{:S(2)}, u32[]{:S(2)}) collective-permute-start(bf16[216,128]{1,0:T(8,128)(2,1)S(1)} %add_convert_fusion.1), channel_id=1, source_target_pairs={{0,32},{1,33},{2,34},{3,35},{4,36},{5,37},{6,38},{7,39},{8,40},{9,... | collective-permute-start | bytes 165896 | tf_op jit(solution)/shard_map/ppermute | solution.py:55
  66.4 0.6 collective-permute-start.9
  67.0 0.0 collective-permute-start.8
  67.0 4.1 %collective-permute-start.12 = (bf16[2,4,128,128]{3,2,1,0:T(8,128)(2,1)S(1)}, bf16[2,4,128,128]{3,2,1,0:T(8,128)(2,1)S(1)}, u32[]{:S(2)}, u32[]{:S(2)}) collective-permute-start(bf16[2,4,128,128]{3,2,1,0:T(8,128)(2,1)S(1)} %pad_maximum_fusion.2.own_ref), channel_id=1, source_target_pairs={{0,1},{1,0},{2,3},{3,2},{4,5},{5,4},{6,7},{7,6},{8,9},{9,8},{10,11... | collective-permute-start | bytes 786440 | tf_op jit(solution)/shard_map/ppermute | solution.py:55
  71.1 1.1 %collective-permute-start.11 = (bf16[2,4,128,128]{3,2,1,0:T(8,128)(2,1)S(1)}, bf16[2,4,128,128]{3,2,1,0:T(8,128)(2,1)S(1)}, u32[]{:S(2)}, u32[]{:S(2)}) collective-permute-start(bf16[2,4,128,128]{3,2,1,0:T(8,128)(2,1)S(1)} %pad_maximum_fusion.2.own_ref), channel_id=1, source_target_pairs={{0,64},{1,65},{2,66},{3,67},{4,68},{5,69},{6,70},{7,71},{8,72},{9,... | collective-permute-start | bytes 786440 | tf_op jit(solution)/shard_map/ppermute | solution.py:55
  72.3 0.0 collective-permute-done.10
  72.3 0.4 collective-permute-done.9
  72.7 0.0 collective-permute-done.8
  72.7 3.5 %collective-permute-done.12.far_ref = bf16[2,4,128,128]{3,2,1,0:T(8,128)(2,1)S(1)} collective-permute-done((bf16[2,4,128,128]{3,2,1,0:T(8,128)(2,1)S(1)}, bf16[2,4,128,128]{3,2,1,0:T(8,128)(2,1)S(1)}, u32[]{:S(2)}, u32[]{:S(2)}) %collective-permute-start.12) | collective-permute-done | bytes 262176 | tf_op jit(solution)/shard_map/ppermute | solution.py:55
  76.3 0.0 collective-permute-done.11.near_ref
  76.3 0.1 broadcast_in_dim.45
  76.4 18.3 %all_to_all.10 = bf16[16,216,128]{2,1,0:T(8,128)(2,1)S(1)} all-to-all(bf16[16,216,128]{2,1,0:T(8,128)(2,1)S(1)} %broadcast_in_dim.45), channel_id=1, replica_groups={{0,1,2,3,4,5,6,7,8,9,10,11,12,13,14,15},{16,17,18,19,20,21,22,23,24,25,..., dimensions={0} | all-to-all | bytes 1769472 | tf_op jit(solution)/shard_map/all_to_all | solution.py:59
  94.7 2.0 %collective-permute-start.13 = (bf16[3456,128]{1,0:T(8,128)(2,1)S(1)}, bf16[3456,128]{1,0:T(8,128)(2,1)S(1)}, u32[]{:S(2)}, u32[]{:S(2)}) collective-permute-start(bf16[3456,128]{1,0:T(8,128)(2,1)S(1)} %bitcast.57), channel_id=1, source_target_pairs={{0,64},{1,65},{2,66},{3,67},{4,68},{5,69},{6,70},{7,71},{8,72},{9,... | collective-permute-start | bytes 2654216 | tf_op jit(solution)/shard_map/ppermute | solution.py:55
  96.7 2.3 %shard_map.77 = bf16[2,2,128,128]{3,2,1,0:T(8,128)(2,1)} custom-call(s32[2]{0:T(128)S(1)} %pad_add_fusion.place_ref, bf16[2,4,128,128]{3,2,1,0:T(8,128)(2,1)S(1)} %collective-permute-done.11.near_ref, bf16[2,4,128,128]{3,2,1,0:T(8,128)(2,1)S(1)} %collective-permute-done.12.far_ref, bf16[2,4,128,128]{3,2,1,0:T(8,128)(2,1)S(1)} %pad_maximum_fusion.2.own_ref, ...), custom_call_target="tpu_custom_call" | custom-call | flops 452984832 | bytes 1048576 | tf_op jit(solution)/shard_map/pallas_call | solution.py:68
  99.0 0.0 collective-permute-done.13
  99.0 0.2 broadcast_select_fusion
  99.2 1.4 %convert.5 = f32[3,3,3,128,128]{4,3,2,1,0:T(8,128)} convert(bf16[3,3,3,128,128]{4,3,2,1,0:T(8,128)(2,1)S(1)} %bitcast.59) | non-fusion elementwise | flops 442368 | bytes 2654208 | tf_op jit(solution)/shard_map/reshape | solution.py:267
  100.6 1.4 %convert.6 = f32[3,3,3,128,128]{4,3,2,1,0:T(8,128)} convert(bf16[3,3,3,128,128]{4,3,2,1,0:T(8,128)(2,1)S(1)} %bitcast.58) | non-fusion elementwise | flops 442368 | bytes 2654208 | tf_op jit(solution)/shard_map/reshape | solution.py:267
  (18 shorter events, 0.3 us)
Async XLA Ops:
  0.6 12.3 %copy-start.2 = (bf16[2,2,128,128]{3,2,1,0:T(8,128)(2,1)S(1)}, bf16[2,2,128,128]{3,2,1,0:T(8,128)(2,1)}, u32[]{:S(2)}) copy-start(bf16[2,2,128,128]{3,2,1,0:T(8,128)(2,1)} %param.7) | copy-start | bytes 393220
  3.4 4.4 %collective-permute-start.1 = (bf16[4,128,128]{2,1,0:T(8,128)(2,1)S(1)}, bf16[4,128,128]{2,1,0:T(8,128)(2,1)S(1)}, u32[]{:S(2)}, u32[]{:S(2)}) collective-permute-start(bf16[4,128,128]{2,1,0:T(8,128)(2,1)S(1)} %pad_maximum_fusion.3), channel_id=1, source_target_pairs={{0,64},{1,2},{2,1},{3,4},{4,3},{5,6},{6,5},{7,8},{8,7},{9,10},{10,... | collective-permute-start | bytes 393224 | tf_op jit(solution)/shard_map/ppermute | solution.py:55
  7.7 5.2 %collective-permute-start = (bf16[4,128,128]{2,1,0:T(8,128)(2,1)S(1)}, bf16[4,128,128]{2,1,0:T(8,128)(2,1)S(1)}, u32[]{:S(2)}, u32[]{:S(2)}) collective-permute-start(bf16[4,128,128]{2,1,0:T(8,128)(2,1)S(1)} %pad_maximum_fusion.4), channel_id=1, source_target_pairs={{0,1},{1,0},{2,3},{3,2},{4,5},{5,4},{6,7},{7,6},{8,9},{9,8},{10,11... | collective-permute-start | bytes 393224 | tf_op jit(solution)/shard_map/ppermute | solution.py:55
  13.0 7.6 %copy-start = (bf16[3,3,3,128,128]{4,3,2,1,0:T(8,128)(2,1)S(1)}, bf16[3,3,3,128,128]{4,3,2,1,0:T(8,128)(2,1)}, u32[]{:S(2)}) copy-start(bf16[3,3,3,128,128]{4,3,2,1,0:T(8,128)(2,1)} %param.8) | copy-start | bytes 2654212
  13.0 7.6 %copy-start.1 = (bf16[3,3,3,128,128]{4,3,2,1,0:T(8,128)(2,1)S(1)}, bf16[3,3,3,128,128]{4,3,2,1,0:T(8,128)(2,1)}, u32[]{:S(2)}) copy-start(bf16[3,3,3,128,128]{4,3,2,1,0:T(8,128)(2,1)} %param.9) | copy-start | bytes 2654212
  13.2 7.2 %collective-permute-start.3 = (bf16[2,4,128,128]{3,2,0,1:T(8,128)(2,1)S(1)}, bf16[2,4,128,128]{3,2,0,1:T(8,128)(2,1)S(1)}, u32[]{:S(2)}, u32[]{:S(2)}) collective-permute-start(bf16[2,4,128,128]{3,2,0,1:T(8,128)(2,1)S(1)} %get-tuple-element.31), channel_id=1, source_target_pairs={{0,1},{1,0},{2,3},{3,2},{4,5},{5,4},{6,7},{7,6},{8,9},{9,8},{10,11... | collective-permute-start | bytes 786440 | tf_op jit(solution)/shard_map/ppermute | solution.py:55
  14.2 6.3 %collective-permute-start.2 = (bf16[2,4,128,128]{3,2,0,1:T(8,128)(2,1)S(1)}, bf16[2,4,128,128]{3,2,0,1:T(8,128)(2,1)S(1)}, u32[]{:S(2)}, u32[]{:S(2)}) collective-permute-start(bf16[2,4,128,128]{3,2,0,1:T(8,128)(2,1)S(1)} %get-tuple-element.32), channel_id=1, source_target_pairs={{0,64},{1,65},{2,66},{3,67},{4,68},{5,69},{6,70},{7,71},{8,72},{9,... | collective-permute-start | bytes 786440 | tf_op jit(solution)/shard_map/ppermute | solution.py:55
  27.5 2.5 %collective-permute-start.4 = (bf16[3456,128]{1,0:T(8,128)(2,1)S(1)}, bf16[3456,128]{1,0:T(8,128)(2,1)S(1)}, u32[]{:S(2)}, u32[]{:S(2)}) collective-permute-start(bf16[3456,128]{1,0:T(8,128)(2,1)S(1)} %get-tuple-element.21), channel_id=1, source_target_pairs={{0,64},{1,65},{2,66},{3,67},{4,68},{5,69},{6,70},{7,71},{8,72},{9,... | collective-permute-start | bytes 2654216 | tf_op jit(solution)/shard_map/ppermute | solution.py:55
  31.1 24.9 %all-to-all-start = ((bf16[16,216,128]{2,1,0:T(8,128)(2,1)}), bf16[16,216,128]{2,1,0:T(8,128)(2,1)S(1)}, u32[]{:S(2)}, u32[]{:S(2)}) async-start(bf16[16,216,128]{2,1,0:T(8,128)(2,1)} %bitcast.14), calls=%async_computation | async-start | bytes 1769472 | tf_op jit(solution)/shard_map/all_to_all | solution.py:59
  41.5 2.6 %collective-permute-start.6 = (bf16[2,128,128]{2,1,0:T(8,128)(2,1)S(1)}, bf16[2,128,128]{2,1,0:T(8,128)(2,1)S(1)}, u32[]{:S(2)}, u32[]{:S(2)}) collective-permute-start(bf16[2,128,128]{2,1,0:T(8,128)(2,1)S(1)} %get-tuple-element.39), channel_id=1, source_target_pairs={{0,64},{1,2},{2,1},{3,4},{4,3},{5,6},{6,5},{7,8},{8,7},{9,10},{10,... | collective-permute-start | bytes 196616 | tf_op jit(solution)/shard_map/ppermute | solution.py:55
  42.3 11.9 %collective-permute-start.5 = (bf16[2,128,128]{2,1,0:T(8,128)(2,1)S(1)}, bf16[2,128,128]{2,1,0:T(8,128)(2,1)S(1)}, u32[]{:S(2)}, u32[]{:S(2)}) collective-permute-start(bf16[2,128,128]{2,1,0:T(8,128)(2,1)S(1)} %get-tuple-element.40), channel_id=1, source_target_pairs={{0,1},{1,0},{2,3},{3,2},{4,5},{5,4},{6,7},{7,6},{8,9},{9,8},{10,11... | collective-permute-start | bytes 196616 | tf_op jit(solution)/shard_map/ppermute | solution.py:55
  56.2 3.1 %collective-permute-start.7 = (bf16[216,128]{1,0:T(8,128)(2,1)S(1)}, bf16[216,128]{1,0:T(8,128)(2,1)S(1)}, u32[]{:S(2)}, u32[]{:S(2)}) collective-permute-start(bf16[216,128]{1,0:T(8,128)(2,1)S(1)} %reduce_sum.12), channel_id=1, source_target_pairs={{0,128},{1,129},{2,130},{3,131},{4,132},{5,133},{6,134},{7,135},{8... | collective-permute-start | bytes 165896 | tf_op jit(solution)/shard_map/ppermute | solution.py:55
  59.3 13.0 %collective-permute-start.10 = (bf16[216,128]{1,0:T(8,128)(2,1)S(1)}, bf16[216,128]{1,0:T(8,128)(2,1)S(1)}, u32[]{:S(2)}, u32[]{:S(2)}) collective-permute-start(bf16[216,128]{1,0:T(8,128)(2,1)S(1)} %add_convert_fusion.1), channel_id=1, source_target_pairs={{0,32},{1,33},{2,34},{3,35},{4,36},{5,37},{6,38},{7,39},{8,40},{9,... | collective-permute-start | bytes 165896 | tf_op jit(solution)/shard_map/ppermute | solution.py:55
  66.4 6.3 %collective-permute-start.9 = (bf16[216,128]{1,0:T(8,128)(2,1)S(1)}, bf16[216,128]{1,0:T(8,128)(2,1)S(1)}, u32[]{:S(2)}, u32[]{:S(2)}) collective-permute-start(bf16[216,128]{1,0:T(8,128)(2,1)S(1)} %add_convert_fusion.1), channel_id=1, source_target_pairs={{0,48},{1,49},{2,50},{3,51},{4,52},{5,53},{6,54},{7,55},{8,56},{9,... | collective-permute-start | bytes 165896 | tf_op jit(solution)/shard_map/ppermute | solution.py:55
  67.0 5.7 %collective-permute-start.8 = (bf16[216,128]{1,0:T(8,128)(2,1)S(1)}, bf16[216,128]{1,0:T(8,128)(2,1)S(1)}, u32[]{:S(2)}, u32[]{:S(2)}) collective-permute-start(bf16[216,128]{1,0:T(8,128)(2,1)S(1)} %add_convert_fusion.1), channel_id=1, source_target_pairs={{0,16},{1,17},{2,18},{3,19},{4,20},{5,21},{6,22},{7,23},{8,24},{9,... | collective-permute-start | bytes 165896 | tf_op jit(solution)/shard_map/ppermute | solution.py:55
  67.0 9.2 %collective-permute-start.12 = (bf16[2,4,128,128]{3,2,1,0:T(8,128)(2,1)S(1)}, bf16[2,4,128,128]{3,2,1,0:T(8,128)(2,1)S(1)}, u32[]{:S(2)}, u32[]{:S(2)}) collective-permute-start(bf16[2,4,128,128]{3,2,1,0:T(8,128)(2,1)S(1)} %pad_maximum_fusion.2.own_ref), channel_id=1, source_target_pairs={{0,1},{1,0},{2,3},{3,2},{4,5},{5,4},{6,7},{7,6},{8,9},{9,8},{10,11... | collective-permute-start | bytes 786440 | tf_op jit(solution)/shard_map/ppermute | solution.py:55
  71.1 5.1 %collective-permute-start.11 = (bf16[2,4,128,128]{3,2,1,0:T(8,128)(2,1)S(1)}, bf16[2,4,128,128]{3,2,1,0:T(8,128)(2,1)S(1)}, u32[]{:S(2)}, u32[]{:S(2)}) collective-permute-start(bf16[2,4,128,128]{3,2,1,0:T(8,128)(2,1)S(1)} %pad_maximum_fusion.2.own_ref), channel_id=1, source_target_pairs={{0,64},{1,65},{2,66},{3,67},{4,68},{5,69},{6,70},{7,71},{8,72},{9,... | collective-permute-start | bytes 786440 | tf_op jit(solution)/shard_map/ppermute | solution.py:55
  94.7 4.3 %collective-permute-start.13 = (bf16[3456,128]{1,0:T(8,128)(2,1)S(1)}, bf16[3456,128]{1,0:T(8,128)(2,1)S(1)}, u32[]{:S(2)}, u32[]{:S(2)}) collective-permute-start(bf16[3456,128]{1,0:T(8,128)(2,1)S(1)} %bitcast.57), channel_id=1, source_target_pairs={{0,64},{1,65},{2,66},{3,67},{4,68},{5,69},{6,70},{7,71},{8,72},{9,... | collective-permute-start | bytes 2654216 | tf_op jit(solution)/shard_map/ppermute | solution.py:55

commit v2 on v1

v2 whole, which is shorter than its diff:
```python
import math

import jax
import jax.numpy as jnp
from jax import lax
from jax.experimental import pallas as pl
from jax.experimental.pallas import tpu as pltpu
from jax.sharding import PartitionSpec as P

BF = jnp.bfloat16
F32 = jnp.float32
AXES = ("tm", "height")
TM, HEIGHT = 4, 64
COUNT = TM * HEIGHT
C = 128
ROWS = 27 * C
PART = ROWS // 16


def tm_pairs(first):
    pairs = []
    for tm in range(TM):
        for h in range(HEIGHT):
            if first:
                pairs.append((tm * HEIGHT + h, (tm ^ 1) * HEIGHT + h))
            elif tm in (1, 2):
                pairs.append((tm * HEIGHT + h, (3 - tm) * HEIGHT + h))
            else:
                pairs.append((tm * HEIGHT + h, tm * HEIGHT + (h ^ 1)))
    return pairs


def height_pairs(odd):
    pairs = []
    for tm in range(TM):
        for h in range(HEIGHT):
            up = (h % 2 == 1) if odd else (h % 2 == 0)
            other = h + 1 if up else h - 1
            if 0 <= other < HEIGHT:
                pairs.append((tm * HEIGHT + h, tm * HEIGHT + other))
            else:
                pairs.append((tm * HEIGHT + h, (tm ^ 1) * HEIGHT + h))
    return pairs


def flip_pairs(mask):
    return [(d, d ^ mask) for d in range(COUNT)]


SIBLING = flip_pairs(64)
PLANE = [[base + n for n in range(16)] for base in range(0, COUNT, 16)]


def send(value, pairs):
    return lax.ppermute(value, AXES, pairs)


def exchange(value):
    return lax.all_to_all(value, AXES, 0, 0, axis_index_groups=PLANE, tiled=True)


VMEM = pl.BlockSpec(memory_space=pltpu.VMEM)
SMEM = pl.BlockSpec(memory_space=pltpu.SMEM)
ANY = pl.BlockSpec(memory_space=pl.ANY)


def call(kernel, outs, ins, scratch=(), specs=None, out_specs=None, flops=0, moved=1 << 20, limit=8):
    return pl.pallas_call(
        kernel,
        out_shape=[jax.ShapeDtypeStruct(shape, kind) for shape, kind in outs],
        in_specs=specs or [VMEM] * len(ins),
        out_specs=out_specs or [VMEM] * len(outs),
        scratch_shapes=list(scratch),
        compiler_params=pltpu.CompilerParams(vmem_limit_bytes=limit << 20),
        cost_estimate=pl.CostEstimate(flops=flops, bytes_accessed=moved, transcendentals=0),
    )(*ins)


def columns(value):
    wide = value.astype(F32)
    row = lax.broadcasted_iota(jnp.int32, wide.shape, 0)
    before = jnp.where(row == 0, 0.0, pltpu.roll(wide, 1, 0)).astype(BF)
    after = jnp.where(row == 127, 0.0, pltpu.roll(wide, 127, 0)).astype(BF)
    return before, value, after


def dot(a, b):
    return lax.dot_general(a, b, (((1,), (0,)), ((), ())), preferred_element_type=F32)


def dot_nt(a, b):
    return lax.dot_general(a, b, (((1,), (1,)), ((), ())), preferred_element_type=F32)


def turned(kernel_ref, i, j):
    base = (2 - i) * 9 + (2 - j) * 3
    return jnp.concatenate([kernel_ref[base + 2], kernel_ref[base + 1], kernel_ref[base]], axis=1)


def fill(slab, t, r, value):
    for k, part in enumerate(columns(value)):
        slab[t, r, :, k * C : (k + 1) * C] = part


def fill_turned(turned_ref, t, r, value):
    flipped = value.T
    if r < 3:
        turned_ref[t, r, :, 0:C] = flipped
    if r > 0:
        turned_ref[t, r - 1, :, C : 2 * C] = flipped


def rows_of(slab, frames, j):
    return slab[frames, j : j + 2].reshape(-1, slab.shape[3])


BOTH, FIRST, SECOND = slice(0, 2), slice(0, 1), slice(1, 2)


def own_kernel(
    place_ref, value_ref, margin_ref, one_ref, two_ref,
    turned_ref, pre_ref, hid_ref, slab_i, slab_g,
):
    core = place_ref[0]
    for t in range(2):
        for r in range(4):
            first, second = (
                value_ref[n, t, r - 1] if 0 < r < 3 else margin_ref[n, t, r // 3] for n in range(2)
            )
            fill(slab_i, t, r, first)
            fill(slab_g, t, r, second)
            fill_turned(turned_ref, t, r, jnp.where(core == 0, first, second).astype(BF))
    pre = jnp.zeros((512, C), F32)
    hid = jnp.zeros((512, C), F32)
    pre_1 = jnp.zeros((256, C), F32)
    hid_0 = jnp.zeros((256, C), F32)
    for j in range(3):
        pre += dot(rows_of(slab_i, BOTH, j), one_ref[6 + j])
        pre_1 += dot(rows_of(slab_i, FIRST, j), one_ref[3 + j])
        hid += dot_nt(rows_of(slab_g, BOTH, j), turned(two_ref, 0, j))
        hid_0 += dot_nt(rows_of(slab_g, SECOND, j), turned(two_ref, 1, j))
    pre_ref[0:256] = pre[0:256]
    pre_ref[256:512] = pre[256:512] + pre_1
    hid_ref[0:256] = hid[0:256] + hid_0
    hid_ref[256:512] = hid[256:512]


def pick(own_ref, margin_ref, t, r, *n):
    return own_ref[(*n, t, r - 1)] if 0 < r < 3 else margin_ref[(*n, t, r // 3)]


def rest_kernel(
    place_ref, near_own, near_margin, far_own, far_margin, pre_ref, hid_ref, one_ref, two_ref,
    stay_ref, leave_ref, pre_grad_ref, past_i, later_g,
):
    core = place_ref[0]
    for t in range(2):
        for r in range(4):
            far = pick(far_own, far_margin, t, r)
            value = jnp.where(core == 1, pick(near_own, near_margin, t, r, 0), far)
            fill(past_i, t, r, jnp.where(place_ref[1] > 0, value, 0).astype(BF))
            value = jnp.where(core == 0, pick(near_own, near_margin, t, r, 1), far)
            fill(later_g, t, r, jnp.where(place_ref[1] < TM - 1, value, 0).astype(BF))
    pre = pre_ref[...]
    hid = hid_ref[...]
    pre_0 = jnp.zeros((256, C), F32)
    hid_1 = jnp.zeros((256, C), F32)
    for j in range(3):
        pre += dot(rows_of(past_i, BOTH, j), one_ref[j])
        pre_0 += dot(rows_of(past_i, SECOND, j), one_ref[3 + j])
        hid += dot_nt(rows_of(later_g, BOTH, j), turned(two_ref, 2, j))
        hid_1 += dot_nt(rows_of(later_g, FIRST, j), turned(two_ref, 1, j))
    pre = jnp.concatenate([pre[0:256] + pre_0, pre[256:512]], axis=0)
    hid = jnp.concatenate([hid[0:256], hid[256:512] + hid_1], axis=0)
    gate = 1.0 / (1.0 + jnp.exp(-pre))
    hidden = (pre * gate).astype(BF).reshape(2, 2, C, C)
    pre_grad = (hid * gate * (1.0 + pre * (1.0 - gate))).astype(BF).reshape(2, 2, C, C)
    pre_grad_ref[...] = pre_grad
    stay_ref[...] = jnp.where(core == 0, pre_grad, hidden).astype(BF)
    leave_ref[...] = jnp.where(core == 0, hidden, pre_grad).astype(BF)


def turn_kernel(place_ref, near_own, near_margin, far_own, far_margin, low_ref, high_ref):
    core = place_ref[0]
    inner = (place_ref[1] == 1) | (place_ref[1] == 2)
    for t in range(2):
        for r in range(4):
            far = jnp.where(inner, pick(far_own, far_margin, t, r), 0).astype(BF)
            first = pick(near_own, near_margin, t, r, 0)
            second = pick(near_own, near_margin, t, r, 1)
            fill_turned(low_ref, t, r, jnp.where(core == 0, far, second).astype(BF))
            fill_turned(high_ref, t, r, jnp.where(core == 0, first, far).astype(BF))


def sums_kernel(place_ref, stay_ref, got_ref, low_ref, own_ref, high_ref, out_ref, slab):
    core = place_ref[0]
    for t in range(4):
        for r in range(2):
            early, late = (stay_ref, got_ref) if t < 2 else (got_ref, stay_ref)
            value = jnp.where(core == 0, early[t % 2, r], late[t % 2, r]).astype(BF)
            for k, part in enumerate(columns(value)):
                slab[t, r * C : (r + 1) * C, k * C : (k + 1) * C] = part
    frames = [ref.at[t] for ref in (low_ref, own_ref, high_ref) for t in range(2)]
    for i in range(3):
        total = jnp.zeros((3 * C, 3 * C), F32)
        for t in range(4):
            total += dot(frames[i + t][...].reshape(3 * C, 2 * C), slab[t])
        total = total.astype(BF)
        for j in range(3):
            for k in range(3):
                n = i * 9 + j * 3 + k
                out_ref[n * C : (n + 1) * C, :] = total[j * C : (j + 1) * C, k * C : (k + 1) * C]


def in_grad_kernel(place_ref, near_ref, far_ref, own_ref, one_ref, out_ref, slab):
    def later(t, r):
        value = jnp.where(place_ref[0] == 0, near_ref[t, r], far_ref[t, r])
        return jnp.where(place_ref[1] < TM - 1, value, 0).astype(BF)

    for t in range(4):
        for r in range(4):
            value = own_ref[t, r] if t < 2 else later(t - 2, r)
            for k, part in enumerate(columns(value)):
                slab[t, r, :, k * C : (k + 1) * C] = part
    total = jnp.zeros((512, C), F32)
    for i in range(3):
        for j in range(3):
            total += dot_nt(slab[i : i + 2, j : j + 2].reshape(512, 3 * C), turned(one_ref, i, j))
    out_ref[...] = total.astype(BF).reshape(2, 2, C, C)


def write_kernel(half, place_ref, part_ref, *refs):
    targets, whole, sems = refs[-4:-2], refs[-2], refs[-1]
    third = ROWS // 3

    def copy(kind, i):
        rows = pl.ds(i * third, third)
        return pltpu.make_async_copy(whole.at[rows, :], targets[kind].at[rows, :], sems.at[i])

    for kind in range(2):

        @pl.when(place_ref[0] == (kind + half) % 2)
        def _():
            for i in range(3):
                for j in range(3):
                    for k in range(3):
                        n = (i * 9 + j * 3 + k) * C
                        value = part_ref[n : n + C, :]
                        if kind:
                            m = ((2 - i) * 9 + (2 - j) * 3 + k) * C
                            value = value.T
                        else:
                            m = (i * 9 + j * 3 + 2 - k) * C
                        whole[m : m + C, :] = value.astype(F32)
                copy(kind, 2 - i if kind else i).start()
            for i in range(3):
                copy(kind, i).wait()


def write(half, where, part, targets=()):
    return pl.pallas_call(
        lambda *refs: write_kernel(half, *refs),
        out_shape=[jax.ShapeDtypeStruct((ROWS, C), F32)] * 2,
        in_specs=[SMEM, VMEM] + [ANY] * len(targets),
        out_specs=[ANY, ANY],
        input_output_aliases={2 + n: n for n in range(len(targets))},
        scratch_shapes=[pltpu.VMEM((ROWS, C), F32), pltpu.SemaphoreType.DMA((3,))],
        compiler_params=pltpu.CompilerParams(vmem_limit_bytes=8 << 20),
        cost_estimate=pl.CostEstimate(flops=0, bytes_accessed=3 << 20, transcendentals=0),
    )(where, part, *targets)


def body(quantized, exponents, out_grad, kernel_one, kernel_two):
    tm = lax.axis_index("tm")
    index = lax.axis_index("height")
    core = tm % 2
    odd = index % 2 == 1
    where = jnp.stack([core, tm, index % 2]).astype(jnp.int32)
    one = kernel_one.reshape(27, C, C)
    two = kernel_two.reshape(27, C, C)
    nine = one.reshape(9, 3 * C, C)
    block = (2, 2, C, C)

    def met(near, far):
        inside = jnp.where(odd, index < HEIGHT - 1, index > 0)
        far = lax.optimization_barrier(jnp.where(inside, far, 0))
        before = jnp.where(odd, near, far)
        after = jnp.where(odd, far, near)
        return before, after

    def band(before, value, after):
        return jnp.concatenate([before[:, None], value, after[:, None]], axis=1)

    scale = jnp.exp2(exponents.astype(F32))
    scale = jnp.repeat(jnp.transpose(scale, (1, 2, 0)), C // 4, axis=2)
    scale = jnp.stack([scale, jnp.ones_like(scale)])[:, :, :, None, :]
    both = lax.optimization_barrier(jnp.stack([quantized, out_grad]))
    both = (both.astype(F32) * scale).astype(BF)
    pair = (4, C, C)
    near = send(jnp.where(odd, both[:, :, 0], both[:, :, 1]).reshape(pair), height_pairs(False))
    far = send(jnp.where(odd, both[:, :, 1], both[:, :, 0]).reshape(pair), height_pairs(True))
    near_own = send(both, tm_pairs(True))
    far_own = send(jnp.where(core == 0, both[1], both[0]), tm_pairs(False))
    before, after = met(near, far)
    margin = jnp.stack([before.reshape(2, 2, C, C), after.reshape(2, 2, C, C)], axis=2)
    near_margin = send(margin, tm_pairs(True))
    far_margin = send(jnp.where(core == 0, margin[1], margin[0]), tm_pairs(False))
    slab = (2, 4, C, 3 * C)
    flipped = (2, 3, C, 2 * C)
    half = 2 * 27 * C * C * 512
    middle, pre, hid = call(
        own_kernel,
        [(flipped, BF), ((512, C), F32), ((512, C), F32)],
        [where, both, margin, nine, two],
        specs=[SMEM] + [VMEM] * 4,
        scratch=[pltpu.VMEM(slab, BF), pltpu.VMEM(slab, BF)],
        flops=half,
        limit=16,
    )
    beside = [near_own, near_margin, far_own, far_margin]
    stay, leave, pre_grad = call(
        rest_kernel,
        [(block, BF)] * 3,
        [where, *beside, pre, hid, nine, two],
        specs=[SMEM] + [VMEM] * 8,
        scratch=[pltpu.VMEM(slab, BF), pltpu.VMEM(slab, BF)],
        flops=half,
        limit=16,
    )
    low, high = call(
        turn_kernel,
        [(flipped, BF)] * 2,
        [where, *beside],
        specs=[SMEM] + [VMEM] * 4,
        limit=16,
    )
    got = send(leave, SIBLING)
    (total,) = call(
        sums_kernel,
        [((ROWS, C), BF)],
        [where, stay, got, low, middle, high],
        specs=[SMEM] + [VMEM] * 5,
        scratch=[pltpu.VMEM((4, 2 * C, 3 * C), BF)],
        flops=2 * half,
        limit=16,
    )
    near = send(jnp.where(odd, pre_grad[:, 0], pre_grad[:, 1]), height_pairs(False))
    far = send(jnp.where(odd, pre_grad[:, 1], pre_grad[:, 0]), height_pairs(True))
    before, after = met(near, far)
    total = jnp.sum(exchange(total.reshape(16, PART, C)).astype(F32), axis=0).astype(BF)
    total, before, after = lax.optimization_barrier((total, before, after))
    pre_banded = band(before, pre_grad, after)
    pre_near = send(pre_banded, tm_pairs(True))
    pre_far = send(pre_banded, tm_pairs(False))
    total = total.astype(F32) + send(total, flip_pairs(128)).astype(F32)
    total = total.astype(BF)
    others = [send(total, flip_pairs(16 * n)).astype(F32) for n in (1, 3, 2)]
    factor = 1.0 / math.sqrt(8 * 128 * 128)
    total = (((total.astype(F32) + others[0]) + (others[1] + others[2])) * factor).astype(BF)
    total, pre_near, pre_far = lax.optimization_barrier((total, pre_near, pre_far))
    mine = exchange(jnp.broadcast_to(total[None], (16, PART, C))).reshape(ROWS, C)
    (in_grad,) = call(
        in_grad_kernel,
        [(block, BF)],
        [where, pre_near, pre_far, pre_banded, one],
        specs=[SMEM] + [VMEM] * 4,
        scratch=[pltpu.VMEM((4, 4, C, 3 * C), BF)],
        flops=2 * 27 * C * C * 512,
    )
    mine, in_grad = lax.optimization_barrier((mine, in_grad))
    theirs = send(mine, SIBLING)
    totals = write(0, where, mine)
    one_total, two_total = write(1, where, theirs, totals)
    shape = (3, 3, 3, C, C)
    return (in_grad, one_total.reshape(shape), two_total.reshape(shape))


def solution(mesh):
    placed = (
        P("tm", "height", None, None),
        P(None, "tm", "height"),
        P("tm", "height", None, None),
        P(),
        P(),
    )
    return jax.shard_map(
        body,
        mesh=mesh,
        in_specs=placed,
        out_specs=(P("tm", "height", None, None), P(), P()),
        check_vma=False,
    )
```

time: 102 us -> 96.3 us (0.944)
  blocking collectives: 18.3 us -> 0 us
  starting transfers between devices: 32.7 us -> 40.1 us
  waiting for transfers between devices: 32.2 us -> 38.4 us
  other arithmetic: 8.22 us -> 2.35 us
  Pallas kernels: 9.25 us -> 13 us
    all_to_all x1 -> x0, blocking collectives: 18.3 us -> none  [exchange(): lax.all_to_all(value, AXES, 0, 0, axis_index_groups=PLANE, tiled=True)]
    all_to_all x1 -> x2, waiting for transfers between devices: 1.9 us -> 13.4 us  [exchange(): lax.all_to_all(value, AXES, 0, 0, axis_index_groups=PLANE, tiled=True)]
    ppermute x14 -> x16, waiting for transfers between devices: 30.3 us -> 25 us  [send(): return lax.ppermute(value, AXES, pairs)]
    ppermute x14 -> x16, starting transfers between devices: 22.3 us -> 26.6 us  [send(): return lax.ppermute(value, AXES, pairs)]
    pallas_call x0 -> x2, Pallas kernels: none -> 3.73 us  [write(): pl.pallas_call(lambda *refs: write_kernel(half, *refs), out_shape=[jax.Sh...]
    all_to_all x1 -> x2, starting transfers between devices: 10.3 us -> 13.5 us  [exchange(): lax.all_to_all(value, AXES, 0, 0, axis_index_groups=PLANE, tiled=True)]
    convert_element_type x3 -> x1, other arithmetic: 2.93 us -> 0.06 us  [body(): both = (both.astype(F32) * scale).astype(BF)]
    reshape x2 -> x0, other arithmetic: 2.81 us -> none  [body(): return (in_grad, one_total.reshape(shape), two_total.reshape(shape))]
  transfers between devices with their start and end apart: 15 -> 18, of which waited for: 8 -> 10; matrix products, arithmetic and copies ran while one was open for 1% -> 0% of each run, Pallas kernels for 2% -> 7%
where the time goes in v2:
time: 96.3 us; the launch traced here: 96 us
  starting transfers between devices  40.1 us (42%)
  waiting for transfers between devices  38.4 us (40%)
  Pallas kernels  13 us (13%)
  other arithmetic  2.35 us (2%)
  local copies, waits for them, and re-layouts  1.2 us (1%)
    ppermute x16, starting transfers between devices, send(): return lax.ppermute(value, AXES, pairs)  26.6 us
    ppermute x16, waiting for transfers between devices, send(): return lax.ppermute(value, AXES, pairs)  25 us
    all_to_all x2, starting transfers between devices, exchange(): lax.all_to_all(value, AXES, 0, 0, axis_index_groups=PLANE, tiled=True)  13.5 us
    all_to_all x2, waiting for transfers between devices, exchange(): lax.all_to_all(value, AXES, 0, 0, axis_index_groups=PLANE, tiled=True)  13.4 us
    pallas_call x5, Pallas kernels, call(): pl.pallas_call(kernel, out_shape=[jax.ShapeDtypeStruct(shape, kind) for s...  9.29 us
    pallas_call x2, Pallas kernels, write(): pl.pallas_call(lambda *refs: write_kernel(half, *refs), out_shape=[jax.Sh...  3.73 us
  transfers between devices with their start and end apart: 18, of which 10 were waited for; matrix products, arithmetic and copies ran while one was open for 0% of the time, Pallas kernels for 7%

profile of v2, /device:TPU:1, one launch (start us, length us, event | category | flops | bytes accessed | tf_op | source)
XLA Modules:
  0.0 96.0 jit_solution(10520098537289460539)
XLA Ops:
  0.6 0.7 exponential_bitcast_fusion
  1.3 0.1 broadcast_in_dim.24
  1.4 0.1 stack_reshape.9
  1.5 0.0 copy-start
  1.5 0.0 copy-start.1
  1.5 1.1 %pad_maximum_fusion.1 = bf16[2,2,2,128,128]{4,3,2,1,0:T(8,128)(2,1)S(1)} fusion(bf16[1,2,2,128,128]{4,3,2,1,0:T(8,128)(2,1)} %bitcast.47, bf16[1,2,2,128,128]{4,3,2,1,0:T(8,128)(2,1)} %bitcast.48), kind=kLoop, calls=%fused_computation.6 | loop fusion | flops 131072 | bytes 524288 | tf_op jit(solution)/shard_map/stack | solution.py:297
  2.6 0.1 multiply_convert_fusion.value_ref
  2.7 3.3 %collective-permute-start = (bf16[2,2,2,128,128]{4,3,2,1,0:T(8,128)(2,1)S(1)}, bf16[2,2,2,128,128]{4,3,2,1,0:T(8,128)(2,1)S(1)}, u32[]{:S(2)}, u32[]{:S(2)}) collective-permute-start(bf16[2,2,2,128,128]{4,3,2,1,0:T(8,128)(2,1)S(1)} %multiply_convert_fusion.value_ref), channel_id=1, source_target_pairs={{0,64},{1,65},{2,66},{3,67},{4,68},{5,69},{6,70},{7,71},{8,72},{9,... | collective-permute-start | bytes 786440 | tf_op jit(solution)/shard_map/ppermute | solution.py:55
  6.0 0.1 collective-permute-start.2
  6.2 0.3 collective-permute-start.4
  6.5 2.2 %collective-permute-start.1 = (bf16[4,128,128]{2,1,0:T(8,128)(2,1)S(1)}, bf16[4,128,128]{2,1,0:T(8,128)(2,1)S(1)}, u32[]{:S(2)}, u32[]{:S(2)}) collective-permute-start(bf16[4,128,128]{2,1,0:T(8,128)(2,1)S(1)} %bitcast.45), channel_id=1, source_target_pairs={{0,1},{1,0},{2,3},{3,2},{4,5},{5,4},{6,7},{7,6},{8,9},{9,8},{10,11... | collective-permute-start | bytes 393224 | tf_op jit(solution)/shard_map/ppermute | solution.py:55
  8.8 0.0 collective-permute-done.2
  8.8 4.0 %collective-permute-done.1 = bf16[4,128,128]{2,1,0:T(8,128)(2,1)S(1)} collective-permute-done((bf16[4,128,128]{2,1,0:T(8,128)(2,1)S(1)}, bf16[4,128,128]{2,1,0:T(8,128)(2,1)S(1)}, u32[]{:S(2)}, u32[]{:S(2)}) %collective-permute-start.1) | collective-permute-done | bytes 131104 | tf_op jit(solution)/shard_map/ppermute | solution.py:55
  12.9 1.8 %collective-permute-start.3 = (bf16[2,2,2,128,128]{4,3,2,1,0:T(8,128)(2,1)S(1)}, bf16[2,2,2,128,128]{4,3,2,1,0:T(8,128)(2,1)S(1)}, u32[]{:S(2)}, u32[]{:S(2)}) collective-permute-start(bf16[2,2,2,128,128]{4,3,2,1,0:T(8,128)(2,1)S(1)} %pad_maximum_fusion.margin_ref), channel_id=1, source_target_pairs={{0,64},{1,65},{2,66},{3,67},{4,68},{5,69},{6,70},{7,71},{8,72},{9,... | collective-permute-start | bytes 786440 | tf_op jit(solution)/shard_map/ppermute | solution.py:55
  14.7 0.1 collective-permute-start.5
  14.8 0.1 pad_add_fusion.place_ref.refs_0_
  14.9 0.0 copy-done
  14.9 0.0 copy-done.1
  14.9 1.6 %shard_map.76 = (bf16[2,3,128,256]{3,2,1,0:T(8,128)(2,1)S(1)}, f32[512,128]{1,0:T(8,128)S(1)}, f32[512,128]{1,0:T(8,128)S(1)}) custom-call(s32[3]{0:T(128)S(1)} %pad_add_fusion.place_ref.refs_0_, bf16[2,2,2,128,128]{4,3,2,1,0:T(8,128)(2,1)S(1)} %multiply_convert_fusion.value_ref, bf16[2,2,2,128,128]{4,3,2,1,0:T(8,128)(2,1)S(1)} %pad_maximum_fusion.margin_ref, ...), custom_call_target="tpu_custom_call" | custom-call | flops 452984832 | bytes 1048576 | tf_op jit(solution)/shard_map/pallas_call | solution.py:68
  16.5 0.0 collective-permute-done.4.far_own
  16.5 2.8 %collective-permute-done.5.far_margin = bf16[2,2,128,128]{3,2,1,0:T(8,128)(2,1)S(1)} collective-permute-done((bf16[2,2,128,128]{3,2,1,0:T(8,128)(2,1)S(1)}, bf16[2,2,128,128]{3,2,1,0:T(8,128)(2,1)S(1)}, u32[]{:S(2)}, u32[]{:S(2)}) %collective-permute-start.5) | collective-permute-done | bytes 131104 | tf_op jit(solution)/shard_map/ppermute | solution.py:55
  19.4 0.0 collective-permute-done.near_own
  19.4 0.0 collective-permute-done.3.near_margin
  19.4 1.7 %shard_map.77 = (bf16[2,2,128,128]{3,2,1,0:T(8,128)(2,1)S(1)}, bf16[2,2,128,128]{3,2,1,0:T(8,128)(2,1)S(1)}, bf16[2,2,128,128]{3,2,1,0:T(8,128)(2,1)S(1)}) custom-call(s32[3]{0:T(128)S(1)} %pad_add_fusion.place_ref.refs_0_, bf16[2,2,2,128,128]{4,3,2,1,0:T(8,128)(2,1)S(1)} %collective-permute-done.near_own, ...), custom_call_target="tpu_custom_call" | custom-call | flops 452984832 | bytes 1048576 | tf_op jit(solution)/shard_map/pallas_call | solution.py:68
  21.1 0.5 collective-permute-start.6
  21.6 0.7 shard_map.78
  22.3 0.2 collective-permute-done.6.got_ref
  22.6 2.9 %shard_map.79 = bf16[3456,128]{1,0:T(8,128)(2,1)} custom-call(s32[3]{0:T(128)S(1)} %pad_add_fusion.place_ref.refs_0_, bf16[2,2,128,128]{3,2,1,0:T(8,128)(2,1)S(1)} %get-tuple-element.25.stay_ref, bf16[2,2,128,128]{3,2,1,0:T(8,128)(2,1)S(1)} %collective-permute-done.6.got_ref, bf16[2,3,128,256]{3,2,1,0:T(8,128)(2,1)S(1)} %get-tuple-element.27.low_ref, ...), custom_call_target="tpu_custom_call" | custom-call | flops 905969664 | bytes 1048576 | tf_op jit(solution)/shard_map/pallas_call | solution.py:68
  25.5 9.9 %all-to-all-start = ((bf16[16,216,128]{2,1,0:T(8,128)(2,1)}), bf16[16,216,128]{2,1,0:T(8,128)(2,1)S(1)}, u32[]{:S(2)}, u32[]{:S(2)}) async-start(bf16[16,216,128]{2,1,0:T(8,128)(2,1)} %bitcast.14), calls=%async_computation | async-start | bytes 1769472 | tf_op jit(solution)/shard_map/all_to_all | solution.py:59
  35.4 0.7 collective-permute-start.8
  36.1 1.9 %collective-permute-start.7 = (bf16[2,128,128]{2,1,0:T(8,128)(2,1)S(1)}, bf16[2,128,128]{2,1,0:T(8,128)(2,1)S(1)}, u32[]{:S(2)}, u32[]{:S(2)}) collective-permute-start(bf16[2,128,128]{2,1,0:T(8,128)(2,1)S(1)} %get-tuple-element.50), channel_id=1, source_target_pairs={{0,1},{1,0},{2,3},{3,2},{4,5},{5,4},{6,7},{7,6},{8,9},{9,8},{10,11... | collective-permute-start | bytes 196616 | tf_op jit(solution)/shard_map/ppermute | solution.py:55
  38.0 0.0 collective-permute-done.8
  38.0 10.0 %collective-permute-done.7 = bf16[2,128,128]{2,1,0:T(8,128)(2,1)S(1)} collective-permute-done((bf16[2,128,128]{2,1,0:T(8,128)(2,1)S(1)}, bf16[2,128,128]{2,1,0:T(8,128)(2,1)S(1)}, u32[]{:S(2)}, u32[]{:S(2)}) %collective-permute-start.7) | collective-permute-done | bytes 65568 | tf_op jit(solution)/shard_map/ppermute | solution.py:55
  48.0 1.9 %all-to-all-done = bf16[16,216,128]{2,1,0:T(8,128)(2,1)S(1)} async-done(((bf16[16,216,128]{2,1,0:T(8,128)(2,1)}), bf16[16,216,128]{2,1,0:T(8,128)(2,1)S(1)}, u32[]{:S(2)}, u32[]{:S(2)}) %all-to-all-start) | async-done | bytes 884768 | tf_op jit(solution)/shard_map/all_to_all | solution.py:59
  49.9 0.1 reduce_sum.12
  50.1 0.1 collective-permute-start.9
  50.2 3.0 %collective-permute-done.9 = bf16[216,128]{1,0:T(8,128)(2,1)S(1)} collective-permute-done((bf16[216,128]{1,0:T(8,128)(2,1)S(1)}, bf16[216,128]{1,0:T(8,128)(2,1)S(1)}, u32[]{:S(2)}, u32[]{:S(2)}) %collective-permute-start.9) | collective-permute-done | bytes 55328 | tf_op jit(solution)/shard_map/ppermute | solution.py:55
  53.2 7.3 %collective-permute-start.12 = (bf16[216,128]{1,0:T(8,128)(2,1)S(1)}, bf16[216,128]{1,0:T(8,128)(2,1)S(1)}, u32[]{:S(2)}, u32[]{:S(2)}) collective-permute-start(bf16[216,128]{1,0:T(8,128)(2,1)S(1)} %add_convert_fusion), channel_id=1, source_target_pairs={{0,32},{1,33},{2,34},{3,35},{4,36},{5,37},{6,38},{7,39},{8,40},{9,... | collective-permute-start | bytes 165896 | tf_op jit(solution)/shard_map/ppermute | solution.py:55
  60.5 0.5 collective-permute-start.11
  61.0 0.0 collective-permute-start.10
  61.0 4.3 %collective-permute-start.14 = (bf16[2,4,128,128]{3,2,1,0:T(8,128)(2,1)S(1)}, bf16[2,4,128,128]{3,2,1,0:T(8,128)(2,1)S(1)}, u32[]{:S(2)}, u32[]{:S(2)}) collective-permute-start(bf16[2,4,128,128]{3,2,1,0:T(8,128)(2,1)S(1)} %pad_maximum_fusion.2.own_ref), channel_id=1, source_target_pairs={{0,1},{1,0},{2,3},{3,2},{4,5},{5,4},{6,7},{7,6},{8,9},{9,8},{10,11... | collective-permute-start | bytes 786440 | tf_op jit(solution)/shard_map/ppermute | solution.py:55
  65.3 0.7 collective-permute-start.13
  66.0 0.0 collective-permute-done.12
  66.0 0.9 collective-permute-done.11
  66.9 0.0 collective-permute-done.10
  66.9 3.9 %collective-permute-done.14.far_ref = bf16[2,4,128,128]{3,2,1,0:T(8,128)(2,1)S(1)} collective-permute-done((bf16[2,4,128,128]{3,2,1,0:T(8,128)(2,1)S(1)}, bf16[2,4,128,128]{3,2,1,0:T(8,128)(2,1)S(1)}, u32[]{:S(2)}, u32[]{:S(2)}) %collective-permute-start.14) | collective-permute-done | bytes 262176 | tf_op jit(solution)/shard_map/ppermute | solution.py:55
  70.8 0.0 collective-permute-done.13.near_ref
  70.8 1.0 %broadcast_in_dim.29 = bf16[16,216,128]{2,1,0:T(8,128)(2,1)} broadcast(bf16[216,128]{1,0:T(8,128)(2,1)S(1)} %multiply_convert_fusion.1), dimensions={1,2} | broadcast | bytes 940032 | tf_op jit(solution)/shard_map/broadcast_in_dim | solution.py:361
  71.8 3.6 %all-to-all-start.1 = ((bf16[16,216,128]{2,1,0:T(8,128)(2,1)}), bf16[16,216,128]{2,1,0:T(8,128)(2,1)S(1)}, u32[]{:S(2)}, u32[]{:S(2)}) async-start(bf16[16,216,128]{2,1,0:T(8,128)(2,1)} %broadcast_in_dim.29), calls=%async_computation.1 | async-start | bytes 1769472 | tf_op jit(solution)/shard_map/all_to_all | solution.py:59
  75.5 2.3 %shard_map.80 = bf16[2,2,128,128]{3,2,1,0:T(8,128)(2,1)} custom-call(s32[3]{0:T(128)S(1)} %pad_add_fusion.place_ref.refs_0_, bf16[2,4,128,128]{3,2,1,0:T(8,128)(2,1)S(1)} %collective-permute-done.13.near_ref, bf16[2,4,128,128]{3,2,1,0:T(8,128)(2,1)S(1)} %collective-permute-done.14.far_ref, bf16[2,4,128,128]{3,2,1,0:T(8,128)(2,1)S(1)} %pad_maximum_fusion.2.own_ref, ...), custom_call_target="tpu_custom_call" | custom-call | flops 452984832 | bytes 1048576 | tf_op jit(solution)/shard_map/pallas_call | solution.py:68
  77.8 11.5 %all-to-all-done.1 = bf16[16,216,128]{2,1,0:T(8,128)(2,1)S(1)} async-done(((bf16[16,216,128]{2,1,0:T(8,128)(2,1)}), bf16[16,216,128]{2,1,0:T(8,128)(2,1)S(1)}, u32[]{:S(2)}, u32[]{:S(2)}) %all-to-all-start.1) | async-done | bytes 884768 | tf_op jit(solution)/shard_map/all_to_all | solution.py:59
  89.3 2.6 %collective-permute-start.15 = (bf16[3456,128]{1,0:T(8,128)(2,1)S(1)}, bf16[3456,128]{1,0:T(8,128)(2,1)S(1)}, u32[]{:S(2)}, u32[]{:S(2)}) collective-permute-start(bf16[3456,128]{1,0:T(8,128)(2,1)S(1)} %bitcast.35), channel_id=1, source_target_pairs={{0,64},{1,65},{2,66},{3,67},{4,68},{5,69},{6,70},{7,71},{8,72},{9,... | collective-permute-start | bytes 2654216 | tf_op jit(solution)/shard_map/ppermute | solution.py:55
  92.0 1.9 %shard_map.81 = (f32[3456,128]{1,0:T(8,128)}, f32[3456,128]{1,0:T(8,128)}) custom-call(s32[3]{0:T(128)S(1)} %pad_add_fusion.place_ref.refs_0_, bf16[3456,128]{1,0:T(8,128)(2,1)S(1)} %bitcast.36), custom_call_target="tpu_custom_call" | custom-call | bytes 3145728 | tf_op jit(solution)/shard_map/pallas_call | solution.py:261
  93.9 0.1 collective-permute-done.15.refs_1_
  94.0 1.8 %shard_map.82 = (f32[3456,128]{1,0:T(8,128)}, f32[3456,128]{1,0:T(8,128)}) custom-call(s32[3]{0:T(128)S(1)} %pad_add_fusion.place_ref.refs_0_, bf16[3456,128]{1,0:T(8,128)(2,1)S(1)} %collective-permute-done.15.refs_1_, f32[3456,128]{1,0:T(8,128)} %get-tuple-element.39.refs_2_, ...), custom_call_target="tpu_custom_call", output_to_operand_aliasing={{0}: (2, {}), {1}: (3, {})} | custom-call | bytes 3145728 | tf_op jit(solution)/shard_map/pallas_call | solution.py:261
  (13 shorter events, 0.3 us)
Async XLA Ops:
  1.5 13.4 %copy-start = (bf16[3,3,3,128,128]{4,3,2,1,0:T(8,128)(2,1)S(1)}, bf16[3,3,3,128,128]{4,3,2,1,0:T(8,128)(2,1)}, u32[]{:S(2)}) copy-start(bf16[3,3,3,128,128]{4,3,2,1,0:T(8,128)(2,1)} %param.8) | copy-start | bytes 2654212
  1.5 13.4 %copy-start.1 = (bf16[3,3,3,128,128]{4,3,2,1,0:T(8,128)(2,1)S(1)}, bf16[3,3,3,128,128]{4,3,2,1,0:T(8,128)(2,1)}, u32[]{:S(2)}) copy-start(bf16[3,3,3,128,128]{4,3,2,1,0:T(8,128)(2,1)} %param.9) | copy-start | bytes 2654212
  2.7 16.7 %collective-permute-start = (bf16[2,2,2,128,128]{4,3,2,1,0:T(8,128)(2,1)S(1)}, bf16[2,2,2,128,128]{4,3,2,1,0:T(8,128)(2,1)S(1)}, u32[]{:S(2)}, u32[]{:S(2)}) collective-permute-start(bf16[2,2,2,128,128]{4,3,2,1,0:T(8,128)(2,1)S(1)} %multiply_convert_fusion.value_ref), channel_id=1, source_target_pairs={{0,64},{1,65},{2,66},{3,67},{4,68},{5,69},{6,70},{7,71},{8,72},{9,... | collective-permute-start | bytes 786440 | tf_op jit(solution)/shard_map/ppermute | solution.py:55
  6.0 2.7 %collective-permute-start.2 = (bf16[4,128,128]{2,1,0:T(8,128)(2,1)S(1)}, bf16[4,128,128]{2,1,0:T(8,128)(2,1)S(1)}, u32[]{:S(2)}, u32[]{:S(2)}) collective-permute-start(bf16[4,128,128]{2,1,0:T(8,128)(2,1)S(1)} %bitcast.46), channel_id=1, source_target_pairs={{0,64},{1,2},{2,1},{3,4},{4,3},{5,6},{6,5},{7,8},{8,7},{9,10},{10,... | collective-permute-start | bytes 393224 | tf_op jit(solution)/shard_map/ppermute | solution.py:55
  6.2 10.3 %collective-permute-start.4 = (bf16[2,2,128,128]{3,2,1,0:T(8,128)(2,1)S(1)}, bf16[2,2,128,128]{3,2,1,0:T(8,128)(2,1)S(1)}, u32[]{:S(2)}, u32[]{:S(2)}) collective-permute-start(bf16[2,2,128,128]{3,2,1,0:T(8,128)(2,1)S(1)} %fusion.4), channel_id=1, source_target_pairs={{0,1},{1,0},{2,3},{3,2},{4,5},{5,4},{6,7},{7,6},{8,9},{9,8},{10,11... | collective-permute-start | bytes 393224 | tf_op jit(solution)/shard_map/ppermute | solution.py:55
  6.5 6.3 %collective-permute-start.1 = (bf16[4,128,128]{2,1,0:T(8,128)(2,1)S(1)}, bf16[4,128,128]{2,1,0:T(8,128)(2,1)S(1)}, u32[]{:S(2)}, u32[]{:S(2)}) collective-permute-start(bf16[4,128,128]{2,1,0:T(8,128)(2,1)S(1)} %bitcast.45), channel_id=1, source_target_pairs={{0,1},{1,0},{2,3},{3,2},{4,5},{5,4},{6,7},{7,6},{8,9},{9,8},{10,11... | collective-permute-start | bytes 393224 | tf_op jit(solution)/shard_map/ppermute | solution.py:55
  12.9 6.5 %collective-permute-start.3 = (bf16[2,2,2,128,128]{4,3,2,1,0:T(8,128)(2,1)S(1)}, bf16[2,2,2,128,128]{4,3,2,1,0:T(8,128)(2,1)S(1)}, u32[]{:S(2)}, u32[]{:S(2)}) collective-permute-start(bf16[2,2,2,128,128]{4,3,2,1,0:T(8,128)(2,1)S(1)} %pad_maximum_fusion.margin_ref), channel_id=1, source_target_pairs={{0,64},{1,65},{2,66},{3,67},{4,68},{5,69},{6,70},{7,71},{8,72},{9,... | collective-permute-start | bytes 786440 | tf_op jit(solution)/shard_map/ppermute | solution.py:55
  14.7 4.7 %collective-permute-start.5 = (bf16[2,2,128,128]{3,2,1,0:T(8,128)(2,1)S(1)}, bf16[2,2,128,128]{3,2,1,0:T(8,128)(2,1)S(1)}, u32[]{:S(2)}, u32[]{:S(2)}) collective-permute-start(bf16[2,2,128,128]{3,2,1,0:T(8,128)(2,1)S(1)} %fusion.2), channel_id=1, source_target_pairs={{0,1},{1,0},{2,3},{3,2},{4,5},{5,4},{6,7},{7,6},{8,9},{9,8},{10,11... | collective-permute-start | bytes 393224 | tf_op jit(solution)/shard_map/ppermute | solution.py:55
  21.1 1.5 %collective-permute-start.6 = (bf16[2,2,128,128]{3,2,1,0:T(8,128)(2,1)S(1)}, bf16[2,2,128,128]{3,2,1,0:T(8,128)(2,1)S(1)}, u32[]{:S(2)}, u32[]{:S(2)}) collective-permute-start(bf16[2,2,128,128]{3,2,1,0:T(8,128)(2,1)S(1)} %get-tuple-element.26), channel_id=1, source_target_pairs={{0,64},{1,65},{2,66},{3,67},{4,68},{5,69},{6,70},{7,71},{8,72},{9,... | collective-permute-start | bytes 393224 | tf_op jit(solution)/shard_map/ppermute | solution.py:55
  25.5 24.5 %all-to-all-start = ((bf16[16,216,128]{2,1,0:T(8,128)(2,1)}), bf16[16,216,128]{2,1,0:T(8,128)(2,1)S(1)}, u32[]{:S(2)}, u32[]{:S(2)}) async-start(bf16[16,216,128]{2,1,0:T(8,128)(2,1)} %bitcast.14), calls=%async_computation | async-start | bytes 1769472 | tf_op jit(solution)/shard_map/all_to_all | solution.py:59
  35.4 2.6 %collective-permute-start.8 = (bf16[2,128,128]{2,1,0:T(8,128)(2,1)S(1)}, bf16[2,128,128]{2,1,0:T(8,128)(2,1)S(1)}, u32[]{:S(2)}, u32[]{:S(2)}) collective-permute-start(bf16[2,128,128]{2,1,0:T(8,128)(2,1)S(1)} %get-tuple-element.49), channel_id=1, source_target_pairs={{0,64},{1,2},{2,1},{3,4},{4,3},{5,6},{6,5},{7,8},{8,7},{9,10},{10,... | collective-permute-start | bytes 196616 | tf_op jit(solution)/shard_map/ppermute | solution.py:55
  36.1 11.9 %collective-permute-start.7 = (bf16[2,128,128]{2,1,0:T(8,128)(2,1)S(1)}, bf16[2,128,128]{2,1,0:T(8,128)(2,1)S(1)}, u32[]{:S(2)}, u32[]{:S(2)}) collective-permute-start(bf16[2,128,128]{2,1,0:T(8,128)(2,1)S(1)} %get-tuple-element.50), channel_id=1, source_target_pairs={{0,1},{1,0},{2,3},{3,2},{4,5},{5,4},{6,7},{7,6},{8,9},{9,8},{10,11... | collective-permute-start | bytes 196616 | tf_op jit(solution)/shard_map/ppermute | solution.py:55
  50.1 3.1 %collective-permute-start.9 = (bf16[216,128]{1,0:T(8,128)(2,1)S(1)}, bf16[216,128]{1,0:T(8,128)(2,1)S(1)}, u32[]{:S(2)}, u32[]{:S(2)}) collective-permute-start(bf16[216,128]{1,0:T(8,128)(2,1)S(1)} %reduce_sum.12), channel_id=1, source_target_pairs={{0,128},{1,129},{2,130},{3,131},{4,132},{5,133},{6,134},{7,135},{8... | collective-permute-start | bytes 165896 | tf_op jit(solution)/shard_map/ppermute | solution.py:55
  53.2 12.9 %collective-permute-start.12 = (bf16[216,128]{1,0:T(8,128)(2,1)S(1)}, bf16[216,128]{1,0:T(8,128)(2,1)S(1)}, u32[]{:S(2)}, u32[]{:S(2)}) collective-permute-start(bf16[216,128]{1,0:T(8,128)(2,1)S(1)} %add_convert_fusion), channel_id=1, source_target_pairs={{0,32},{1,33},{2,34},{3,35},{4,36},{5,37},{6,38},{7,39},{8,40},{9,... | collective-permute-start | bytes 165896 | tf_op jit(solution)/shard_map/ppermute | solution.py:55
  60.5 6.4 %collective-permute-start.11 = (bf16[216,128]{1,0:T(8,128)(2,1)S(1)}, bf16[216,128]{1,0:T(8,128)(2,1)S(1)}, u32[]{:S(2)}, u32[]{:S(2)}) collective-permute-start(bf16[216,128]{1,0:T(8,128)(2,1)S(1)} %add_convert_fusion), channel_id=1, source_target_pairs={{0,48},{1,49},{2,50},{3,51},{4,52},{5,53},{6,54},{7,55},{8,56},{9,... | collective-permute-start | bytes 165896 | tf_op jit(solution)/shard_map/ppermute | solution.py:55
  61.0 5.9 %collective-permute-start.10 = (bf16[216,128]{1,0:T(8,128)(2,1)S(1)}, bf16[216,128]{1,0:T(8,128)(2,1)S(1)}, u32[]{:S(2)}, u32[]{:S(2)}) collective-permute-start(bf16[216,128]{1,0:T(8,128)(2,1)S(1)} %add_convert_fusion), channel_id=1, source_target_pairs={{0,16},{1,17},{2,18},{3,19},{4,20},{5,21},{6,22},{7,23},{8,24},{9,... | collective-permute-start | bytes 165896 | tf_op jit(solution)/shard_map/ppermute | solution.py:55
  61.0 9.8 %collective-permute-start.14 = (bf16[2,4,128,128]{3,2,1,0:T(8,128)(2,1)S(1)}, bf16[2,4,128,128]{3,2,1,0:T(8,128)(2,1)S(1)}, u32[]{:S(2)}, u32[]{:S(2)}) collective-permute-start(bf16[2,4,128,128]{3,2,1,0:T(8,128)(2,1)S(1)} %pad_maximum_fusion.2.own_ref), channel_id=1, source_target_pairs={{0,1},{1,0},{2,3},{3,2},{4,5},{5,4},{6,7},{7,6},{8,9},{9,8},{10,11... | collective-permute-start | bytes 786440 | tf_op jit(solution)/shard_map/ppermute | solution.py:55
  65.3 5.5 %collective-permute-start.13 = (bf16[2,4,128,128]{3,2,1,0:T(8,128)(2,1)S(1)}, bf16[2,4,128,128]{3,2,1,0:T(8,128)(2,1)S(1)}, u32[]{:S(2)}, u32[]{:S(2)}) collective-permute-start(bf16[2,4,128,128]{3,2,1,0:T(8,128)(2,1)S(1)} %pad_maximum_fusion.2.own_ref), channel_id=1, source_target_pairs={{0,64},{1,65},{2,66},{3,67},{4,68},{5,69},{6,70},{7,71},{8,72},{9,... | collective-permute-start | bytes 786440 | tf_op jit(solution)/shard_map/ppermute | solution.py:55
  71.8 17.5 %all-to-all-start.1 = ((bf16[16,216,128]{2,1,0:T(8,128)(2,1)}), bf16[16,216,128]{2,1,0:T(8,128)(2,1)S(1)}, u32[]{:S(2)}, u32[]{:S(2)}) async-start(bf16[16,216,128]{2,1,0:T(8,128)(2,1)} %broadcast_in_dim.29), calls=%async_computation.1 | async-start | bytes 1769472 | tf_op jit(solution)/shard_map/all_to_all | solution.py:59
  89.3 4.7 %collective-permute-start.15 = (bf16[3456,128]{1,0:T(8,128)(2,1)S(1)}, bf16[3456,128]{1,0:T(8,128)(2,1)S(1)}, u32[]{:S(2)}, u32[]{:S(2)}) collective-permute-start(bf16[3456,128]{1,0:T(8,128)(2,1)S(1)} %bitcast.35), channel_id=1, source_target_pairs={{0,64},{1,65},{2,66},{3,67},{4,68},{5,69},{6,70},{7,71},{8,72},{9,... | collective-permute-start | bytes 2654216 | tf_op jit(solution)/shard_map/ppermute | solution.py:55

commit v3 on v2

--- a/solution.py
+++ b/solution.py
@@ -48,7 +48,7 @@
 
 
 SIBLING = flip_pairs(64)
-PLANE = [[base + n for n in range(16)] for base in range(0, COUNT, 16)]
+PLANE = [[base + (n + 10) % 16 for n in range(16)] for base in range(0, COUNT, 16)]
 
 
 def send(value, pairs):
@@ -352,13 +352,10 @@
     pre_banded = band(before, pre_grad, after)
     pre_near = send(pre_banded, tm_pairs(True))
     pre_far = send(pre_banded, tm_pairs(False))
-    total = total.astype(F32) + send(total, flip_pairs(128)).astype(F32)
+    other = send(total, flip_pairs(128))
+    total = total.astype(F32) + other.astype(F32)
     total = total.astype(BF)
-    others = [send(total, flip_pairs(16 * n)).astype(F32) for n in (1, 3, 2)]
-    factor = 1.0 / math.sqrt(8 * 128 * 128)
-    total = (((total.astype(F32) + others[0]) + (others[1] + others[2])) * factor).astype(BF)
-    total, pre_near, pre_far = lax.optimization_barrier((total, pre_near, pre_far))
-    mine = exchange(jnp.broadcast_to(total[None], (16, PART, C))).reshape(ROWS, C)
+    others = [send(total, flip_pairs(16 * n)) for n in (1, 3, 2)]
     (in_grad,) = call(
         in_grad_kernel,
         [(block, BF)],
@@ -367,7 +364,11 @@
         scratch=[pltpu.VMEM((4, 4, C, 3 * C), BF)],
         flops=2 * 27 * C * C * 512,
     )
-    mine, in_grad = lax.optimization_barrier((mine, in_grad))
+    others, in_grad = lax.optimization_barrier((others, in_grad))
+    total, *others = (part.astype(F32) for part in (total, *others))
+    factor = 1.0 / math.sqrt(8 * 128 * 128)
+    total = (((total + others[0]) + (others[1] + others[2])) * factor).astype(BF)
+    mine = exchange(jnp.broadcast_to(total[None], (16, PART, C))).reshape(ROWS, C)
     theirs = send(mine, SIBLING)
     totals = write(0, where, mine)
     one_total, two_total = write(1, where, theirs, totals)

time: 96.3 us -> 90.3 us (0.938)
  waiting for transfers between devices: 38.4 us -> 21.3 us
  blocking collectives: 0 us -> 16 us
  starting transfers between devices: 40.1 us -> 36.1 us
    all_to_all x0 -> x1, blocking collectives: none -> 16 us  [exchange(): lax.all_to_all(value, AXES, 0, 0, axis_index_groups=PLANE, tiled=True)]
    all_to_all x2 -> x1, waiting for transfers between devices: 13.4 us -> 0.01 us  [exchange(): lax.all_to_all(value, AXES, 0, 0, axis_index_groups=PLANE, tiled=True)]
    ppermute x16, waiting for transfers between devices: 25 us -> 21.3 us  [send(): return lax.ppermute(value, AXES, pairs)]
    ppermute x16, starting transfers between devices: 26.6 us -> 24.2 us  [send(): return lax.ppermute(value, AXES, pairs)]
    all_to_all x2 -> x1, starting transfers between devices: 13.5 us -> 11.9 us  [exchange(): lax.all_to_all(value, AXES, 0, 0, axis_index_groups=PLANE, tiled=True)]
  transfers between devices with their start and end apart: 18 -> 17, of which waited for: 10 -> 8; matrix products, arithmetic and copies ran while one was open for 0% -> 0% of each run, Pallas kernels for 7% -> 7%
where the time goes in v3:
time: 90.3 us; the launch traced here: 90 us
  starting transfers between devices  36.1 us (40%)
  waiting for transfers between devices  21.3 us (24%)
  blocking collectives  16 us (18%)
  Pallas kernels  13 us (14%)
  other arithmetic  2.35 us (3%)
  between operations  0.95 us (1%)
    ppermute x16, starting transfers between devices, send(): return lax.ppermute(value, AXES, pairs)  24.2 us
    ppermute x16, waiting for transfers between devices, send(): return lax.ppermute(value, AXES, pairs)  21.3 us
    all_to_all x1, blocking collectives, exchange(): lax.all_to_all(value, AXES, 0, 0, axis_index_groups=PLANE, tiled=True)  16 us
    all_to_all x1, starting transfers between devices, exchange(): lax.all_to_all(value, AXES, 0, 0, axis_index_groups=PLANE, tiled=True)  11.9 us
    pallas_call x5, Pallas kernels, call(): pl.pallas_call(kernel, out_shape=[jax.ShapeDtypeStruct(shape, kind) for s...  9.29 us
    pallas_call x2, Pallas kernels, write(): pl.pallas_call(lambda *refs: write_kernel(half, *refs), out_shape=[jax.Sh...  3.73 us
  transfers between devices with their start and end apart: 17, of which 8 were waited for; matrix products, arithmetic and copies ran while one was open for 0% of the time, Pallas kernels for 7%

profile of v3, /device:TPU:1, one launch (start us, length us, event | category | flops | bytes accessed | tf_op | source)
XLA Modules:
  0.0 90.0 jit_solution(11383094809300447763)
XLA Ops:
  0.6 0.7 exponential_bitcast_fusion
  1.3 0.1 broadcast_in_dim.24
  1.4 0.1 stack_reshape.9
  1.5 0.0 copy-start
  1.5 0.0 copy-start.1
  1.5 1.1 %pad_maximum_fusion.1 = bf16[2,2,2,128,128]{4,3,2,1,0:T(8,128)(2,1)S(1)} fusion(bf16[1,2,2,128,128]{4,3,2,1,0:T(8,128)(2,1)} %bitcast.47, bf16[1,2,2,128,128]{4,3,2,1,0:T(8,128)(2,1)} %bitcast.48), kind=kLoop, calls=%fused_computation.6 | loop fusion | flops 131072 | bytes 524288 | tf_op jit(solution)/shard_map/stack | solution.py:297
  2.6 0.1 multiply_convert_fusion.value_ref
  2.7 3.3 %collective-permute-start = (bf16[2,2,2,128,128]{4,3,2,1,0:T(8,128)(2,1)S(1)}, bf16[2,2,2,128,128]{4,3,2,1,0:T(8,128)(2,1)S(1)}, u32[]{:S(2)}, u32[]{:S(2)}) collective-permute-start(bf16[2,2,2,128,128]{4,3,2,1,0:T(8,128)(2,1)S(1)} %multiply_convert_fusion.value_ref), channel_id=1, source_target_pairs={{0,64},{1,65},{2,66},{3,67},{4,68},{5,69},{6,70},{7,71},{8,72},{9,... | collective-permute-start | bytes 786440 | tf_op jit(solution)/shard_map/ppermute | solution.py:55
  6.0 0.1 collective-permute-start.2
  6.2 0.3 collective-permute-start.4
  6.5 2.2 %collective-permute-start.1 = (bf16[4,128,128]{2,1,0:T(8,128)(2,1)S(1)}, bf16[4,128,128]{2,1,0:T(8,128)(2,1)S(1)}, u32[]{:S(2)}, u32[]{:S(2)}) collective-permute-start(bf16[4,128,128]{2,1,0:T(8,128)(2,1)S(1)} %bitcast.45), channel_id=1, source_target_pairs={{0,1},{1,0},{2,3},{3,2},{4,5},{5,4},{6,7},{7,6},{8,9},{9,8},{10,11... | collective-permute-start | bytes 393224 | tf_op jit(solution)/shard_map/ppermute | solution.py:55
  8.8 0.0 collective-permute-done.2
  8.8 4.0 %collective-permute-done.1 = bf16[4,128,128]{2,1,0:T(8,128)(2,1)S(1)} collective-permute-done((bf16[4,128,128]{2,1,0:T(8,128)(2,1)S(1)}, bf16[4,128,128]{2,1,0:T(8,128)(2,1)S(1)}, u32[]{:S(2)}, u32[]{:S(2)}) %collective-permute-start.1) | collective-permute-done | bytes 131104 | tf_op jit(solution)/shard_map/ppermute | solution.py:55
  12.9 1.8 %collective-permute-start.3 = (bf16[2,2,2,128,128]{4,3,2,1,0:T(8,128)(2,1)S(1)}, bf16[2,2,2,128,128]{4,3,2,1,0:T(8,128)(2,1)S(1)}, u32[]{:S(2)}, u32[]{:S(2)}) collective-permute-start(bf16[2,2,2,128,128]{4,3,2,1,0:T(8,128)(2,1)S(1)} %pad_maximum_fusion.margin_ref), channel_id=1, source_target_pairs={{0,64},{1,65},{2,66},{3,67},{4,68},{5,69},{6,70},{7,71},{8,72},{9,... | collective-permute-start | bytes 786440 | tf_op jit(solution)/shard_map/ppermute | solution.py:55
  14.7 0.1 collective-permute-start.5
  14.8 0.1 pad_add_fusion.place_ref.refs_0_
  14.9 0.0 copy-done
  14.9 0.0 copy-done.1
  14.9 1.6 %shard_map.76 = (bf16[2,3,128,256]{3,2,1,0:T(8,128)(2,1)S(1)}, f32[512,128]{1,0:T(8,128)S(1)}, f32[512,128]{1,0:T(8,128)S(1)}) custom-call(s32[3]{0:T(128)S(1)} %pad_add_fusion.place_ref.refs_0_, bf16[2,2,2,128,128]{4,3,2,1,0:T(8,128)(2,1)S(1)} %multiply_convert_fusion.value_ref, bf16[2,2,2,128,128]{4,3,2,1,0:T(8,128)(2,1)S(1)} %pad_maximum_fusion.margin_ref, ...), custom_call_target="tpu_custom_call" | custom-call | flops 452984832 | bytes 1048576 | tf_op jit(solution)/shard_map/pallas_call | solution.py:68
  16.5 0.0 collective-permute-done.4.far_own
  16.5 2.8 %collective-permute-done.5.far_margin = bf16[2,2,128,128]{3,2,1,0:T(8,128)(2,1)S(1)} collective-permute-done((bf16[2,2,128,128]{3,2,1,0:T(8,128)(2,1)S(1)}, bf16[2,2,128,128]{3,2,1,0:T(8,128)(2,1)S(1)}, u32[]{:S(2)}, u32[]{:S(2)}) %collective-permute-start.5) | collective-permute-done | bytes 131104 | tf_op jit(solution)/shard_map/ppermute | solution.py:55
  19.4 0.0 collective-permute-done.near_own
  19.4 0.0 collective-permute-done.3.near_margin
  19.4 1.7 %shard_map.77 = (bf16[2,2,128,128]{3,2,1,0:T(8,128)(2,1)S(1)}, bf16[2,2,128,128]{3,2,1,0:T(8,128)(2,1)S(1)}, bf16[2,2,128,128]{3,2,1,0:T(8,128)(2,1)S(1)}) custom-call(s32[3]{0:T(128)S(1)} %pad_add_fusion.place_ref.refs_0_, bf16[2,2,2,128,128]{4,3,2,1,0:T(8,128)(2,1)S(1)} %collective-permute-done.near_own, ...), custom_call_target="tpu_custom_call" | custom-call | flops 452984832 | bytes 1048576 | tf_op jit(solution)/shard_map/pallas_call | solution.py:68
  21.1 0.5 collective-permute-start.6
  21.6 0.7 shard_map.78
  22.3 0.2 collective-permute-done.6.got_ref
  22.6 2.9 %shard_map.79 = bf16[3456,128]{1,0:T(8,128)(2,1)} custom-call(s32[3]{0:T(128)S(1)} %pad_add_fusion.place_ref.refs_0_, bf16[2,2,128,128]{3,2,1,0:T(8,128)(2,1)S(1)} %get-tuple-element.24.stay_ref, bf16[2,2,128,128]{3,2,1,0:T(8,128)(2,1)S(1)} %collective-permute-done.6.got_ref, bf16[2,3,128,256]{3,2,1,0:T(8,128)(2,1)S(1)} %get-tuple-element.26.low_ref, ...), custom_call_target="tpu_custom_call" | custom-call | flops 905969664 | bytes 1048576 | tf_op jit(solution)/shard_map/pallas_call | solution.py:68
  25.5 11.9 %all-to-all-start = ((bf16[16,216,128]{2,1,0:T(8,128)(2,1)}), bf16[16,216,128]{2,1,0:T(8,128)(2,1)S(1)}, u32[]{:S(2)}, u32[]{:S(2)}) async-start(bf16[16,216,128]{2,1,0:T(8,128)(2,1)} %bitcast.14), calls=%async_computation | async-start | bytes 1769472 | tf_op jit(solution)/shard_map/all_to_all | solution.py:59
  37.4 1.0 %collective-permute-start.8 = (bf16[2,128,128]{2,1,0:T(8,128)(2,1)S(1)}, bf16[2,128,128]{2,1,0:T(8,128)(2,1)S(1)}, u32[]{:S(2)}, u32[]{:S(2)}) collective-permute-start(bf16[2,128,128]{2,1,0:T(8,128)(2,1)S(1)} %get-tuple-element.47), channel_id=1, source_target_pairs={{0,64},{1,2},{2,1},{3,4},{4,3},{5,6},{6,5},{7,8},{8,7},{9,10},{10,... | collective-permute-start | bytes 196616 | tf_op jit(solution)/shard_map/ppermute | solution.py:55
  38.4 0.0 collective-permute-start.7
  38.4 0.9 collective-permute-done.8
  39.3 9.0 %collective-permute-done.7 = bf16[2,128,128]{2,1,0:T(8,128)(2,1)S(1)} collective-permute-done((bf16[2,128,128]{2,1,0:T(8,128)(2,1)S(1)}, bf16[2,128,128]{2,1,0:T(8,128)(2,1)S(1)}, u32[]{:S(2)}, u32[]{:S(2)}) %collective-permute-start.7) | collective-permute-done | bytes 65568 | tf_op jit(solution)/shard_map/ppermute | solution.py:55
  48.3 0.0 all-to-all-done
  48.3 0.1 reduce_sum.12
  48.4 0.1 collective-permute-start.9
  48.6 3.2 %collective-permute-start.14 = (bf16[2,4,128,128]{3,2,1,0:T(8,128)(2,1)S(1)}, bf16[2,4,128,128]{3,2,1,0:T(8,128)(2,1)S(1)}, u32[]{:S(2)}, u32[]{:S(2)}) collective-permute-start(bf16[2,4,128,128]{3,2,1,0:T(8,128)(2,1)S(1)} %pad_maximum_fusion.2.own_ref), channel_id=1, source_target_pairs={{0,1},{1,0},{2,3},{3,2},{4,5},{5,4},{6,7},{7,6},{8,9},{9,8},{10,11... | collective-permute-start | bytes 786440 | tf_op jit(solution)/shard_map/ppermute | solution.py:55
  51.8 0.7 collective-permute-start.13
  52.4 0.0 collective-permute-done.9
  52.5 7.1 %collective-permute-start.12 = (bf16[216,128]{1,0:T(8,128)(2,1)S(1)}, bf16[216,128]{1,0:T(8,128)(2,1)S(1)}, u32[]{:S(2)}, u32[]{:S(2)}) collective-permute-start(bf16[216,128]{1,0:T(8,128)(2,1)S(1)} %add_convert_fusion), channel_id=1, source_target_pairs={{0,32},{1,33},{2,34},{3,35},{4,36},{5,37},{6,38},{7,39},{8,40},{9,... | collective-permute-start | bytes 165896 | tf_op jit(solution)/shard_map/ppermute | solution.py:55
  59.5 0.5 collective-permute-start.11
  60.0 0.1 collective-permute-start.10
  60.1 0.0 collective-permute-done.14.far_ref
  60.1 0.0 collective-permute-done.13.near_ref
  60.1 2.3 %shard_map.80 = bf16[2,2,128,128]{3,2,1,0:T(8,128)(2,1)} custom-call(s32[3]{0:T(128)S(1)} %pad_add_fusion.place_ref.refs_0_, bf16[2,4,128,128]{3,2,1,0:T(8,128)(2,1)S(1)} %collective-permute-done.13.near_ref, bf16[2,4,128,128]{3,2,1,0:T(8,128)(2,1)S(1)} %collective-permute-done.14.far_ref, bf16[2,4,128,128]{3,2,1,0:T(8,128)(2,1)S(1)} %pad_maximum_fusion.2.own_ref, ...), custom_call_target="tpu_custom_call" | custom-call | flops 452984832 | bytes 1048576 | tf_op jit(solution)/shard_map/pallas_call | solution.py:68
  62.4 3.2 %collective-permute-done.12 = bf16[216,128]{1,0:T(8,128)(2,1)S(1)} collective-permute-done((bf16[216,128]{1,0:T(8,128)(2,1)S(1)}, bf16[216,128]{1,0:T(8,128)(2,1)S(1)}, u32[]{:S(2)}, u32[]{:S(2)}) %collective-permute-start.12) | collective-permute-done | bytes 55328 | tf_op jit(solution)/shard_map/ppermute | solution.py:55
  65.6 1.0 %collective-permute-done.11 = bf16[216,128]{1,0:T(8,128)(2,1)S(1)} collective-permute-done((bf16[216,128]{1,0:T(8,128)(2,1)S(1)}, bf16[216,128]{1,0:T(8,128)(2,1)S(1)}, u32[]{:S(2)}, u32[]{:S(2)}) %collective-permute-start.11) | collective-permute-done | bytes 55328 | tf_op jit(solution)/shard_map/ppermute | solution.py:55
  66.6 0.0 collective-permute-done.10
  66.6 0.1 broadcast_in_dim.29
  66.7 16.0 %all_to_all.10 = bf16[16,216,128]{2,1,0:T(8,128)(2,1)S(1)} all-to-all(bf16[16,216,128]{2,1,0:T(8,128)(2,1)S(1)} %broadcast_in_dim.29), channel_id=1, replica_groups={{10,11,12,13,14,15,0,1,2,3,4,5,6,7,8,9},{26,27,28,29,30,31,16,17,18,19,..., dimensions={0} | all-to-all | bytes 1769472 | tf_op jit(solution)/shard_map/all_to_all | solution.py:59
  82.8 3.2 %collective-permute-start.15 = (bf16[3456,128]{1,0:T(8,128)(2,1)S(1)}, bf16[3456,128]{1,0:T(8,128)(2,1)S(1)}, u32[]{:S(2)}, u32[]{:S(2)}) collective-permute-start(bf16[3456,128]{1,0:T(8,128)(2,1)S(1)} %bitcast.35), channel_id=1, source_target_pairs={{0,64},{1,65},{2,66},{3,67},{4,68},{5,69},{6,70},{7,71},{8,72},{9,... | collective-permute-start | bytes 2654216 | tf_op jit(solution)/shard_map/ppermute | solution.py:55
  86.0 1.9 %shard_map.81 = (f32[3456,128]{1,0:T(8,128)}, f32[3456,128]{1,0:T(8,128)}) custom-call(s32[3]{0:T(128)S(1)} %pad_add_fusion.place_ref.refs_0_, bf16[3456,128]{1,0:T(8,128)(2,1)S(1)} %bitcast.36), custom_call_target="tpu_custom_call" | custom-call | bytes 3145728 | tf_op jit(solution)/shard_map/pallas_call | solution.py:261
  87.9 0.1 collective-permute-done.15.refs_1_
  88.0 1.8 %shard_map.82 = (f32[3456,128]{1,0:T(8,128)}, f32[3456,128]{1,0:T(8,128)}) custom-call(s32[3]{0:T(128)S(1)} %pad_add_fusion.place_ref.refs_0_, bf16[3456,128]{1,0:T(8,128)(2,1)S(1)} %collective-permute-done.15.refs_1_, f32[3456,128]{1,0:T(8,128)} %get-tuple-element.37.refs_2_, ...), custom_call_target="tpu_custom_call", output_to_operand_aliasing={{0}: (2, {}), {1}: (3, {})} | custom-call | bytes 3145728 | tf_op jit(solution)/shard_map/pallas_call | solution.py:261
  (13 shorter events, 0.3 us)
Async XLA Ops:
  1.5 13.4 %copy-start = (bf16[3,3,3,128,128]{4,3,2,1,0:T(8,128)(2,1)S(1)}, bf16[3,3,3,128,128]{4,3,2,1,0:T(8,128)(2,1)}, u32[]{:S(2)}) copy-start(bf16[3,3,3,128,128]{4,3,2,1,0:T(8,128)(2,1)} %param.8) | copy-start | bytes 2654212
  1.5 13.4 %copy-start.1 = (bf16[3,3,3,128,128]{4,3,2,1,0:T(8,128)(2,1)S(1)}, bf16[3,3,3,128,128]{4,3,2,1,0:T(8,128)(2,1)}, u32[]{:S(2)}) copy-start(bf16[3,3,3,128,128]{4,3,2,1,0:T(8,128)(2,1)} %param.9) | copy-start | bytes 2654212
  2.7 16.7 %collective-permute-start = (bf16[2,2,2,128,128]{4,3,2,1,0:T(8,128)(2,1)S(1)}, bf16[2,2,2,128,128]{4,3,2,1,0:T(8,128)(2,1)S(1)}, u32[]{:S(2)}, u32[]{:S(2)}) collective-permute-start(bf16[2,2,2,128,128]{4,3,2,1,0:T(8,128)(2,1)S(1)} %multiply_convert_fusion.value_ref), channel_id=1, source_target_pairs={{0,64},{1,65},{2,66},{3,67},{4,68},{5,69},{6,70},{7,71},{8,72},{9,... | collective-permute-start | bytes 786440 | tf_op jit(solution)/shard_map/ppermute | solution.py:55
  6.0 2.7 %collective-permute-start.2 = (bf16[4,128,128]{2,1,0:T(8,128)(2,1)S(1)}, bf16[4,128,128]{2,1,0:T(8,128)(2,1)S(1)}, u32[]{:S(2)}, u32[]{:S(2)}) collective-permute-start(bf16[4,128,128]{2,1,0:T(8,128)(2,1)S(1)} %bitcast.46), channel_id=1, source_target_pairs={{0,64},{1,2},{2,1},{3,4},{4,3},{5,6},{6,5},{7,8},{8,7},{9,10},{10,... | collective-permute-start | bytes 393224 | tf_op jit(solution)/shard_map/ppermute | solution.py:55
  6.2 10.3 %collective-permute-start.4 = (bf16[2,2,128,128]{3,2,1,0:T(8,128)(2,1)S(1)}, bf16[2,2,128,128]{3,2,1,0:T(8,128)(2,1)S(1)}, u32[]{:S(2)}, u32[]{:S(2)}) collective-permute-start(bf16[2,2,128,128]{3,2,1,0:T(8,128)(2,1)S(1)} %fusion.4), channel_id=1, source_target_pairs={{0,1},{1,0},{2,3},{3,2},{4,5},{5,4},{6,7},{7,6},{8,9},{9,8},{10,11... | collective-permute-start | bytes 393224 | tf_op jit(solution)/shard_map/ppermute | solution.py:55
  6.5 6.3 %collective-permute-start.1 = (bf16[4,128,128]{2,1,0:T(8,128)(2,1)S(1)}, bf16[4,128,128]{2,1,0:T(8,128)(2,1)S(1)}, u32[]{:S(2)}, u32[]{:S(2)}) collective-permute-start(bf16[4,128,128]{2,1,0:T(8,128)(2,1)S(1)} %bitcast.45), channel_id=1, source_target_pairs={{0,1},{1,0},{2,3},{3,2},{4,5},{5,4},{6,7},{7,6},{8,9},{9,8},{10,11... | collective-permute-start | bytes 393224 | tf_op jit(solution)/shard_map/ppermute | solution.py:55
  12.9 6.5 %collective-permute-start.3 = (bf16[2,2,2,128,128]{4,3,2,1,0:T(8,128)(2,1)S(1)}, bf16[2,2,2,128,128]{4,3,2,1,0:T(8,128)(2,1)S(1)}, u32[]{:S(2)}, u32[]{:S(2)}) collective-permute-start(bf16[2,2,2,128,128]{4,3,2,1,0:T(8,128)(2,1)S(1)} %pad_maximum_fusion.margin_ref), channel_id=1, source_target_pairs={{0,64},{1,65},{2,66},{3,67},{4,68},{5,69},{6,70},{7,71},{8,72},{9,... | collective-permute-start | bytes 786440 | tf_op jit(solution)/shard_map/ppermute | solution.py:55
  14.7 4.7 %collective-permute-start.5 = (bf16[2,2,128,128]{3,2,1,0:T(8,128)(2,1)S(1)}, bf16[2,2,128,128]{3,2,1,0:T(8,128)(2,1)S(1)}, u32[]{:S(2)}, u32[]{:S(2)}) collective-permute-start(bf16[2,2,128,128]{3,2,1,0:T(8,128)(2,1)S(1)} %fusion.2), channel_id=1, source_target_pairs={{0,1},{1,0},{2,3},{3,2},{4,5},{5,4},{6,7},{7,6},{8,9},{9,8},{10,11... | collective-permute-start | bytes 393224 | tf_op jit(solution)/shard_map/ppermute | solution.py:55
  21.1 1.5 %collective-permute-start.6 = (bf16[2,2,128,128]{3,2,1,0:T(8,128)(2,1)S(1)}, bf16[2,2,128,128]{3,2,1,0:T(8,128)(2,1)S(1)}, u32[]{:S(2)}, u32[]{:S(2)}) collective-permute-start(bf16[2,2,128,128]{3,2,1,0:T(8,128)(2,1)S(1)} %get-tuple-element.25), channel_id=1, source_target_pairs={{0,64},{1,65},{2,66},{3,67},{4,68},{5,69},{6,70},{7,71},{8,72},{9,... | collective-permute-start | bytes 393224 | tf_op jit(solution)/shard_map/ppermute | solution.py:55
  25.5 22.8 %all-to-all-start = ((bf16[16,216,128]{2,1,0:T(8,128)(2,1)}), bf16[16,216,128]{2,1,0:T(8,128)(2,1)S(1)}, u32[]{:S(2)}, u32[]{:S(2)}) async-start(bf16[16,216,128]{2,1,0:T(8,128)(2,1)} %bitcast.14), calls=%async_computation | async-start | bytes 1769472 | tf_op jit(solution)/shard_map/all_to_all | solution.py:59
  37.4 1.9 %collective-permute-start.8 = (bf16[2,128,128]{2,1,0:T(8,128)(2,1)S(1)}, bf16[2,128,128]{2,1,0:T(8,128)(2,1)S(1)}, u32[]{:S(2)}, u32[]{:S(2)}) collective-permute-start(bf16[2,128,128]{2,1,0:T(8,128)(2,1)S(1)} %get-tuple-element.47), channel_id=1, source_target_pairs={{0,64},{1,2},{2,1},{3,4},{4,3},{5,6},{6,5},{7,8},{8,7},{9,10},{10,... | collective-permute-start | bytes 196616 | tf_op jit(solution)/shard_map/ppermute | solution.py:55
  38.4 9.9 %collective-permute-start.7 = (bf16[2,128,128]{2,1,0:T(8,128)(2,1)S(1)}, bf16[2,128,128]{2,1,0:T(8,128)(2,1)S(1)}, u32[]{:S(2)}, u32[]{:S(2)}) collective-permute-start(bf16[2,128,128]{2,1,0:T(8,128)(2,1)S(1)} %get-tuple-element.48), channel_id=1, source_target_pairs={{0,1},{1,0},{2,3},{3,2},{4,5},{5,4},{6,7},{7,6},{8,9},{9,8},{10,11... | collective-permute-start | bytes 196616 | tf_op jit(solution)/shard_map/ppermute | solution.py:55
  48.4 4.0 %collective-permute-start.9 = (bf16[216,128]{1,0:T(8,128)(2,1)S(1)}, bf16[216,128]{1,0:T(8,128)(2,1)S(1)}, u32[]{:S(2)}, u32[]{:S(2)}) collective-permute-start(bf16[216,128]{1,0:T(8,128)(2,1)S(1)} %reduce_sum.12), channel_id=1, source_target_pairs={{0,128},{1,129},{2,130},{3,131},{4,132},{5,133},{6,134},{7,135},{8... | collective-permute-start | bytes 165896 | tf_op jit(solution)/shard_map/ppermute | solution.py:55
  48.6 11.5 %collective-permute-start.14 = (bf16[2,4,128,128]{3,2,1,0:T(8,128)(2,1)S(1)}, bf16[2,4,128,128]{3,2,1,0:T(8,128)(2,1)S(1)}, u32[]{:S(2)}, u32[]{:S(2)}) collective-permute-start(bf16[2,4,128,128]{3,2,1,0:T(8,128)(2,1)S(1)} %pad_maximum_fusion.2.own_ref), channel_id=1, source_target_pairs={{0,1},{1,0},{2,3},{3,2},{4,5},{5,4},{6,7},{7,6},{8,9},{9,8},{10,11... | collective-permute-start | bytes 786440 | tf_op jit(solution)/shard_map/ppermute | solution.py:55
  51.8 8.3 %collective-permute-start.13 = (bf16[2,4,128,128]{3,2,1,0:T(8,128)(2,1)S(1)}, bf16[2,4,128,128]{3,2,1,0:T(8,128)(2,1)S(1)}, u32[]{:S(2)}, u32[]{:S(2)}) collective-permute-start(bf16[2,4,128,128]{3,2,1,0:T(8,128)(2,1)S(1)} %pad_maximum_fusion.2.own_ref), channel_id=1, source_target_pairs={{0,64},{1,65},{2,66},{3,67},{4,68},{5,69},{6,70},{7,71},{8,72},{9,... | collective-permute-start | bytes 786440 | tf_op jit(solution)/shard_map/ppermute | solution.py:55
  52.5 13.1 %collective-permute-start.12 = (bf16[216,128]{1,0:T(8,128)(2,1)S(1)}, bf16[216,128]{1,0:T(8,128)(2,1)S(1)}, u32[]{:S(2)}, u32[]{:S(2)}) collective-permute-start(bf16[216,128]{1,0:T(8,128)(2,1)S(1)} %add_convert_fusion), channel_id=1, source_target_pairs={{0,32},{1,33},{2,34},{3,35},{4,36},{5,37},{6,38},{7,39},{8,40},{9,... | collective-permute-start | bytes 165896 | tf_op jit(solution)/shard_map/ppermute | solution.py:55
  59.5 7.0 %collective-permute-start.11 = (bf16[216,128]{1,0:T(8,128)(2,1)S(1)}, bf16[216,128]{1,0:T(8,128)(2,1)S(1)}, u32[]{:S(2)}, u32[]{:S(2)}) collective-permute-start(bf16[216,128]{1,0:T(8,128)(2,1)S(1)} %add_convert_fusion), channel_id=1, source_target_pairs={{0,48},{1,49},{2,50},{3,51},{4,52},{5,53},{6,54},{7,55},{8,56},{9,... | collective-permute-start | bytes 165896 | tf_op jit(solution)/shard_map/ppermute | solution.py:55
  60.0 6.6 %collective-permute-start.10 = (bf16[216,128]{1,0:T(8,128)(2,1)S(1)}, bf16[216,128]{1,0:T(8,128)(2,1)S(1)}, u32[]{:S(2)}, u32[]{:S(2)}) collective-permute-start(bf16[216,128]{1,0:T(8,128)(2,1)S(1)} %add_convert_fusion), channel_id=1, source_target_pairs={{0,16},{1,17},{2,18},{3,19},{4,20},{5,21},{6,22},{7,23},{8,24},{9,... | collective-permute-start | bytes 165896 | tf_op jit(solution)/shard_map/ppermute | solution.py:55
  82.8 5.3 %collective-permute-start.15 = (bf16[3456,128]{1,0:T(8,128)(2,1)S(1)}, bf16[3456,128]{1,0:T(8,128)(2,1)S(1)}, u32[]{:S(2)}, u32[]{:S(2)}) collective-permute-start(bf16[3456,128]{1,0:T(8,128)(2,1)S(1)} %bitcast.35), channel_id=1, source_target_pairs={{0,64},{1,65},{2,66},{3,67},{4,68},{5,69},{6,70},{7,71},{8,72},{9,... | collective-permute-start | bytes 2654216 | tf_op jit(solution)/shard_map/ppermute | solution.py:55

commit v4 on v3

--- a/solution.py
+++ b/solution.py
@@ -192,7 +192,7 @@
             fill_turned(high_ref, t, r, jnp.where(core == 0, first, far).astype(BF))
 
 
-def sums_kernel(place_ref, stay_ref, got_ref, low_ref, own_ref, high_ref, out_ref, slab):
+def sums_kernel(place_ref, stay_ref, got_ref, low_ref, own_ref, high_ref, out_hbm, slab, out_ref, sems):
     core = place_ref[0]
     for t in range(4):
         for r in range(2):
@@ -201,6 +201,7 @@
             for k, part in enumerate(columns(value)):
                 slab[t, r * C : (r + 1) * C, k * C : (k + 1) * C] = part
     frames = [ref.at[t] for ref in (low_ref, own_ref, high_ref) for t in range(2)]
+    copies = []
     for i in range(3):
         total = jnp.zeros((3 * C, 3 * C), F32)
         for t in range(4):
@@ -210,6 +211,11 @@
             for k in range(3):
                 n = i * 9 + j * 3 + k
                 out_ref[n * C : (n + 1) * C, :] = total[j * C : (j + 1) * C, k * C : (k + 1) * C]
+        rows = pl.ds(i * (ROWS // 3), ROWS // 3)
+        copies.append(pltpu.make_async_copy(out_ref.at[rows, :], out_hbm.at[rows, :], sems.at[i]))
+        copies[-1].start()
+    for copy in copies:
+        copy.wait()
 
 
 def in_grad_kernel(place_ref, near_ref, far_ref, own_ref, one_ref, out_ref, slab):
@@ -340,7 +346,12 @@
         [((ROWS, C), BF)],
         [where, stay, got, low, middle, high],
         specs=[SMEM] + [VMEM] * 5,
-        scratch=[pltpu.VMEM((4, 2 * C, 3 * C), BF)],
+        out_specs=[ANY],
+        scratch=[
+            pltpu.VMEM((4, 2 * C, 3 * C), BF),
+            pltpu.VMEM((ROWS, C), BF),
+            pltpu.SemaphoreType.DMA((3,)),
+        ],
         flops=2 * half,
         limit=16,
     )

time: 90.3 us -> 90.1 us (level)
  no operation moved by 1% of the time
where the time goes in v4:
time: 90.1 us; the launch traced here: 89.9 us
  starting transfers between devices  36.1 us (40%)
  waiting for transfers between devices  21.3 us (24%)
  blocking collectives  16 us (18%)
  Pallas kernels  12.8 us (14%)
  other arithmetic  2.35 us (3%)
  between operations  0.96 us (1%)
    ppermute x16, starting transfers between devices, send(): return lax.ppermute(value, AXES, pairs)  24.2 us
    ppermute x16, waiting for transfers between devices, send(): return lax.ppermute(value, AXES, pairs)  21.3 us
    all_to_all x1, blocking collectives, exchange(): lax.all_to_all(value, AXES, 0, 0, axis_index_groups=PLANE, tiled=True)  16 us
    all_to_all x1, starting transfers between devices, exchange(): lax.all_to_all(value, AXES, 0, 0, axis_index_groups=PLANE, tiled=True)  11.9 us
    pallas_call x5, Pallas kernels, call(): pl.pallas_call(kernel, out_shape=[jax.ShapeDtypeStruct(shape, kind) for s...  9.12 us
    pallas_call x2, Pallas kernels, write(): pl.pallas_call(lambda *refs: write_kernel(half, *refs), out_shape=[jax.Sh...  3.73 us
  transfers between devices with their start and end apart: 17, of which 8 were waited for; matrix products, arithmetic and copies ran while one was open for 0% of the time, Pallas kernels for 7%

profile of v4, /device:TPU:1, one launch (start us, length us, event | category | flops | bytes accessed | tf_op | source)
XLA Modules:
  0.0 89.9 jit_solution(9404652631911377392)
XLA Ops:
  0.6 0.7 exponential_bitcast_fusion
  1.3 0.1 broadcast_in_dim.24
  1.4 0.1 stack_reshape.9
  1.5 0.0 copy-start
  1.5 0.0 copy-start.1
  1.5 1.1 %pad_maximum_fusion.1 = bf16[2,2,2,128,128]{4,3,2,1,0:T(8,128)(2,1)S(1)} fusion(bf16[1,2,2,128,128]{4,3,2,1,0:T(8,128)(2,1)} %bitcast.47, bf16[1,2,2,128,128]{4,3,2,1,0:T(8,128)(2,1)} %bitcast.48), kind=kLoop, calls=%fused_computation.6 | loop fusion | flops 131072 | bytes 524288 | tf_op jit(solution)/shard_map/stack | solution.py:303
  2.6 0.1 multiply_convert_fusion.value_ref
  2.7 3.3 %collective-permute-start = (bf16[2,2,2,128,128]{4,3,2,1,0:T(8,128)(2,1)S(1)}, bf16[2,2,2,128,128]{4,3,2,1,0:T(8,128)(2,1)S(1)}, u32[]{:S(2)}, u32[]{:S(2)}) collective-permute-start(bf16[2,2,2,128,128]{4,3,2,1,0:T(8,128)(2,1)S(1)} %multiply_convert_fusion.value_ref), channel_id=1, source_target_pairs={{0,64},{1,65},{2,66},{3,67},{4,68},{5,69},{6,70},{7,71},{8,72},{9,... | collective-permute-start | bytes 786440 | tf_op jit(solution)/shard_map/ppermute | solution.py:55
  6.0 0.1 collective-permute-start.2
  6.2 0.3 collective-permute-start.4
  6.5 2.2 %collective-permute-start.1 = (bf16[4,128,128]{2,1,0:T(8,128)(2,1)S(1)}, bf16[4,128,128]{2,1,0:T(8,128)(2,1)S(1)}, u32[]{:S(2)}, u32[]{:S(2)}) collective-permute-start(bf16[4,128,128]{2,1,0:T(8,128)(2,1)S(1)} %bitcast.45), channel_id=1, source_target_pairs={{0,1},{1,0},{2,3},{3,2},{4,5},{5,4},{6,7},{7,6},{8,9},{9,8},{10,11... | collective-permute-start | bytes 393224 | tf_op jit(solution)/shard_map/ppermute | solution.py:55
  8.8 0.0 collective-permute-done.2
  8.8 4.0 %collective-permute-done.1 = bf16[4,128,128]{2,1,0:T(8,128)(2,1)S(1)} collective-permute-done((bf16[4,128,128]{2,1,0:T(8,128)(2,1)S(1)}, bf16[4,128,128]{2,1,0:T(8,128)(2,1)S(1)}, u32[]{:S(2)}, u32[]{:S(2)}) %collective-permute-start.1) | collective-permute-done | bytes 131104 | tf_op jit(solution)/shard_map/ppermute | solution.py:55
  12.9 1.8 %collective-permute-start.3 = (bf16[2,2,2,128,128]{4,3,2,1,0:T(8,128)(2,1)S(1)}, bf16[2,2,2,128,128]{4,3,2,1,0:T(8,128)(2,1)S(1)}, u32[]{:S(2)}, u32[]{:S(2)}) collective-permute-start(bf16[2,2,2,128,128]{4,3,2,1,0:T(8,128)(2,1)S(1)} %pad_maximum_fusion.margin_ref), channel_id=1, source_target_pairs={{0,64},{1,65},{2,66},{3,67},{4,68},{5,69},{6,70},{7,71},{8,72},{9,... | collective-permute-start | bytes 786440 | tf_op jit(solution)/shard_map/ppermute | solution.py:55
  14.7 0.1 collective-permute-start.5
  14.8 0.1 pad_add_fusion.place_ref.refs_0_
  14.9 0.0 copy-done
  14.9 0.0 copy-done.1
  14.9 1.6 %shard_map.76 = (bf16[2,3,128,256]{3,2,1,0:T(8,128)(2,1)S(1)}, f32[512,128]{1,0:T(8,128)S(1)}, f32[512,128]{1,0:T(8,128)S(1)}) custom-call(s32[3]{0:T(128)S(1)} %pad_add_fusion.place_ref.refs_0_, bf16[2,2,2,128,128]{4,3,2,1,0:T(8,128)(2,1)S(1)} %multiply_convert_fusion.value_ref, bf16[2,2,2,128,128]{4,3,2,1,0:T(8,128)(2,1)S(1)} %pad_maximum_fusion.margin_ref, ...), custom_call_target="tpu_custom_call" | custom-call | flops 452984832 | bytes 1048576 | tf_op jit(solution)/shard_map/pallas_call | solution.py:68
  16.5 0.0 collective-permute-done.4.far_own
  16.5 2.8 %collective-permute-done.5.far_margin = bf16[2,2,128,128]{3,2,1,0:T(8,128)(2,1)S(1)} collective-permute-done((bf16[2,2,128,128]{3,2,1,0:T(8,128)(2,1)S(1)}, bf16[2,2,128,128]{3,2,1,0:T(8,128)(2,1)S(1)}, u32[]{:S(2)}, u32[]{:S(2)}) %collective-permute-start.5) | collective-permute-done | bytes 131104 | tf_op jit(solution)/shard_map/ppermute | solution.py:55
  19.4 0.0 collective-permute-done.near_own
  19.4 0.0 collective-permute-done.3.near_margin
  19.4 1.7 %shard_map.77 = (bf16[2,2,128,128]{3,2,1,0:T(8,128)(2,1)S(1)}, bf16[2,2,128,128]{3,2,1,0:T(8,128)(2,1)S(1)}, bf16[2,2,128,128]{3,2,1,0:T(8,128)(2,1)S(1)}) custom-call(s32[3]{0:T(128)S(1)} %pad_add_fusion.place_ref.refs_0_, bf16[2,2,2,128,128]{4,3,2,1,0:T(8,128)(2,1)S(1)} %collective-permute-done.near_own, ...), custom_call_target="tpu_custom_call" | custom-call | flops 452984832 | bytes 1048576 | tf_op jit(solution)/shard_map/pallas_call | solution.py:68
  21.1 0.5 collective-permute-start.6
  21.6 0.7 shard_map.78
  22.3 0.2 collective-permute-done.6.got_ref
  22.6 2.7 %shard_map.79 = bf16[3456,128]{1,0:T(8,128)(2,1)} custom-call(s32[3]{0:T(128)S(1)} %pad_add_fusion.place_ref.refs_0_, bf16[2,2,128,128]{3,2,1,0:T(8,128)(2,1)S(1)} %get-tuple-element.24.stay_ref, bf16[2,2,128,128]{3,2,1,0:T(8,128)(2,1)S(1)} %collective-permute-done.6.got_ref, bf16[2,3,128,256]{3,2,1,0:T(8,128)(2,1)S(1)} %get-tuple-element.26.low_ref, ...), custom_call_target="tpu_custom_call" | custom-call | flops 905969664 | bytes 1048576 | tf_op jit(solution)/shard_map/pallas_call | solution.py:68
  25.3 11.9 %all-to-all-start = ((bf16[16,216,128]{2,1,0:T(8,128)(2,1)}), bf16[16,216,128]{2,1,0:T(8,128)(2,1)S(1)}, u32[]{:S(2)}, u32[]{:S(2)}) async-start(bf16[16,216,128]{2,1,0:T(8,128)(2,1)} %bitcast.14), calls=%async_computation | async-start | bytes 1769472 | tf_op jit(solution)/shard_map/all_to_all | solution.py:59
  37.2 1.0 %collective-permute-start.8 = (bf16[2,128,128]{2,1,0:T(8,128)(2,1)S(1)}, bf16[2,128,128]{2,1,0:T(8,128)(2,1)S(1)}, u32[]{:S(2)}, u32[]{:S(2)}) collective-permute-start(bf16[2,128,128]{2,1,0:T(8,128)(2,1)S(1)} %get-tuple-element.47), channel_id=1, source_target_pairs={{0,64},{1,2},{2,1},{3,4},{4,3},{5,6},{6,5},{7,8},{8,7},{9,10},{10,... | collective-permute-start | bytes 196616 | tf_op jit(solution)/shard_map/ppermute | solution.py:55
  38.2 0.0 collective-permute-start.7
  38.2 0.9 %collective-permute-done.8 = bf16[2,128,128]{2,1,0:T(8,128)(2,1)S(1)} collective-permute-done((bf16[2,128,128]{2,1,0:T(8,128)(2,1)S(1)}, bf16[2,128,128]{2,1,0:T(8,128)(2,1)S(1)}, u32[]{:S(2)}, u32[]{:S(2)}) %collective-permute-start.8) | collective-permute-done | bytes 65568 | tf_op jit(solution)/shard_map/ppermute | solution.py:55
  39.1 9.0 %collective-permute-done.7 = bf16[2,128,128]{2,1,0:T(8,128)(2,1)S(1)} collective-permute-done((bf16[2,128,128]{2,1,0:T(8,128)(2,1)S(1)}, bf16[2,128,128]{2,1,0:T(8,128)(2,1)S(1)}, u32[]{:S(2)}, u32[]{:S(2)}) %collective-permute-start.7) | collective-permute-done | bytes 65568 | tf_op jit(solution)/shard_map/ppermute | solution.py:55
  48.1 0.0 all-to-all-done
  48.1 0.1 reduce_sum.12
  48.3 0.1 collective-permute-start.9
  48.4 3.2 %collective-permute-start.14 = (bf16[2,4,128,128]{3,2,1,0:T(8,128)(2,1)S(1)}, bf16[2,4,128,128]{3,2,1,0:T(8,128)(2,1)S(1)}, u32[]{:S(2)}, u32[]{:S(2)}) collective-permute-start(bf16[2,4,128,128]{3,2,1,0:T(8,128)(2,1)S(1)} %pad_maximum_fusion.2.own_ref), channel_id=1, source_target_pairs={{0,1},{1,0},{2,3},{3,2},{4,5},{5,4},{6,7},{7,6},{8,9},{9,8},{10,11... | collective-permute-start | bytes 786440 | tf_op jit(solution)/shard_map/ppermute | solution.py:55
  51.6 0.7 collective-permute-start.13
  52.3 0.0 collective-permute-done.9
  52.3 7.1 %collective-permute-start.12 = (bf16[216,128]{1,0:T(8,128)(2,1)S(1)}, bf16[216,128]{1,0:T(8,128)(2,1)S(1)}, u32[]{:S(2)}, u32[]{:S(2)}) collective-permute-start(bf16[216,128]{1,0:T(8,128)(2,1)S(1)} %add_convert_fusion), channel_id=1, source_target_pairs={{0,32},{1,33},{2,34},{3,35},{4,36},{5,37},{6,38},{7,39},{8,40},{9,... | collective-permute-start | bytes 165896 | tf_op jit(solution)/shard_map/ppermute | solution.py:55
  59.4 0.5 collective-permute-start.11
  59.9 0.1 collective-permute-start.10
  60.0 0.0 collective-permute-done.14.far_ref
  60.0 0.0 collective-permute-done.13.near_ref
  60.0 2.3 %shard_map.80 = bf16[2,2,128,128]{3,2,1,0:T(8,128)(2,1)} custom-call(s32[3]{0:T(128)S(1)} %pad_add_fusion.place_ref.refs_0_, bf16[2,4,128,128]{3,2,1,0:T(8,128)(2,1)S(1)} %collective-permute-done.13.near_ref, bf16[2,4,128,128]{3,2,1,0:T(8,128)(2,1)S(1)} %collective-permute-done.14.far_ref, bf16[2,4,128,128]{3,2,1,0:T(8,128)(2,1)S(1)} %pad_maximum_fusion.2.own_ref, ...), custom_call_target="tpu_custom_call" | custom-call | flops 452984832 | bytes 1048576 | tf_op jit(solution)/shard_map/pallas_call | solution.py:68
  62.3 3.2 %collective-permute-done.12 = bf16[216,128]{1,0:T(8,128)(2,1)S(1)} collective-permute-done((bf16[216,128]{1,0:T(8,128)(2,1)S(1)}, bf16[216,128]{1,0:T(8,128)(2,1)S(1)}, u32[]{:S(2)}, u32[]{:S(2)}) %collective-permute-start.12) | collective-permute-done | bytes 55328 | tf_op jit(solution)/shard_map/ppermute | solution.py:55
  65.4 1.0 %collective-permute-done.11 = bf16[216,128]{1,0:T(8,128)(2,1)S(1)} collective-permute-done((bf16[216,128]{1,0:T(8,128)(2,1)S(1)}, bf16[216,128]{1,0:T(8,128)(2,1)S(1)}, u32[]{:S(2)}, u32[]{:S(2)}) %collective-permute-start.11) | collective-permute-done | bytes 55328 | tf_op jit(solution)/shard_map/ppermute | solution.py:55
  66.4 0.0 collective-permute-done.10
  66.5 0.1 broadcast_in_dim.29
  66.6 16.0 %all_to_all.10 = bf16[16,216,128]{2,1,0:T(8,128)(2,1)S(1)} all-to-all(bf16[16,216,128]{2,1,0:T(8,128)(2,1)S(1)} %broadcast_in_dim.29), channel_id=1, replica_groups={{10,11,12,13,14,15,0,1,2,3,4,5,6,7,8,9},{26,27,28,29,30,31,16,17,18,19,..., dimensions={0} | all-to-all | bytes 1769472 | tf_op jit(solution)/shard_map/all_to_all | solution.py:59
  82.6 3.2 %collective-permute-start.15 = (bf16[3456,128]{1,0:T(8,128)(2,1)S(1)}, bf16[3456,128]{1,0:T(8,128)(2,1)S(1)}, u32[]{:S(2)}, u32[]{:S(2)}) collective-permute-start(bf16[3456,128]{1,0:T(8,128)(2,1)S(1)} %bitcast.35), channel_id=1, source_target_pairs={{0,64},{1,65},{2,66},{3,67},{4,68},{5,69},{6,70},{7,71},{8,72},{9,... | collective-permute-start | bytes 2654216 | tf_op jit(solution)/shard_map/ppermute | solution.py:55
  85.8 1.9 %shard_map.81 = (f32[3456,128]{1,0:T(8,128)}, f32[3456,128]{1,0:T(8,128)}) custom-call(s32[3]{0:T(128)S(1)} %pad_add_fusion.place_ref.refs_0_, bf16[3456,128]{1,0:T(8,128)(2,1)S(1)} %bitcast.36), custom_call_target="tpu_custom_call" | custom-call | bytes 3145728 | tf_op jit(solution)/shard_map/pallas_call | solution.py:267
  87.8 0.1 collective-permute-done.15.refs_1_
  87.9 1.8 %shard_map.82 = (f32[3456,128]{1,0:T(8,128)}, f32[3456,128]{1,0:T(8,128)}) custom-call(s32[3]{0:T(128)S(1)} %pad_add_fusion.place_ref.refs_0_, bf16[3456,128]{1,0:T(8,128)(2,1)S(1)} %collective-permute-done.15.refs_1_, f32[3456,128]{1,0:T(8,128)} %get-tuple-element.37.refs_2_, ...), custom_call_target="tpu_custom_call", output_to_operand_aliasing={{0}: (2, {}), {1}: (3, {})} | custom-call | bytes 3145728 | tf_op jit(solution)/shard_map/pallas_call | solution.py:267
  (13 shorter events, 0.3 us)
Async XLA Ops:
  1.5 13.4 %copy-start = (bf16[3,3,3,128,128]{4,3,2,1,0:T(8,128)(2,1)S(1)}, bf16[3,3,3,128,128]{4,3,2,1,0:T(8,128)(2,1)}, u32[]{:S(2)}) copy-start(bf16[3,3,3,128,128]{4,3,2,1,0:T(8,128)(2,1)} %param.8) | copy-start | bytes 2654212
  1.5 13.4 %copy-start.1 = (bf16[3,3,3,128,128]{4,3,2,1,0:T(8,128)(2,1)S(1)}, bf16[3,3,3,128,128]{4,3,2,1,0:T(8,128)(2,1)}, u32[]{:S(2)}) copy-start(bf16[3,3,3,128,128]{4,3,2,1,0:T(8,128)(2,1)} %param.9) | copy-start | bytes 2654212
  2.7 16.7 %collective-permute-start = (bf16[2,2,2,128,128]{4,3,2,1,0:T(8,128)(2,1)S(1)}, bf16[2,2,2,128,128]{4,3,2,1,0:T(8,128)(2,1)S(1)}, u32[]{:S(2)}, u32[]{:S(2)}) collective-permute-start(bf16[2,2,2,128,128]{4,3,2,1,0:T(8,128)(2,1)S(1)} %multiply_convert_fusion.value_ref), channel_id=1, source_target_pairs={{0,64},{1,65},{2,66},{3,67},{4,68},{5,69},{6,70},{7,71},{8,72},{9,... | collective-permute-start | bytes 786440 | tf_op jit(solution)/shard_map/ppermute | solution.py:55
  6.0 2.7 %collective-permute-start.2 = (bf16[4,128,128]{2,1,0:T(8,128)(2,1)S(1)}, bf16[4,128,128]{2,1,0:T(8,128)(2,1)S(1)}, u32[]{:S(2)}, u32[]{:S(2)}) collective-permute-start(bf16[4,128,128]{2,1,0:T(8,128)(2,1)S(1)} %bitcast.46), channel_id=1, source_target_pairs={{0,64},{1,2},{2,1},{3,4},{4,3},{5,6},{6,5},{7,8},{8,7},{9,10},{10,... | collective-permute-start | bytes 393224 | tf_op jit(solution)/shard_map/ppermute | solution.py:55
  6.2 10.3 %collective-permute-start.4 = (bf16[2,2,128,128]{3,2,1,0:T(8,128)(2,1)S(1)}, bf16[2,2,128,128]{3,2,1,0:T(8,128)(2,1)S(1)}, u32[]{:S(2)}, u32[]{:S(2)}) collective-permute-start(bf16[2,2,128,128]{3,2,1,0:T(8,128)(2,1)S(1)} %fusion.4), channel_id=1, source_target_pairs={{0,1},{1,0},{2,3},{3,2},{4,5},{5,4},{6,7},{7,6},{8,9},{9,8},{10,11... | collective-permute-start | bytes 393224 | tf_op jit(solution)/shard_map/ppermute | solution.py:55
  6.5 6.3 %collective-permute-start.1 = (bf16[4,128,128]{2,1,0:T(8,128)(2,1)S(1)}, bf16[4,128,128]{2,1,0:T(8,128)(2,1)S(1)}, u32[]{:S(2)}, u32[]{:S(2)}) collective-permute-start(bf16[4,128,128]{2,1,0:T(8,128)(2,1)S(1)} %bitcast.45), channel_id=1, source_target_pairs={{0,1},{1,0},{2,3},{3,2},{4,5},{5,4},{6,7},{7,6},{8,9},{9,8},{10,11... | collective-permute-start | bytes 393224 | tf_op jit(solution)/shard_map/ppermute | solution.py:55
  12.9 6.5 %collective-permute-start.3 = (bf16[2,2,2,128,128]{4,3,2,1,0:T(8,128)(2,1)S(1)}, bf16[2,2,2,128,128]{4,3,2,1,0:T(8,128)(2,1)S(1)}, u32[]{:S(2)}, u32[]{:S(2)}) collective-permute-start(bf16[2,2,2,128,128]{4,3,2,1,0:T(8,128)(2,1)S(1)} %pad_maximum_fusion.margin_ref), channel_id=1, source_target_pairs={{0,64},{1,65},{2,66},{3,67},{4,68},{5,69},{6,70},{7,71},{8,72},{9,... | collective-permute-start | bytes 786440 | tf_op jit(solution)/shard_map/ppermute | solution.py:55
  14.7 4.7 %collective-permute-start.5 = (bf16[2,2,128,128]{3,2,1,0:T(8,128)(2,1)S(1)}, bf16[2,2,128,128]{3,2,1,0:T(8,128)(2,1)S(1)}, u32[]{:S(2)}, u32[]{:S(2)}) collective-permute-start(bf16[2,2,128,128]{3,2,1,0:T(8,128)(2,1)S(1)} %fusion.2), channel_id=1, source_target_pairs={{0,1},{1,0},{2,3},{3,2},{4,5},{5,4},{6,7},{7,6},{8,9},{9,8},{10,11... | collective-permute-start | bytes 393224 | tf_op jit(solution)/shard_map/ppermute | solution.py:55
  21.1 1.5 %collective-permute-start.6 = (bf16[2,2,128,128]{3,2,1,0:T(8,128)(2,1)S(1)}, bf16[2,2,128,128]{3,2,1,0:T(8,128)(2,1)S(1)}, u32[]{:S(2)}, u32[]{:S(2)}) collective-permute-start(bf16[2,2,128,128]{3,2,1,0:T(8,128)(2,1)S(1)} %get-tuple-element.25), channel_id=1, source_target_pairs={{0,64},{1,65},{2,66},{3,67},{4,68},{5,69},{6,70},{7,71},{8,72},{9,... | collective-permute-start | bytes 393224 | tf_op jit(solution)/shard_map/ppermute | solution.py:55
  25.3 22.8 %all-to-all-start = ((bf16[16,216,128]{2,1,0:T(8,128)(2,1)}), bf16[16,216,128]{2,1,0:T(8,128)(2,1)S(1)}, u32[]{:S(2)}, u32[]{:S(2)}) async-start(bf16[16,216,128]{2,1,0:T(8,128)(2,1)} %bitcast.14), calls=%async_computation | async-start | bytes 1769472 | tf_op jit(solution)/shard_map/all_to_all | solution.py:59
  37.2 1.9 %collective-permute-start.8 = (bf16[2,128,128]{2,1,0:T(8,128)(2,1)S(1)}, bf16[2,128,128]{2,1,0:T(8,128)(2,1)S(1)}, u32[]{:S(2)}, u32[]{:S(2)}) collective-permute-start(bf16[2,128,128]{2,1,0:T(8,128)(2,1)S(1)} %get-tuple-element.47), channel_id=1, source_target_pairs={{0,64},{1,2},{2,1},{3,4},{4,3},{5,6},{6,5},{7,8},{8,7},{9,10},{10,... | collective-permute-start | bytes 196616 | tf_op jit(solution)/shard_map/ppermute | solution.py:55
  38.2 9.9 %collective-permute-start.7 = (bf16[2,128,128]{2,1,0:T(8,128)(2,1)S(1)}, bf16[2,128,128]{2,1,0:T(8,128)(2,1)S(1)}, u32[]{:S(2)}, u32[]{:S(2)}) collective-permute-start(bf16[2,128,128]{2,1,0:T(8,128)(2,1)S(1)} %get-tuple-element.48), channel_id=1, source_target_pairs={{0,1},{1,0},{2,3},{3,2},{4,5},{5,4},{6,7},{7,6},{8,9},{9,8},{10,11... | collective-permute-start | bytes 196616 | tf_op jit(solution)/shard_map/ppermute | solution.py:55
  48.3 4.0 %collective-permute-start.9 = (bf16[216,128]{1,0:T(8,128)(2,1)S(1)}, bf16[216,128]{1,0:T(8,128)(2,1)S(1)}, u32[]{:S(2)}, u32[]{:S(2)}) collective-permute-start(bf16[216,128]{1,0:T(8,128)(2,1)S(1)} %reduce_sum.12), channel_id=1, source_target_pairs={{0,128},{1,129},{2,130},{3,131},{4,132},{5,133},{6,134},{7,135},{8... | collective-permute-start | bytes 165896 | tf_op jit(solution)/shard_map/ppermute | solution.py:55
  48.4 11.5 %collective-permute-start.14 = (bf16[2,4,128,128]{3,2,1,0:T(8,128)(2,1)S(1)}, bf16[2,4,128,128]{3,2,1,0:T(8,128)(2,1)S(1)}, u32[]{:S(2)}, u32[]{:S(2)}) collective-permute-start(bf16[2,4,128,128]{3,2,1,0:T(8,128)(2,1)S(1)} %pad_maximum_fusion.2.own_ref), channel_id=1, source_target_pairs={{0,1},{1,0},{2,3},{3,2},{4,5},{5,4},{6,7},{7,6},{8,9},{9,8},{10,11... | collective-permute-start | bytes 786440 | tf_op jit(solution)/shard_map/ppermute | solution.py:55
  51.6 8.3 %collective-permute-start.13 = (bf16[2,4,128,128]{3,2,1,0:T(8,128)(2,1)S(1)}, bf16[2,4,128,128]{3,2,1,0:T(8,128)(2,1)S(1)}, u32[]{:S(2)}, u32[]{:S(2)}) collective-permute-start(bf16[2,4,128,128]{3,2,1,0:T(8,128)(2,1)S(1)} %pad_maximum_fusion.2.own_ref), channel_id=1, source_target_pairs={{0,64},{1,65},{2,66},{3,67},{4,68},{5,69},{6,70},{7,71},{8,72},{9,... | collective-permute-start | bytes 786440 | tf_op jit(solution)/shard_map/ppermute | solution.py:55
  52.3 13.1 %collective-permute-start.12 = (bf16[216,128]{1,0:T(8,128)(2,1)S(1)}, bf16[216,128]{1,0:T(8,128)(2,1)S(1)}, u32[]{:S(2)}, u32[]{:S(2)}) collective-permute-start(bf16[216,128]{1,0:T(8,128)(2,1)S(1)} %add_convert_fusion), channel_id=1, source_target_pairs={{0,32},{1,33},{2,34},{3,35},{4,36},{5,37},{6,38},{7,39},{8,40},{9,... | collective-permute-start | bytes 165896 | tf_op jit(solution)/shard_map/ppermute | solution.py:55
  59.4 7.0 %collective-permute-start.11 = (bf16[216,128]{1,0:T(8,128)(2,1)S(1)}, bf16[216,128]{1,0:T(8,128)(2,1)S(1)}, u32[]{:S(2)}, u32[]{:S(2)}) collective-permute-start(bf16[216,128]{1,0:T(8,128)(2,1)S(1)} %add_convert_fusion), channel_id=1, source_target_pairs={{0,48},{1,49},{2,50},{3,51},{4,52},{5,53},{6,54},{7,55},{8,56},{9,... | collective-permute-start | bytes 165896 | tf_op jit(solution)/shard_map/ppermute | solution.py:55
  59.9 6.6 %collective-permute-start.10 = (bf16[216,128]{1,0:T(8,128)(2,1)S(1)}, bf16[216,128]{1,0:T(8,128)(2,1)S(1)}, u32[]{:S(2)}, u32[]{:S(2)}) collective-permute-start(bf16[216,128]{1,0:T(8,128)(2,1)S(1)} %add_convert_fusion), channel_id=1, source_target_pairs={{0,16},{1,17},{2,18},{3,19},{4,20},{5,21},{6,22},{7,23},{8,24},{9,... | collective-permute-start | bytes 165896 | tf_op jit(solution)/shard_map/ppermute | solution.py:55
  82.6 5.3 %collective-permute-start.15 = (bf16[3456,128]{1,0:T(8,128)(2,1)S(1)}, bf16[3456,128]{1,0:T(8,128)(2,1)S(1)}, u32[]{:S(2)}, u32[]{:S(2)}) collective-permute-start(bf16[3456,128]{1,0:T(8,128)(2,1)S(1)} %bitcast.35), channel_id=1, source_target_pairs={{0,64},{1,65},{2,66},{3,67},{4,68},{5,69},{6,70},{7,71},{8,72},{9,... | collective-permute-start | bytes 2654216 | tf_op jit(solution)/shard_map/ppermute | solution.py:55

commit v5 on v4

--- a/solution.py
+++ b/solution.py
@@ -218,10 +218,9 @@
         copy.wait()
 
 
-def in_grad_kernel(place_ref, near_ref, far_ref, own_ref, one_ref, out_ref, slab):
+def in_grad_kernel(place_ref, later_ref, own_ref, one_ref, out_ref, slab):
     def later(t, r):
-        value = jnp.where(place_ref[0] == 0, near_ref[t, r], far_ref[t, r])
-        return jnp.where(place_ref[1] < TM - 1, value, 0).astype(BF)
+        return jnp.where(place_ref[1] < TM - 1, later_ref[t, r], 0).astype(BF)
 
     for t in range(4):
         for r in range(4):
@@ -361,8 +360,7 @@
     total = jnp.sum(exchange(total.reshape(16, PART, C)).astype(F32), axis=0).astype(BF)
     total, before, after = lax.optimization_barrier((total, before, after))
     pre_banded = band(before, pre_grad, after)
-    pre_near = send(pre_banded, tm_pairs(True))
-    pre_far = send(pre_banded, tm_pairs(False))
+    pre_later = send(pre_banded, [(d, (d - HEIGHT) % COUNT) for d in range(COUNT)])
     other = send(total, flip_pairs(128))
     total = total.astype(F32) + other.astype(F32)
     total = total.astype(BF)
@@ -370,8 +368,8 @@
     (in_grad,) = call(
         in_grad_kernel,
         [(block, BF)],
-        [where, pre_near, pre_far, pre_banded, one],
-        specs=[SMEM] + [VMEM] * 4,
+        [where, pre_later, pre_banded, one],
+        specs=[SMEM] + [VMEM] * 3,
         scratch=[pltpu.VMEM((4, 4, C, 3 * C), BF)],
         flops=2 * 27 * C * C * 512,
     )

time: 90.1 us -> 89.2 us (0.990)
  starting transfers between devices: 36.1 us -> 34.7 us
    ppermute x16 -> x15, starting transfers between devices: 24.2 us -> 22.8 us  [send(): return lax.ppermute(value, AXES, pairs)]
    ppermute x16 -> x15, waiting for transfers between devices: 21.3 us -> 21.4 us  [send(): return lax.ppermute(value, AXES, pairs)]
  transfers between devices with their start and end apart: 17 -> 16, of which waited for: 8 -> 8; matrix products, arithmetic and copies ran while one was open for 0% -> 0% of each run, Pallas kernels for 7% -> 7%
where the time goes in v5:
time: 89.2 us; the launch traced here: 88.9 us
  starting transfers between devices  34.7 us (39%)
  waiting for transfers between devices  21.4 us (24%)
  blocking collectives  16.4 us (18%)
  Pallas kernels  12.8 us (14%)
  other arithmetic  2.35 us (3%)
  between operations  0.95 us (1%)
    ppermute x15, starting transfers between devices, send(): return lax.ppermute(value, AXES, pairs)  22.8 us
    ppermute x15, waiting for transfers between devices, send(): return lax.ppermute(value, AXES, pairs)  21.4 us
    all_to_all x1, blocking collectives, exchange(): lax.all_to_all(value, AXES, 0, 0, axis_index_groups=PLANE, tiled=True)  16.4 us
    all_to_all x1, starting transfers between devices, exchange(): lax.all_to_all(value, AXES, 0, 0, axis_index_groups=PLANE, tiled=True)  11.9 us
    pallas_call x5, Pallas kernels, call(): pl.pallas_call(kernel, out_shape=[jax.ShapeDtypeStruct(shape, kind) for s...  9.11 us
    pallas_call x2, Pallas kernels, write(): pl.pallas_call(lambda *refs: write_kernel(half, *refs), out_shape=[jax.Sh...  3.73 us
  transfers between devices with their start and end apart: 16, of which 8 were waited for; matrix products, arithmetic and copies ran while one was open for 0% of the time, Pallas kernels for 7%

profile of v5, /device:TPU:1, one launch (start us, length us, event | category | flops | bytes accessed | tf_op | source)
XLA Modules:
  0.0 88.9 jit_solution(4601428151195900166)
XLA Ops:
  0.6 0.7 exponential_bitcast_fusion
  1.3 0.1 broadcast_in_dim.24
  1.4 0.1 stack_reshape.9
  1.5 0.0 copy-start
  1.5 0.0 copy-start.1
  1.5 1.1 %pad_maximum_fusion.1 = bf16[2,2,2,128,128]{4,3,2,1,0:T(8,128)(2,1)S(1)} fusion(bf16[1,2,2,128,128]{4,3,2,1,0:T(8,128)(2,1)} %bitcast.47, bf16[1,2,2,128,128]{4,3,2,1,0:T(8,128)(2,1)} %bitcast.48), kind=kLoop, calls=%fused_computation.6 | loop fusion | flops 131072 | bytes 524288 | tf_op jit(solution)/shard_map/stack | solution.py:302
  2.6 0.1 multiply_convert_fusion.value_ref
  2.7 3.3 %collective-permute-start = (bf16[2,2,2,128,128]{4,3,2,1,0:T(8,128)(2,1)S(1)}, bf16[2,2,2,128,128]{4,3,2,1,0:T(8,128)(2,1)S(1)}, u32[]{:S(2)}, u32[]{:S(2)}) collective-permute-start(bf16[2,2,2,128,128]{4,3,2,1,0:T(8,128)(2,1)S(1)} %multiply_convert_fusion.value_ref), channel_id=1, source_target_pairs={{0,64},{1,65},{2,66},{3,67},{4,68},{5,69},{6,70},{7,71},{8,72},{9,... | collective-permute-start | bytes 786440 | tf_op jit(solution)/shard_map/ppermute | solution.py:55
  6.0 0.1 collective-permute-start.2
  6.2 0.3 collective-permute-start.4
  6.5 2.2 %collective-permute-start.1 = (bf16[4,128,128]{2,1,0:T(8,128)(2,1)S(1)}, bf16[4,128,128]{2,1,0:T(8,128)(2,1)S(1)}, u32[]{:S(2)}, u32[]{:S(2)}) collective-permute-start(bf16[4,128,128]{2,1,0:T(8,128)(2,1)S(1)} %bitcast.45), channel_id=1, source_target_pairs={{0,1},{1,0},{2,3},{3,2},{4,5},{5,4},{6,7},{7,6},{8,9},{9,8},{10,11... | collective-permute-start | bytes 393224 | tf_op jit(solution)/shard_map/ppermute | solution.py:55
  8.8 0.0 collective-permute-done.2
  8.8 4.0 %collective-permute-done.1 = bf16[4,128,128]{2,1,0:T(8,128)(2,1)S(1)} collective-permute-done((bf16[4,128,128]{2,1,0:T(8,128)(2,1)S(1)}, bf16[4,128,128]{2,1,0:T(8,128)(2,1)S(1)}, u32[]{:S(2)}, u32[]{:S(2)}) %collective-permute-start.1) | collective-permute-done | bytes 131104 | tf_op jit(solution)/shard_map/ppermute | solution.py:55
  12.9 1.8 %collective-permute-start.3 = (bf16[2,2,2,128,128]{4,3,2,1,0:T(8,128)(2,1)S(1)}, bf16[2,2,2,128,128]{4,3,2,1,0:T(8,128)(2,1)S(1)}, u32[]{:S(2)}, u32[]{:S(2)}) collective-permute-start(bf16[2,2,2,128,128]{4,3,2,1,0:T(8,128)(2,1)S(1)} %pad_maximum_fusion.margin_ref), channel_id=1, source_target_pairs={{0,64},{1,65},{2,66},{3,67},{4,68},{5,69},{6,70},{7,71},{8,72},{9,... | collective-permute-start | bytes 786440 | tf_op jit(solution)/shard_map/ppermute | solution.py:55
  14.7 0.1 collective-permute-start.5
  14.8 0.1 pad_add_fusion.place_ref.refs_0_
  14.9 0.0 copy-done
  14.9 0.0 copy-done.1
  14.9 1.6 %shard_map.76 = (bf16[2,3,128,256]{3,2,1,0:T(8,128)(2,1)S(1)}, f32[512,128]{1,0:T(8,128)S(1)}, f32[512,128]{1,0:T(8,128)S(1)}) custom-call(s32[3]{0:T(128)S(1)} %pad_add_fusion.place_ref.refs_0_, bf16[2,2,2,128,128]{4,3,2,1,0:T(8,128)(2,1)S(1)} %multiply_convert_fusion.value_ref, bf16[2,2,2,128,128]{4,3,2,1,0:T(8,128)(2,1)S(1)} %pad_maximum_fusion.margin_ref, ...), custom_call_target="tpu_custom_call" | custom-call | flops 452984832 | bytes 1048576 | tf_op jit(solution)/shard_map/pallas_call | solution.py:68
  16.5 0.0 collective-permute-done.4.far_own
  16.5 2.8 %collective-permute-done.5.far_margin = bf16[2,2,128,128]{3,2,1,0:T(8,128)(2,1)S(1)} collective-permute-done((bf16[2,2,128,128]{3,2,1,0:T(8,128)(2,1)S(1)}, bf16[2,2,128,128]{3,2,1,0:T(8,128)(2,1)S(1)}, u32[]{:S(2)}, u32[]{:S(2)}) %collective-permute-start.5) | collective-permute-done | bytes 131104 | tf_op jit(solution)/shard_map/ppermute | solution.py:55
  19.4 0.0 collective-permute-done.near_own
  19.4 0.0 collective-permute-done.3.near_margin
  19.4 1.7 %shard_map.77 = (bf16[2,2,128,128]{3,2,1,0:T(8,128)(2,1)S(1)}, bf16[2,2,128,128]{3,2,1,0:T(8,128)(2,1)S(1)}, bf16[2,2,128,128]{3,2,1,0:T(8,128)(2,1)S(1)}) custom-call(s32[3]{0:T(128)S(1)} %pad_add_fusion.place_ref.refs_0_, bf16[2,2,2,128,128]{4,3,2,1,0:T(8,128)(2,1)S(1)} %collective-permute-done.near_own, ...), custom_call_target="tpu_custom_call" | custom-call | flops 452984832 | bytes 1048576 | tf_op jit(solution)/shard_map/pallas_call | solution.py:68
  21.1 0.5 collective-permute-start.6
  21.6 0.7 shard_map.78
  22.3 0.2 collective-permute-done.6.got_ref
  22.6 2.7 %shard_map.79 = bf16[3456,128]{1,0:T(8,128)(2,1)} custom-call(s32[3]{0:T(128)S(1)} %pad_add_fusion.place_ref.refs_0_, bf16[2,2,128,128]{3,2,1,0:T(8,128)(2,1)S(1)} %get-tuple-element.24.stay_ref, bf16[2,2,128,128]{3,2,1,0:T(8,128)(2,1)S(1)} %collective-permute-done.6.got_ref, bf16[2,3,128,256]{3,2,1,0:T(8,128)(2,1)S(1)} %get-tuple-element.26.low_ref, ...), custom_call_target="tpu_custom_call" | custom-call | flops 905969664 | bytes 1048576 | tf_op jit(solution)/shard_map/pallas_call | solution.py:68
  25.3 11.9 %all-to-all-start = ((bf16[16,216,128]{2,1,0:T(8,128)(2,1)}), bf16[16,216,128]{2,1,0:T(8,128)(2,1)S(1)}, u32[]{:S(2)}, u32[]{:S(2)}) async-start(bf16[16,216,128]{2,1,0:T(8,128)(2,1)} %bitcast.14), calls=%async_computation | async-start | bytes 1769472 | tf_op jit(solution)/shard_map/all_to_all | solution.py:59
  37.2 1.0 %collective-permute-start.8 = (bf16[2,128,128]{2,1,0:T(8,128)(2,1)S(1)}, bf16[2,128,128]{2,1,0:T(8,128)(2,1)S(1)}, u32[]{:S(2)}, u32[]{:S(2)}) collective-permute-start(bf16[2,128,128]{2,1,0:T(8,128)(2,1)S(1)} %get-tuple-element.47), channel_id=1, source_target_pairs={{0,64},{1,2},{2,1},{3,4},{4,3},{5,6},{6,5},{7,8},{8,7},{9,10},{10,... | collective-permute-start | bytes 196616 | tf_op jit(solution)/shard_map/ppermute | solution.py:55
  38.2 0.0 collective-permute-start.7
  38.2 0.9 %collective-permute-done.8 = bf16[2,128,128]{2,1,0:T(8,128)(2,1)S(1)} collective-permute-done((bf16[2,128,128]{2,1,0:T(8,128)(2,1)S(1)}, bf16[2,128,128]{2,1,0:T(8,128)(2,1)S(1)}, u32[]{:S(2)}, u32[]{:S(2)}) %collective-permute-start.8) | collective-permute-done | bytes 65568 | tf_op jit(solution)/shard_map/ppermute | solution.py:55
  39.1 9.0 %collective-permute-done.7 = bf16[2,128,128]{2,1,0:T(8,128)(2,1)S(1)} collective-permute-done((bf16[2,128,128]{2,1,0:T(8,128)(2,1)S(1)}, bf16[2,128,128]{2,1,0:T(8,128)(2,1)S(1)}, u32[]{:S(2)}, u32[]{:S(2)}) %collective-permute-start.7) | collective-permute-done | bytes 65568 | tf_op jit(solution)/shard_map/ppermute | solution.py:55
  48.1 0.0 all-to-all-done
  48.1 0.1 reduce_sum.12
  48.3 0.1 collective-permute-start.9
  48.4 1.8 %collective-permute-start.13 = (bf16[2,4,128,128]{3,2,1,0:T(8,128)(2,1)S(1)}, bf16[2,4,128,128]{3,2,1,0:T(8,128)(2,1)S(1)}, u32[]{:S(2)}, u32[]{:S(2)}) collective-permute-start(bf16[2,4,128,128]{3,2,1,0:T(8,128)(2,1)S(1)} %pad_maximum_fusion.2.own_ref), channel_id=1, source_target_pairs={{0,192},{1,193},{2,194},{3,195},{4,196},{5,197},{6,198},{7,199},{8... | collective-permute-start | bytes 786440 | tf_op jit(solution)/shard_map/ppermute | solution.py:55
  50.2 1.2 %collective-permute-done.9 = bf16[216,128]{1,0:T(8,128)(2,1)S(1)} collective-permute-done((bf16[216,128]{1,0:T(8,128)(2,1)S(1)}, bf16[216,128]{1,0:T(8,128)(2,1)S(1)}, u32[]{:S(2)}, u32[]{:S(2)}) %collective-permute-start.9) | collective-permute-done | bytes 55328 | tf_op jit(solution)/shard_map/ppermute | solution.py:55
  51.4 7.3 %collective-permute-start.12 = (bf16[216,128]{1,0:T(8,128)(2,1)S(1)}, bf16[216,128]{1,0:T(8,128)(2,1)S(1)}, u32[]{:S(2)}, u32[]{:S(2)}) collective-permute-start(bf16[216,128]{1,0:T(8,128)(2,1)S(1)} %add_convert_fusion), channel_id=1, source_target_pairs={{0,32},{1,33},{2,34},{3,35},{4,36},{5,37},{6,38},{7,39},{8,40},{9,... | collective-permute-start | bytes 165896 | tf_op jit(solution)/shard_map/ppermute | solution.py:55
  58.7 0.8 collective-permute-start.11
  59.4 0.0 collective-permute-start.10
  59.4 0.0 collective-permute-done.13.later_ref
  59.4 2.3 %shard_map.80 = bf16[2,2,128,128]{3,2,1,0:T(8,128)(2,1)} custom-call(s32[3]{0:T(128)S(1)} %pad_add_fusion.place_ref.refs_0_, bf16[2,4,128,128]{3,2,1,0:T(8,128)(2,1)S(1)} %collective-permute-done.13.later_ref, bf16[2,4,128,128]{3,2,1,0:T(8,128)(2,1)S(1)} %pad_maximum_fusion.2.own_ref, bf16[27,128,128]{2,1,0:T(8,128)(2,1)S(1)} %bitcast.34), custom_call_target="tpu_custom_call" | custom-call | flops 452984832 | bytes 1048576 | tf_op jit(solution)/shard_map/pallas_call | solution.py:68
  61.7 0.0 collective-permute-done.12
  61.7 3.1 %collective-permute-done.11 = bf16[216,128]{1,0:T(8,128)(2,1)S(1)} collective-permute-done((bf16[216,128]{1,0:T(8,128)(2,1)S(1)}, bf16[216,128]{1,0:T(8,128)(2,1)S(1)}, u32[]{:S(2)}, u32[]{:S(2)}) %collective-permute-start.11) | collective-permute-done | bytes 55328 | tf_op jit(solution)/shard_map/ppermute | solution.py:55
  64.8 0.0 collective-permute-done.10
  64.9 0.1 broadcast_in_dim.29
  65.0 16.4 %all_to_all.10 = bf16[16,216,128]{2,1,0:T(8,128)(2,1)S(1)} all-to-all(bf16[16,216,128]{2,1,0:T(8,128)(2,1)S(1)} %broadcast_in_dim.29), channel_id=1, replica_groups={{10,11,12,13,14,15,0,1,2,3,4,5,6,7,8,9},{26,27,28,29,30,31,16,17,18,19,..., dimensions={0} | all-to-all | bytes 1769472 | tf_op jit(solution)/shard_map/all_to_all | solution.py:59
  81.4 3.5 %collective-permute-start.14 = (bf16[3456,128]{1,0:T(8,128)(2,1)S(1)}, bf16[3456,128]{1,0:T(8,128)(2,1)S(1)}, u32[]{:S(2)}, u32[]{:S(2)}) collective-permute-start(bf16[3456,128]{1,0:T(8,128)(2,1)S(1)} %bitcast.35), channel_id=1, source_target_pairs={{0,64},{1,65},{2,66},{3,67},{4,68},{5,69},{6,70},{7,71},{8,72},{9,... | collective-permute-start | bytes 2654216 | tf_op jit(solution)/shard_map/ppermute | solution.py:55
  84.9 1.9 %shard_map.81 = (f32[3456,128]{1,0:T(8,128)}, f32[3456,128]{1,0:T(8,128)}) custom-call(s32[3]{0:T(128)S(1)} %pad_add_fusion.place_ref.refs_0_, bf16[3456,128]{1,0:T(8,128)(2,1)S(1)} %bitcast.36), custom_call_target="tpu_custom_call" | custom-call | bytes 3145728 | tf_op jit(solution)/shard_map/pallas_call | solution.py:266
  86.8 0.1 collective-permute-done.14.refs_1_
  87.0 1.8 %shard_map.82 = (f32[3456,128]{1,0:T(8,128)}, f32[3456,128]{1,0:T(8,128)}) custom-call(s32[3]{0:T(128)S(1)} %pad_add_fusion.place_ref.refs_0_, bf16[3456,128]{1,0:T(8,128)(2,1)S(1)} %collective-permute-done.14.refs_1_, f32[3456,128]{1,0:T(8,128)} %get-tuple-element.37.refs_2_, ...), custom_call_target="tpu_custom_call", output_to_operand_aliasing={{0}: (2, {}), {1}: (3, {})} | custom-call | bytes 3145728 | tf_op jit(solution)/shard_map/pallas_call | solution.py:266
  (13 shorter events, 0.3 us)
Async XLA Ops:
  1.5 13.4 %copy-start = (bf16[3,3,3,128,128]{4,3,2,1,0:T(8,128)(2,1)S(1)}, bf16[3,3,3,128,128]{4,3,2,1,0:T(8,128)(2,1)}, u32[]{:S(2)}) copy-start(bf16[3,3,3,128,128]{4,3,2,1,0:T(8,128)(2,1)} %param.9) | copy-start | bytes 2654212
  1.5 13.4 %copy-start.1 = (bf16[3,3,3,128,128]{4,3,2,1,0:T(8,128)(2,1)S(1)}, bf16[3,3,3,128,128]{4,3,2,1,0:T(8,128)(2,1)}, u32[]{:S(2)}) copy-start(bf16[3,3,3,128,128]{4,3,2,1,0:T(8,128)(2,1)} %param.8) | copy-start | bytes 2654212
  2.7 16.7 %collective-permute-start = (bf16[2,2,2,128,128]{4,3,2,1,0:T(8,128)(2,1)S(1)}, bf16[2,2,2,128,128]{4,3,2,1,0:T(8,128)(2,1)S(1)}, u32[]{:S(2)}, u32[]{:S(2)}) collective-permute-start(bf16[2,2,2,128,128]{4,3,2,1,0:T(8,128)(2,1)S(1)} %multiply_convert_fusion.value_ref), channel_id=1, source_target_pairs={{0,64},{1,65},{2,66},{3,67},{4,68},{5,69},{6,70},{7,71},{8,72},{9,... | collective-permute-start | bytes 786440 | tf_op jit(solution)/shard_map/ppermute | solution.py:55
  6.0 2.7 %collective-permute-start.2 = (bf16[4,128,128]{2,1,0:T(8,128)(2,1)S(1)}, bf16[4,128,128]{2,1,0:T(8,128)(2,1)S(1)}, u32[]{:S(2)}, u32[]{:S(2)}) collective-permute-start(bf16[4,128,128]{2,1,0:T(8,128)(2,1)S(1)} %bitcast.46), channel_id=1, source_target_pairs={{0,64},{1,2},{2,1},{3,4},{4,3},{5,6},{6,5},{7,8},{8,7},{9,10},{10,... | collective-permute-start | bytes 393224 | tf_op jit(solution)/shard_map/ppermute | solution.py:55
  6.2 10.3 %collective-permute-start.4 = (bf16[2,2,128,128]{3,2,1,0:T(8,128)(2,1)S(1)}, bf16[2,2,128,128]{3,2,1,0:T(8,128)(2,1)S(1)}, u32[]{:S(2)}, u32[]{:S(2)}) collective-permute-start(bf16[2,2,128,128]{3,2,1,0:T(8,128)(2,1)S(1)} %fusion.4), channel_id=1, source_target_pairs={{0,1},{1,0},{2,3},{3,2},{4,5},{5,4},{6,7},{7,6},{8,9},{9,8},{10,11... | collective-permute-start | bytes 393224 | tf_op jit(solution)/shard_map/ppermute | solution.py:55
  6.5 6.3 %collective-permute-start.1 = (bf16[4,128,128]{2,1,0:T(8,128)(2,1)S(1)}, bf16[4,128,128]{2,1,0:T(8,128)(2,1)S(1)}, u32[]{:S(2)}, u32[]{:S(2)}) collective-permute-start(bf16[4,128,128]{2,1,0:T(8,128)(2,1)S(1)} %bitcast.45), channel_id=1, source_target_pairs={{0,1},{1,0},{2,3},{3,2},{4,5},{5,4},{6,7},{7,6},{8,9},{9,8},{10,11... | collective-permute-start | bytes 393224 | tf_op jit(solution)/shard_map/ppermute | solution.py:55
  12.9 6.5 %collective-permute-start.3 = (bf16[2,2,2,128,128]{4,3,2,1,0:T(8,128)(2,1)S(1)}, bf16[2,2,2,128,128]{4,3,2,1,0:T(8,128)(2,1)S(1)}, u32[]{:S(2)}, u32[]{:S(2)}) collective-permute-start(bf16[2,2,2,128,128]{4,3,2,1,0:T(8,128)(2,1)S(1)} %pad_maximum_fusion.margin_ref), channel_id=1, source_target_pairs={{0,64},{1,65},{2,66},{3,67},{4,68},{5,69},{6,70},{7,71},{8,72},{9,... | collective-permute-start | bytes 786440 | tf_op jit(solution)/shard_map/ppermute | solution.py:55
  14.7 4.7 %collective-permute-start.5 = (bf16[2,2,128,128]{3,2,1,0:T(8,128)(2,1)S(1)}, bf16[2,2,128,128]{3,2,1,0:T(8,128)(2,1)S(1)}, u32[]{:S(2)}, u32[]{:S(2)}) collective-permute-start(bf16[2,2,128,128]{3,2,1,0:T(8,128)(2,1)S(1)} %fusion.2), channel_id=1, source_target_pairs={{0,1},{1,0},{2,3},{3,2},{4,5},{5,4},{6,7},{7,6},{8,9},{9,8},{10,11... | collective-permute-start | bytes 393224 | tf_op jit(solution)/shard_map/ppermute | solution.py:55
  21.1 1.5 %collective-permute-start.6 = (bf16[2,2,128,128]{3,2,1,0:T(8,128)(2,1)S(1)}, bf16[2,2,128,128]{3,2,1,0:T(8,128)(2,1)S(1)}, u32[]{:S(2)}, u32[]{:S(2)}) collective-permute-start(bf16[2,2,128,128]{3,2,1,0:T(8,128)(2,1)S(1)} %get-tuple-element.25), channel_id=1, source_target_pairs={{0,64},{1,65},{2,66},{3,67},{4,68},{5,69},{6,70},{7,71},{8,72},{9,... | collective-permute-start | bytes 393224 | tf_op jit(solution)/shard_map/ppermute | solution.py:55
  25.3 22.8 %all-to-all-start = ((bf16[16,216,128]{2,1,0:T(8,128)(2,1)}), bf16[16,216,128]{2,1,0:T(8,128)(2,1)S(1)}, u32[]{:S(2)}, u32[]{:S(2)}) async-start(bf16[16,216,128]{2,1,0:T(8,128)(2,1)} %bitcast.14), calls=%async_computation | async-start | bytes 1769472 | tf_op jit(solution)/shard_map/all_to_all | solution.py:59
  37.2 1.9 %collective-permute-start.8 = (bf16[2,128,128]{2,1,0:T(8,128)(2,1)S(1)}, bf16[2,128,128]{2,1,0:T(8,128)(2,1)S(1)}, u32[]{:S(2)}, u32[]{:S(2)}) collective-permute-start(bf16[2,128,128]{2,1,0:T(8,128)(2,1)S(1)} %get-tuple-element.47), channel_id=1, source_target_pairs={{0,64},{1,2},{2,1},{3,4},{4,3},{5,6},{6,5},{7,8},{8,7},{9,10},{10,... | collective-permute-start | bytes 196616 | tf_op jit(solution)/shard_map/ppermute | solution.py:55
  38.2 9.9 %collective-permute-start.7 = (bf16[2,128,128]{2,1,0:T(8,128)(2,1)S(1)}, bf16[2,128,128]{2,1,0:T(8,128)(2,1)S(1)}, u32[]{:S(2)}, u32[]{:S(2)}) collective-permute-start(bf16[2,128,128]{2,1,0:T(8,128)(2,1)S(1)} %get-tuple-element.48), channel_id=1, source_target_pairs={{0,1},{1,0},{2,3},{3,2},{4,5},{5,4},{6,7},{7,6},{8,9},{9,8},{10,11... | collective-permute-start | bytes 196616 | tf_op jit(solution)/shard_map/ppermute | solution.py:55
  48.3 3.1 %collective-permute-start.9 = (bf16[216,128]{1,0:T(8,128)(2,1)S(1)}, bf16[216,128]{1,0:T(8,128)(2,1)S(1)}, u32[]{:S(2)}, u32[]{:S(2)}) collective-permute-start(bf16[216,128]{1,0:T(8,128)(2,1)S(1)} %reduce_sum.12), channel_id=1, source_target_pairs={{0,128},{1,129},{2,130},{3,131},{4,132},{5,133},{6,134},{7,135},{8... | collective-permute-start | bytes 165896 | tf_op jit(solution)/shard_map/ppermute | solution.py:55
  48.4 11.0 %collective-permute-start.13 = (bf16[2,4,128,128]{3,2,1,0:T(8,128)(2,1)S(1)}, bf16[2,4,128,128]{3,2,1,0:T(8,128)(2,1)S(1)}, u32[]{:S(2)}, u32[]{:S(2)}) collective-permute-start(bf16[2,4,128,128]{3,2,1,0:T(8,128)(2,1)S(1)} %pad_maximum_fusion.2.own_ref), channel_id=1, source_target_pairs={{0,192},{1,193},{2,194},{3,195},{4,196},{5,197},{6,198},{7,199},{8... | collective-permute-start | bytes 786440 | tf_op jit(solution)/shard_map/ppermute | solution.py:55
  51.4 10.3 %collective-permute-start.12 = (bf16[216,128]{1,0:T(8,128)(2,1)S(1)}, bf16[216,128]{1,0:T(8,128)(2,1)S(1)}, u32[]{:S(2)}, u32[]{:S(2)}) collective-permute-start(bf16[216,128]{1,0:T(8,128)(2,1)S(1)} %add_convert_fusion), channel_id=1, source_target_pairs={{0,32},{1,33},{2,34},{3,35},{4,36},{5,37},{6,38},{7,39},{8,40},{9,... | collective-permute-start | bytes 165896 | tf_op jit(solution)/shard_map/ppermute | solution.py:55
  58.7 6.2 %collective-permute-start.11 = (bf16[216,128]{1,0:T(8,128)(2,1)S(1)}, bf16[216,128]{1,0:T(8,128)(2,1)S(1)}, u32[]{:S(2)}, u32[]{:S(2)}) collective-permute-start(bf16[216,128]{1,0:T(8,128)(2,1)S(1)} %add_convert_fusion), channel_id=1, source_target_pairs={{0,48},{1,49},{2,50},{3,51},{4,52},{5,53},{6,54},{7,55},{8,56},{9,... | collective-permute-start | bytes 165896 | tf_op jit(solution)/shard_map/ppermute | solution.py:55
  59.4 5.4 %collective-permute-start.10 = (bf16[216,128]{1,0:T(8,128)(2,1)S(1)}, bf16[216,128]{1,0:T(8,128)(2,1)S(1)}, u32[]{:S(2)}, u32[]{:S(2)}) collective-permute-start(bf16[216,128]{1,0:T(8,128)(2,1)S(1)} %add_convert_fusion), channel_id=1, source_target_pairs={{0,16},{1,17},{2,18},{3,19},{4,20},{5,21},{6,22},{7,23},{8,24},{9,... | collective-permute-start | bytes 165896 | tf_op jit(solution)/shard_map/ppermute | solution.py:55
  81.4 5.6 %collective-permute-start.14 = (bf16[3456,128]{1,0:T(8,128)(2,1)S(1)}, bf16[3456,128]{1,0:T(8,128)(2,1)S(1)}, u32[]{:S(2)}, u32[]{:S(2)}) collective-permute-start(bf16[3456,128]{1,0:T(8,128)(2,1)S(1)} %bitcast.35), channel_id=1, source_target_pairs={{0,64},{1,65},{2,66},{3,67},{4,68},{5,69},{6,70},{7,71},{8,72},{9,... | collective-permute-start | bytes 2654216 | tf_op jit(solution)/shard_map/ppermute | solution.py:55

commit v6 on v5

--- a/solution.py
+++ b/solution.py
@@ -236,10 +236,10 @@
 
 def write_kernel(half, place_ref, part_ref, *refs):
     targets, whole, sems = refs[-4:-2], refs[-2], refs[-1]
-    third = ROWS // 3
+    ninth = ROWS // 9
 
     def copy(kind, i):
-        rows = pl.ds(i * third, third)
+        rows = pl.ds(i * ninth, ninth)
         return pltpu.make_async_copy(whole.at[rows, :], targets[kind].at[rows, :], sems.at[i])
 
     for kind in range(2):
@@ -257,8 +257,8 @@
                         else:
                             m = (i * 9 + j * 3 + 2 - k) * C
                         whole[m : m + C, :] = value.astype(F32)
-                copy(kind, 2 - i if kind else i).start()
-            for i in range(3):
+                    copy(kind, 8 - i * 3 - j if kind else i * 3 + j).start()
+            for i in range(9):
                 copy(kind, i).wait()
 
 
@@ -269,7 +269,7 @@
         in_specs=[SMEM, VMEM] + [ANY] * len(targets),
         out_specs=[ANY, ANY],
         input_output_aliases={2 + n: n for n in range(len(targets))},
-        scratch_shapes=[pltpu.VMEM((ROWS, C), F32), pltpu.SemaphoreType.DMA((3,))],
+        scratch_shapes=[pltpu.VMEM((ROWS, C), F32), pltpu.SemaphoreType.DMA((9,))],
         compiler_params=pltpu.CompilerParams(vmem_limit_bytes=8 << 20),
         cost_estimate=pl.CostEstimate(flops=0, bytes_accessed=3 << 20, transcendentals=0),
     )(where, part, *targets)

time: 89.2 us -> 89.2 us (level)
  no operation moved by 1% of the time
where the time goes in v6:
time: 89.2 us; the launch traced here: 88.9 us
  starting transfers between devices  34.7 us (39%)
  waiting for transfers between devices  21.4 us (24%)
  blocking collectives  16.4 us (18%)
  Pallas kernels  12.9 us (14%)
  other arithmetic  2.35 us (3%)
  between operations  0.95 us (1%)
    ppermute x15, starting transfers between devices, send(): return lax.ppermute(value, AXES, pairs)  22.8 us
    ppermute x15, waiting for transfers between devices, send(): return lax.ppermute(value, AXES, pairs)  21.4 us
    all_to_all x1, blocking collectives, exchange(): lax.all_to_all(value, AXES, 0, 0, axis_index_groups=PLANE, tiled=True)  16.4 us
    all_to_all x1, starting transfers between devices, exchange(): lax.all_to_all(value, AXES, 0, 0, axis_index_groups=PLANE, tiled=True)  11.9 us
    pallas_call x5, Pallas kernels, call(): pl.pallas_call(kernel, out_shape=[jax.ShapeDtypeStruct(shape, kind) for s...  9.11 us
    pallas_call x2, Pallas kernels, write(): pl.pallas_call(lambda *refs: write_kernel(half, *refs), out_shape=[jax.Sh...  3.75 us
  transfers between devices with their start and end apart: 16, of which 8 were waited for; matrix products, arithmetic and copies ran while one was open for 0% of the time, Pallas kernels for 7%

profile of v6, /device:TPU:1, one launch (start us, length us, event | category | flops | bytes accessed | tf_op | source)
XLA Modules:
  0.0 88.9 jit_solution(2900239788967337611)
XLA Ops:
  0.6 0.7 exponential_bitcast_fusion
  1.3 0.1 broadcast_in_dim.24
  1.4 0.1 stack_reshape.9
  1.5 0.0 copy-start
  1.5 0.0 copy-start.1
  1.5 1.1 %pad_maximum_fusion.1 = bf16[2,2,2,128,128]{4,3,2,1,0:T(8,128)(2,1)S(1)} fusion(bf16[1,2,2,128,128]{4,3,2,1,0:T(8,128)(2,1)} %bitcast.47, bf16[1,2,2,128,128]{4,3,2,1,0:T(8,128)(2,1)} %bitcast.48), kind=kLoop, calls=%fused_computation.6 | loop fusion | flops 131072 | bytes 524288 | tf_op jit(solution)/shard_map/stack | solution.py:302
  2.6 0.1 multiply_convert_fusion.value_ref
  2.7 3.3 %collective-permute-start = (bf16[2,2,2,128,128]{4,3,2,1,0:T(8,128)(2,1)S(1)}, bf16[2,2,2,128,128]{4,3,2,1,0:T(8,128)(2,1)S(1)}, u32[]{:S(2)}, u32[]{:S(2)}) collective-permute-start(bf16[2,2,2,128,128]{4,3,2,1,0:T(8,128)(2,1)S(1)} %multiply_convert_fusion.value_ref), channel_id=1, source_target_pairs={{0,64},{1,65},{2,66},{3,67},{4,68},{5,69},{6,70},{7,71},{8,72},{9,... | collective-permute-start | bytes 786440 | tf_op jit(solution)/shard_map/ppermute | solution.py:55
  6.0 0.1 collective-permute-start.2
  6.2 0.3 collective-permute-start.4
  6.5 2.2 %collective-permute-start.1 = (bf16[4,128,128]{2,1,0:T(8,128)(2,1)S(1)}, bf16[4,128,128]{2,1,0:T(8,128)(2,1)S(1)}, u32[]{:S(2)}, u32[]{:S(2)}) collective-permute-start(bf16[4,128,128]{2,1,0:T(8,128)(2,1)S(1)} %bitcast.45), channel_id=1, source_target_pairs={{0,1},{1,0},{2,3},{3,2},{4,5},{5,4},{6,7},{7,6},{8,9},{9,8},{10,11... | collective-permute-start | bytes 393224 | tf_op jit(solution)/shard_map/ppermute | solution.py:55
  8.8 0.0 collective-permute-done.2
  8.8 4.0 %collective-permute-done.1 = bf16[4,128,128]{2,1,0:T(8,128)(2,1)S(1)} collective-permute-done((bf16[4,128,128]{2,1,0:T(8,128)(2,1)S(1)}, bf16[4,128,128]{2,1,0:T(8,128)(2,1)S(1)}, u32[]{:S(2)}, u32[]{:S(2)}) %collective-permute-start.1) | collective-permute-done | bytes 131104 | tf_op jit(solution)/shard_map/ppermute | solution.py:55
  12.9 1.8 %collective-permute-start.3 = (bf16[2,2,2,128,128]{4,3,2,1,0:T(8,128)(2,1)S(1)}, bf16[2,2,2,128,128]{4,3,2,1,0:T(8,128)(2,1)S(1)}, u32[]{:S(2)}, u32[]{:S(2)}) collective-permute-start(bf16[2,2,2,128,128]{4,3,2,1,0:T(8,128)(2,1)S(1)} %pad_maximum_fusion.margin_ref), channel_id=1, source_target_pairs={{0,64},{1,65},{2,66},{3,67},{4,68},{5,69},{6,70},{7,71},{8,72},{9,... | collective-permute-start | bytes 786440 | tf_op jit(solution)/shard_map/ppermute | solution.py:55
  14.7 0.1 collective-permute-start.5
  14.8 0.1 pad_add_fusion.place_ref.refs_0_
  14.9 0.0 copy-done
  14.9 0.0 copy-done.1
  14.9 1.6 %shard_map.76 = (bf16[2,3,128,256]{3,2,1,0:T(8,128)(2,1)S(1)}, f32[512,128]{1,0:T(8,128)S(1)}, f32[512,128]{1,0:T(8,128)S(1)}) custom-call(s32[3]{0:T(128)S(1)} %pad_add_fusion.place_ref.refs_0_, bf16[2,2,2,128,128]{4,3,2,1,0:T(8,128)(2,1)S(1)} %multiply_convert_fusion.value_ref, bf16[2,2,2,128,128]{4,3,2,1,0:T(8,128)(2,1)S(1)} %pad_maximum_fusion.margin_ref, ...), custom_call_target="tpu_custom_call" | custom-call | flops 452984832 | bytes 1048576 | tf_op jit(solution)/shard_map/pallas_call | solution.py:68
  16.5 0.0 collective-permute-done.4.far_own
  16.5 2.8 %collective-permute-done.5.far_margin = bf16[2,2,128,128]{3,2,1,0:T(8,128)(2,1)S(1)} collective-permute-done((bf16[2,2,128,128]{3,2,1,0:T(8,128)(2,1)S(1)}, bf16[2,2,128,128]{3,2,1,0:T(8,128)(2,1)S(1)}, u32[]{:S(2)}, u32[]{:S(2)}) %collective-permute-start.5) | collective-permute-done | bytes 131104 | tf_op jit(solution)/shard_map/ppermute | solution.py:55
  19.4 0.0 collective-permute-done.near_own
  19.4 0.0 collective-permute-done.3.near_margin
  19.4 1.7 %shard_map.77 = (bf16[2,2,128,128]{3,2,1,0:T(8,128)(2,1)S(1)}, bf16[2,2,128,128]{3,2,1,0:T(8,128)(2,1)S(1)}, bf16[2,2,128,128]{3,2,1,0:T(8,128)(2,1)S(1)}) custom-call(s32[3]{0:T(128)S(1)} %pad_add_fusion.place_ref.refs_0_, bf16[2,2,2,128,128]{4,3,2,1,0:T(8,128)(2,1)S(1)} %collective-permute-done.near_own, ...), custom_call_target="tpu_custom_call" | custom-call | flops 452984832 | bytes 1048576 | tf_op jit(solution)/shard_map/pallas_call | solution.py:68
  21.1 0.5 collective-permute-start.6
  21.6 0.7 shard_map.78
  22.3 0.2 collective-permute-done.6.got_ref
  22.6 2.7 %shard_map.79 = bf16[3456,128]{1,0:T(8,128)(2,1)} custom-call(s32[3]{0:T(128)S(1)} %pad_add_fusion.place_ref.refs_0_, bf16[2,2,128,128]{3,2,1,0:T(8,128)(2,1)S(1)} %get-tuple-element.24.stay_ref, bf16[2,2,128,128]{3,2,1,0:T(8,128)(2,1)S(1)} %collective-permute-done.6.got_ref, bf16[2,3,128,256]{3,2,1,0:T(8,128)(2,1)S(1)} %get-tuple-element.26.low_ref, ...), custom_call_target="tpu_custom_call" | custom-call | flops 905969664 | bytes 1048576 | tf_op jit(solution)/shard_map/pallas_call | solution.py:68
  25.3 11.9 %all-to-all-start = ((bf16[16,216,128]{2,1,0:T(8,128)(2,1)}), bf16[16,216,128]{2,1,0:T(8,128)(2,1)S(1)}, u32[]{:S(2)}, u32[]{:S(2)}) async-start(bf16[16,216,128]{2,1,0:T(8,128)(2,1)} %bitcast.14), calls=%async_computation | async-start | bytes 1769472 | tf_op jit(solution)/shard_map/all_to_all | solution.py:59
  37.2 1.0 %collective-permute-start.8 = (bf16[2,128,128]{2,1,0:T(8,128)(2,1)S(1)}, bf16[2,128,128]{2,1,0:T(8,128)(2,1)S(1)}, u32[]{:S(2)}, u32[]{:S(2)}) collective-permute-start(bf16[2,128,128]{2,1,0:T(8,128)(2,1)S(1)} %get-tuple-element.47), channel_id=1, source_target_pairs={{0,64},{1,2},{2,1},{3,4},{4,3},{5,6},{6,5},{7,8},{8,7},{9,10},{10,... | collective-permute-start | bytes 196616 | tf_op jit(solution)/shard_map/ppermute | solution.py:55
  38.2 0.0 collective-permute-start.7
  38.2 0.9 %collective-permute-done.8 = bf16[2,128,128]{2,1,0:T(8,128)(2,1)S(1)} collective-permute-done((bf16[2,128,128]{2,1,0:T(8,128)(2,1)S(1)}, bf16[2,128,128]{2,1,0:T(8,128)(2,1)S(1)}, u32[]{:S(2)}, u32[]{:S(2)}) %collective-permute-start.8) | collective-permute-done | bytes 65568 | tf_op jit(solution)/shard_map/ppermute | solution.py:55
  39.1 9.0 %collective-permute-done.7 = bf16[2,128,128]{2,1,0:T(8,128)(2,1)S(1)} collective-permute-done((bf16[2,128,128]{2,1,0:T(8,128)(2,1)S(1)}, bf16[2,128,128]{2,1,0:T(8,128)(2,1)S(1)}, u32[]{:S(2)}, u32[]{:S(2)}) %collective-permute-start.7) | collective-permute-done | bytes 65568 | tf_op jit(solution)/shard_map/ppermute | solution.py:55
  48.1 0.0 all-to-all-done
  48.1 0.1 reduce_sum.12
  48.3 0.1 collective-permute-start.9
  48.4 1.8 %collective-permute-start.13 = (bf16[2,4,128,128]{3,2,1,0:T(8,128)(2,1)S(1)}, bf16[2,4,128,128]{3,2,1,0:T(8,128)(2,1)S(1)}, u32[]{:S(2)}, u32[]{:S(2)}) collective-permute-start(bf16[2,4,128,128]{3,2,1,0:T(8,128)(2,1)S(1)} %pad_maximum_fusion.2.own_ref), channel_id=1, source_target_pairs={{0,192},{1,193},{2,194},{3,195},{4,196},{5,197},{6,198},{7,199},{8... | collective-permute-start | bytes 786440 | tf_op jit(solution)/shard_map/ppermute | solution.py:55
  50.2 1.2 %collective-permute-done.9 = bf16[216,128]{1,0:T(8,128)(2,1)S(1)} collective-permute-done((bf16[216,128]{1,0:T(8,128)(2,1)S(1)}, bf16[216,128]{1,0:T(8,128)(2,1)S(1)}, u32[]{:S(2)}, u32[]{:S(2)}) %collective-permute-start.9) | collective-permute-done | bytes 55328 | tf_op jit(solution)/shard_map/ppermute | solution.py:55
  51.4 7.3 %collective-permute-start.12 = (bf16[216,128]{1,0:T(8,128)(2,1)S(1)}, bf16[216,128]{1,0:T(8,128)(2,1)S(1)}, u32[]{:S(2)}, u32[]{:S(2)}) collective-permute-start(bf16[216,128]{1,0:T(8,128)(2,1)S(1)} %add_convert_fusion), channel_id=1, source_target_pairs={{0,32},{1,33},{2,34},{3,35},{4,36},{5,37},{6,38},{7,39},{8,40},{9,... | collective-permute-start | bytes 165896 | tf_op jit(solution)/shard_map/ppermute | solution.py:55
  58.7 0.8 collective-permute-start.11
  59.4 0.0 collective-permute-start.10
  59.4 0.0 collective-permute-done.13.later_ref
  59.4 2.3 %shard_map.80 = bf16[2,2,128,128]{3,2,1,0:T(8,128)(2,1)} custom-call(s32[3]{0:T(128)S(1)} %pad_add_fusion.place_ref.refs_0_, bf16[2,4,128,128]{3,2,1,0:T(8,128)(2,1)S(1)} %collective-permute-done.13.later_ref, bf16[2,4,128,128]{3,2,1,0:T(8,128)(2,1)S(1)} %pad_maximum_fusion.2.own_ref, bf16[27,128,128]{2,1,0:T(8,128)(2,1)S(1)} %bitcast.34), custom_call_target="tpu_custom_call" | custom-call | flops 452984832 | bytes 1048576 | tf_op jit(solution)/shard_map/pallas_call | solution.py:68
  61.7 0.0 collective-permute-done.12
  61.7 3.1 %collective-permute-done.11 = bf16[216,128]{1,0:T(8,128)(2,1)S(1)} collective-permute-done((bf16[216,128]{1,0:T(8,128)(2,1)S(1)}, bf16[216,128]{1,0:T(8,128)(2,1)S(1)}, u32[]{:S(2)}, u32[]{:S(2)}) %collective-permute-start.11) | collective-permute-done | bytes 55328 | tf_op jit(solution)/shard_map/ppermute | solution.py:55
  64.8 0.0 collective-permute-done.10
  64.9 0.1 broadcast_in_dim.29
  65.0 16.4 %all_to_all.10 = bf16[16,216,128]{2,1,0:T(8,128)(2,1)S(1)} all-to-all(bf16[16,216,128]{2,1,0:T(8,128)(2,1)S(1)} %broadcast_in_dim.29), channel_id=1, replica_groups={{10,11,12,13,14,15,0,1,2,3,4,5,6,7,8,9},{26,27,28,29,30,31,16,17,18,19,..., dimensions={0} | all-to-all | bytes 1769472 | tf_op jit(solution)/shard_map/all_to_all | solution.py:59
  81.4 3.5 %collective-permute-start.14 = (bf16[3456,128]{1,0:T(8,128)(2,1)S(1)}, bf16[3456,128]{1,0:T(8,128)(2,1)S(1)}, u32[]{:S(2)}, u32[]{:S(2)}) collective-permute-start(bf16[3456,128]{1,0:T(8,128)(2,1)S(1)} %bitcast.35), channel_id=1, source_target_pairs={{0,64},{1,65},{2,66},{3,67},{4,68},{5,69},{6,70},{7,71},{8,72},{9,... | collective-permute-start | bytes 2654216 | tf_op jit(solution)/shard_map/ppermute | solution.py:55
  84.9 1.9 %shard_map.81 = (f32[3456,128]{1,0:T(8,128)}, f32[3456,128]{1,0:T(8,128)}) custom-call(s32[3]{0:T(128)S(1)} %pad_add_fusion.place_ref.refs_0_, bf16[3456,128]{1,0:T(8,128)(2,1)S(1)} %bitcast.36), custom_call_target="tpu_custom_call" | custom-call | bytes 3145728 | tf_op jit(solution)/shard_map/pallas_call | solution.py:266
  86.8 0.1 collective-permute-done.14.refs_1_
  87.0 1.8 %shard_map.82 = (f32[3456,128]{1,0:T(8,128)}, f32[3456,128]{1,0:T(8,128)}) custom-call(s32[3]{0:T(128)S(1)} %pad_add_fusion.place_ref.refs_0_, bf16[3456,128]{1,0:T(8,128)(2,1)S(1)} %collective-permute-done.14.refs_1_, f32[3456,128]{1,0:T(8,128)} %get-tuple-element.37.refs_2_, ...), custom_call_target="tpu_custom_call", output_to_operand_aliasing={{0}: (2, {}), {1}: (3, {})} | custom-call | bytes 3145728 | tf_op jit(solution)/shard_map/pallas_call | solution.py:266
  (13 shorter events, 0.3 us)
Async XLA Ops:
  1.5 13.4 %copy-start = (bf16[3,3,3,128,128]{4,3,2,1,0:T(8,128)(2,1)S(1)}, bf16[3,3,3,128,128]{4,3,2,1,0:T(8,128)(2,1)}, u32[]{:S(2)}) copy-start(bf16[3,3,3,128,128]{4,3,2,1,0:T(8,128)(2,1)} %param.9) | copy-start | bytes 2654212
  1.5 13.4 %copy-start.1 = (bf16[3,3,3,128,128]{4,3,2,1,0:T(8,128)(2,1)S(1)}, bf16[3,3,3,128,128]{4,3,2,1,0:T(8,128)(2,1)}, u32[]{:S(2)}) copy-start(bf16[3,3,3,128,128]{4,3,2,1,0:T(8,128)(2,1)} %param.8) | copy-start | bytes 2654212
  2.7 16.7 %collective-permute-start = (bf16[2,2,2,128,128]{4,3,2,1,0:T(8,128)(2,1)S(1)}, bf16[2,2,2,128,128]{4,3,2,1,0:T(8,128)(2,1)S(1)}, u32[]{:S(2)}, u32[]{:S(2)}) collective-permute-start(bf16[2,2,2,128,128]{4,3,2,1,0:T(8,128)(2,1)S(1)} %multiply_convert_fusion.value_ref), channel_id=1, source_target_pairs={{0,64},{1,65},{2,66},{3,67},{4,68},{5,69},{6,70},{7,71},{8,72},{9,... | collective-permute-start | bytes 786440 | tf_op jit(solution)/shard_map/ppermute | solution.py:55
  6.0 2.7 %collective-permute-start.2 = (bf16[4,128,128]{2,1,0:T(8,128)(2,1)S(1)}, bf16[4,128,128]{2,1,0:T(8,128)(2,1)S(1)}, u32[]{:S(2)}, u32[]{:S(2)}) collective-permute-start(bf16[4,128,128]{2,1,0:T(8,128)(2,1)S(1)} %bitcast.46), channel_id=1, source_target_pairs={{0,64},{1,2},{2,1},{3,4},{4,3},{5,6},{6,5},{7,8},{8,7},{9,10},{10,... | collective-permute-start | bytes 393224 | tf_op jit(solution)/shard_map/ppermute | solution.py:55
  6.2 10.3 %collective-permute-start.4 = (bf16[2,2,128,128]{3,2,1,0:T(8,128)(2,1)S(1)}, bf16[2,2,128,128]{3,2,1,0:T(8,128)(2,1)S(1)}, u32[]{:S(2)}, u32[]{:S(2)}) collective-permute-start(bf16[2,2,128,128]{3,2,1,0:T(8,128)(2,1)S(1)} %fusion.4), channel_id=1, source_target_pairs={{0,1},{1,0},{2,3},{3,2},{4,5},{5,4},{6,7},{7,6},{8,9},{9,8},{10,11... | collective-permute-start | bytes 393224 | tf_op jit(solution)/shard_map/ppermute | solution.py:55
  6.5 6.3 %collective-permute-start.1 = (bf16[4,128,128]{2,1,0:T(8,128)(2,1)S(1)}, bf16[4,128,128]{2,1,0:T(8,128)(2,1)S(1)}, u32[]{:S(2)}, u32[]{:S(2)}) collective-permute-start(bf16[4,128,128]{2,1,0:T(8,128)(2,1)S(1)} %bitcast.45), channel_id=1, source_target_pairs={{0,1},{1,0},{2,3},{3,2},{4,5},{5,4},{6,7},{7,6},{8,9},{9,8},{10,11... | collective-permute-start | bytes 393224 | tf_op jit(solution)/shard_map/ppermute | solution.py:55
  12.9 6.5 %collective-permute-start.3 = (bf16[2,2,2,128,128]{4,3,2,1,0:T(8,128)(2,1)S(1)}, bf16[2,2,2,128,128]{4,3,2,1,0:T(8,128)(2,1)S(1)}, u32[]{:S(2)}, u32[]{:S(2)}) collective-permute-start(bf16[2,2,2,128,128]{4,3,2,1,0:T(8,128)(2,1)S(1)} %pad_maximum_fusion.margin_ref), channel_id=1, source_target_pairs={{0,64},{1,65},{2,66},{3,67},{4,68},{5,69},{6,70},{7,71},{8,72},{9,... | collective-permute-start | bytes 786440 | tf_op jit(solution)/shard_map/ppermute | solution.py:55
  14.7 4.7 %collective-permute-start.5 = (bf16[2,2,128,128]{3,2,1,0:T(8,128)(2,1)S(1)}, bf16[2,2,128,128]{3,2,1,0:T(8,128)(2,1)S(1)}, u32[]{:S(2)}, u32[]{:S(2)}) collective-permute-start(bf16[2,2,128,128]{3,2,1,0:T(8,128)(2,1)S(1)} %fusion.2), channel_id=1, source_target_pairs={{0,1},{1,0},{2,3},{3,2},{4,5},{5,4},{6,7},{7,6},{8,9},{9,8},{10,11... | collective-permute-start | bytes 393224 | tf_op jit(solution)/shard_map/ppermute | solution.py:55
  21.1 1.5 %collective-permute-start.6 = (bf16[2,2,128,128]{3,2,1,0:T(8,128)(2,1)S(1)}, bf16[2,2,128,128]{3,2,1,0:T(8,128)(2,1)S(1)}, u32[]{:S(2)}, u32[]{:S(2)}) collective-permute-start(bf16[2,2,128,128]{3,2,1,0:T(8,128)(2,1)S(1)} %get-tuple-element.25), channel_id=1, source_target_pairs={{0,64},{1,65},{2,66},{3,67},{4,68},{5,69},{6,70},{7,71},{8,72},{9,... | collective-permute-start | bytes 393224 | tf_op jit(solution)/shard_map/ppermute | solution.py:55
  25.3 22.8 %all-to-all-start = ((bf16[16,216,128]{2,1,0:T(8,128)(2,1)}), bf16[16,216,128]{2,1,0:T(8,128)(2,1)S(1)}, u32[]{:S(2)}, u32[]{:S(2)}) async-start(bf16[16,216,128]{2,1,0:T(8,128)(2,1)} %bitcast.14), calls=%async_computation | async-start | bytes 1769472 | tf_op jit(solution)/shard_map/all_to_all | solution.py:59
  37.2 1.9 %collective-permute-start.8 = (bf16[2,128,128]{2,1,0:T(8,128)(2,1)S(1)}, bf16[2,128,128]{2,1,0:T(8,128)(2,1)S(1)}, u32[]{:S(2)}, u32[]{:S(2)}) collective-permute-start(bf16[2,128,128]{2,1,0:T(8,128)(2,1)S(1)} %get-tuple-element.47), channel_id=1, source_target_pairs={{0,64},{1,2},{2,1},{3,4},{4,3},{5,6},{6,5},{7,8},{8,7},{9,10},{10,... | collective-permute-start | bytes 196616 | tf_op jit(solution)/shard_map/ppermute | solution.py:55
  38.2 9.9 %collective-permute-start.7 = (bf16[2,128,128]{2,1,0:T(8,128)(2,1)S(1)}, bf16[2,128,128]{2,1,0:T(8,128)(2,1)S(1)}, u32[]{:S(2)}, u32[]{:S(2)}) collective-permute-start(bf16[2,128,128]{2,1,0:T(8,128)(2,1)S(1)} %get-tuple-element.48), channel_id=1, source_target_pairs={{0,1},{1,0},{2,3},{3,2},{4,5},{5,4},{6,7},{7,6},{8,9},{9,8},{10,11... | collective-permute-start | bytes 196616 | tf_op jit(solution)/shard_map/ppermute | solution.py:55
  48.3 3.1 %collective-permute-start.9 = (bf16[216,128]{1,0:T(8,128)(2,1)S(1)}, bf16[216,128]{1,0:T(8,128)(2,1)S(1)}, u32[]{:S(2)}, u32[]{:S(2)}) collective-permute-start(bf16[216,128]{1,0:T(8,128)(2,1)S(1)} %reduce_sum.12), channel_id=1, source_target_pairs={{0,128},{1,129},{2,130},{3,131},{4,132},{5,133},{6,134},{7,135},{8... | collective-permute-start | bytes 165896 | tf_op jit(solution)/shard_map/ppermute | solution.py:55
  48.4 11.0 %collective-permute-start.13 = (bf16[2,4,128,128]{3,2,1,0:T(8,128)(2,1)S(1)}, bf16[2,4,128,128]{3,2,1,0:T(8,128)(2,1)S(1)}, u32[]{:S(2)}, u32[]{:S(2)}) collective-permute-start(bf16[2,4,128,128]{3,2,1,0:T(8,128)(2,1)S(1)} %pad_maximum_fusion.2.own_ref), channel_id=1, source_target_pairs={{0,192},{1,193},{2,194},{3,195},{4,196},{5,197},{6,198},{7,199},{8... | collective-permute-start | bytes 786440 | tf_op jit(solution)/shard_map/ppermute | solution.py:55
  51.4 10.3 %collective-permute-start.12 = (bf16[216,128]{1,0:T(8,128)(2,1)S(1)}, bf16[216,128]{1,0:T(8,128)(2,1)S(1)}, u32[]{:S(2)}, u32[]{:S(2)}) collective-permute-start(bf16[216,128]{1,0:T(8,128)(2,1)S(1)} %add_convert_fusion), channel_id=1, source_target_pairs={{0,32},{1,33},{2,34},{3,35},{4,36},{5,37},{6,38},{7,39},{8,40},{9,... | collective-permute-start | bytes 165896 | tf_op jit(solution)/shard_map/ppermute | solution.py:55
  58.7 6.2 %collective-permute-start.11 = (bf16[216,128]{1,0:T(8,128)(2,1)S(1)}, bf16[216,128]{1,0:T(8,128)(2,1)S(1)}, u32[]{:S(2)}, u32[]{:S(2)}) collective-permute-start(bf16[216,128]{1,0:T(8,128)(2,1)S(1)} %add_convert_fusion), channel_id=1, source_target_pairs={{0,48},{1,49},{2,50},{3,51},{4,52},{5,53},{6,54},{7,55},{8,56},{9,... | collective-permute-start | bytes 165896 | tf_op jit(solution)/shard_map/ppermute | solution.py:55
  59.4 5.4 %collective-permute-start.10 = (bf16[216,128]{1,0:T(8,128)(2,1)S(1)}, bf16[216,128]{1,0:T(8,128)(2,1)S(1)}, u32[]{:S(2)}, u32[]{:S(2)}) collective-permute-start(bf16[216,128]{1,0:T(8,128)(2,1)S(1)} %add_convert_fusion), channel_id=1, source_target_pairs={{0,16},{1,17},{2,18},{3,19},{4,20},{5,21},{6,22},{7,23},{8,24},{9,... | collective-permute-start | bytes 165896 | tf_op jit(solution)/shard_map/ppermute | solution.py:55
  81.4 5.6 %collective-permute-start.14 = (bf16[3456,128]{1,0:T(8,128)(2,1)S(1)}, bf16[3456,128]{1,0:T(8,128)(2,1)S(1)}, u32[]{:S(2)}, u32[]{:S(2)}) collective-permute-start(bf16[3456,128]{1,0:T(8,128)(2,1)S(1)} %bitcast.35), channel_id=1, source_target_pairs={{0,64},{1,65},{2,66},{3,67},{4,68},{5,69},{6,70},{7,71},{8,72},{9,... | collective-permute-start | bytes 2654216 | tf_op jit(solution)/shard_map/ppermute | solution.py:55
